TPU v7x, 32 devices: a whole 2x2x4 slice. The times are simulated.
32 devices in a mesh: lat: 8 (over y, x, core), lon: 4 (over z).
Axes of the slice: x: 2, y: 2, z: 4, core: 2. Of those that a mesh axis runs over, the one named last changes fastest.
Arguments:
- signal: float32 [16, 1440, 384], P('lat', 'lon'), may hold values from -6 to 6
- band_rows: int32 [8], replicated, may hold values from 1 to 2, 12 in all
- filter_modes: float32 [16, 3, 3, 2, 720], P('lat'), may hold values from -3 to 3
- mixing: float32 [3, 384, 384], replicated, may hold values from -0.1875 to 0.1875
- cotangent: float32 [16, 1440, 384], P('lat', 'lon'), may hold values from -6 to 6
Outputs:
- output: float32 [16, 1440, 384], P('lat', 'lon')
- grad_signal: float32 [16, 1440, 384], P('lat', 'lon')
- weight_grad: float32 [3, 384, 384], replicated
Inputs may be any that keep to these rules, and one draw needn't show every extreme that they name: Band b uses row slots 0 to band_rows[b] - 1 of its 2 slots; the other slots hold values that no output reads. Some band is full.
All inputs are finite; a program needn't handle non-finite values.
Results may differ from a plain program's by a relative error of at most 0.0001.
Values sent between devices are 32-bit elements; how exact they have to be, the bound alone decides.
No kernel may reach another device: no remote copies, remote signals or barrier semaphores. Data moves between devices by JAX's collectives and lax.ppermute only.
A program may use at most 128 MiB of HBM per device.

v0:
```python
import math

import jax
import jax.numpy as jnp
from jax import lax
from jax.sharding import PartitionSpec as P


def extended(block, sides, width):
    for axis, dim in sides:
        count = lax.axis_size(axis)
        forward = [(i, i + 1) for i in range(count - 1)]
        backward = [(target, source) for source, target in forward]
        low = lax.ppermute(
            lax.slice_in_dim(block, block.shape[dim] - width, None, axis=dim), axis, forward
        )
        high = lax.ppermute(lax.slice_in_dim(block, 0, width, axis=dim), axis, backward)
        block = jnp.concatenate([low, block, high], axis=dim)
    return block


def angle_tables(length, mode_count):
    positions = jnp.arange(length, dtype=jnp.int32)
    mode_ids = jnp.arange(mode_count, dtype=jnp.int32)
    phase_ids = positions[:, None] * mode_ids[None, :] % length
    angles = phase_ids.astype(jnp.float32) * (2.0 * math.pi / length)
    return (jnp.cos(angles), jnp.sin(angles))


def local(signal, band_rows, filter_modes, mixing, cotangent):
    exact = lax.Precision.HIGHEST
    row_slots = signal.shape[0]
    channels = signal.shape[2]
    lon_ways = lax.axis_size("lon")
    length = signal.shape[1] * lon_ways
    mode_count = length // 2
    slice_width = channels // lon_ways
    basis_count = mixing.shape[0]
    cosine, sine_table = angle_tables(length, mode_count)
    forward_table = jnp.concatenate([cosine, -sine_table], axis=1)
    scale_row = jnp.where(jnp.arange(mode_count) == 0, 1.0, 2.0).astype(jnp.float32) / length
    inverse_table = jnp.concatenate(
        [(cosine * scale_row[None, :]).T, (-sine_table * scale_row[None, :]).T], axis=0
    )
    band_index = lax.axis_index("lat")
    channel_start = lax.axis_index("lon") * slice_width
    live_rows = lax.dynamic_index_in_dim(band_rows, band_index, 0, keepdims=False)
    slot_index = jnp.arange(row_slots, dtype=jnp.int32)
    live_mask = (slot_index < live_rows).astype(jnp.float32)
    go_on = slot_index + 1 < live_rows
    real_part = filter_modes[:, :, :, 0, :]
    imag_part = filter_modes[:, :, :, 1, :]
    spectrum = jnp.einsum(
        "rnc,nf->rcf",
        lax.all_to_all(signal, "lon", split_axis=2, concat_axis=1, tiled=True),
        forward_table,
        precision=exact,
    )
    last_live = lax.dynamic_index_in_dim(spectrum, live_rows - 1, 0, keepdims=True)
    boundary = jnp.concatenate([spectrum[:1], last_live], axis=0)
    padded = extended(boundary, (("lat", 0),), 1)
    lower_rows = jnp.concatenate([padded[0][None], spectrum[:-1]], axis=0)
    next_rows = jnp.concatenate([spectrum[1:], jnp.zeros_like(spectrum[:1])], axis=0)
    upper_rows = jnp.where(go_on[:, None, None], next_rows, padded[3][None])
    stacked = jnp.stack([lower_rows, spectrum, upper_rows], axis=1)
    stack_real = stacked[..., :mode_count]
    stack_imag = stacked[..., mode_count:]
    out_real = jnp.einsum("rdkm,rdcm->rkcm", real_part, stack_real, precision=exact) - jnp.einsum(
        "rdkm,rdcm->rkcm", imag_part, stack_imag, precision=exact
    )
    out_imag = jnp.einsum("rdkm,rdcm->rkcm", real_part, stack_imag, precision=exact) + jnp.einsum(
        "rdkm,rdcm->rkcm", imag_part, stack_real, precision=exact
    )
    filtered = jnp.concatenate([out_real, out_imag], axis=-1)
    masked_grad = cotangent * live_mask[:, None, None]
    weight_rows = lax.dynamic_slice_in_dim(mixing, channel_start, slice_width, 1)
    columns = inverse_table
    column_part = jnp.einsum("rkcm,mn->nrkc", filtered, columns, precision=exact)
    summed = lax.psum_scatter(
        jnp.einsum("nrkc,kco->nro", column_part, weight_rows, precision=exact),
        "lon",
        scatter_dimension=0,
        tiled=True,
    )
    output = jnp.transpose(summed, (1, 0, 2)) * live_mask[:, None, None]
    fields = jnp.einsum("rkcm,mn->rknc", filtered, inverse_table, precision=exact)
    gathered_piece = lax.all_gather(masked_grad, "lon", axis=1, tiled=True)
    piece_grad = jnp.einsum("rno,kco->rknc", gathered_piece, weight_rows, precision=exact)
    columns = inverse_table
    grad_total = jnp.einsum("rknc,mn->rkcm", piece_grad, columns, precision=exact)
    weight_total = jnp.einsum("rknc,rno->kco", fields, gathered_piece, precision=exact)
    weight_part = lax.dynamic_update_slice_in_dim(
        jnp.zeros((basis_count, channels, channels), jnp.float32), weight_total, channel_start, 1
    )
    weight_grad = lax.psum(weight_part, ("lat", "lon"))
    grad_real = grad_total[..., :mode_count]
    grad_imag = grad_total[..., mode_count:]
    back_real = jnp.einsum("rdkm,rkcm->rdcm", real_part, grad_real, precision=exact) + jnp.einsum(
        "rdkm,rkcm->rdcm", imag_part, grad_imag, precision=exact
    )
    back_imag = jnp.einsum("rdkm,rkcm->rdcm", real_part, grad_imag, precision=exact) - jnp.einsum(
        "rdkm,rkcm->rdcm", imag_part, grad_real, precision=exact
    )
    back_terms = jnp.concatenate([back_real, back_imag], axis=-1)
    to_lower = back_terms[:, 0]
    own_term = back_terms[:, 1]
    to_upper = back_terms[:, 2]
    upward = jnp.where(go_on[:, None, None], to_upper, 0.0)
    zero_row = jnp.zeros_like(own_term[:1])
    local_grad = (
        own_term
        + jnp.concatenate([to_lower[1:], zero_row], axis=0)
        + jnp.concatenate([zero_row, upward[:-1]], axis=0)
    )
    leaving_up = lax.dynamic_index_in_dim(to_upper, live_rows - 1, 0, keepdims=True)
    outgoing = jnp.concatenate([to_lower[:1], leaving_up], axis=0)
    arrivals = extended(outgoing, (("lat", 0),), 1)
    first_slot = (slot_index == 0).astype(jnp.float32)
    last_slot = (slot_index == live_rows - 1).astype(jnp.float32)
    local_grad = (
        local_grad
        + first_slot[:, None, None] * arrivals[0][None]
        + last_slot[:, None, None] * arrivals[3][None]
    )
    grad_cycles = jnp.einsum("rcf,nf->rnc", local_grad, forward_table, precision=exact)
    grad_signal = lax.all_to_all(grad_cycles, "lon", split_axis=1, concat_axis=2, tiled=True)
    return (output, grad_signal, weight_grad)


def solution(mesh):
    placed = (
        P("lat", "lon", None),
        P(),
        P("lat", None, None, None, None),
        P(),
        P("lat", "lon", None),
    )
    return jax.shard_map(
        local,
        mesh=mesh,
        in_specs=placed,
        out_specs=(P("lat", "lon", None), P("lat", "lon", None), P()),
        check_vma=False,
    )
```

profile of v0, /device:TPU:0, one launch (start us, length us, event | category | flops | bytes accessed | tf_op | source)
XLA Modules:
  0.0 496.8 jit_solution(17462286237640965524)
XLA Ops:
  10.7 6.3 %all-to-all-start = ((f32[2,360,384]{1,0,2:T(2,128)}), f32[2,360,384]{1,0,2:T(2,128)S(1)}, u32[]{:S(2)}, u32[]{:S(2)}) async-start(f32[2,360,384]{1,0,2:T(2,128)} %copy.36), calls=%async_computation | async-start | bytes 2359296 | tf_op jit(solution)/shard_map/all_to_all | solution.py:55
  20.8 20.1 %cosine_multiply_fusion = (f32[720,1440]{1,0:T(8,128)}, f32[720,1440]{1,0:T(8,128)}) fusion(f32[720]{0:T(1024)S(1)} %select_multiply_fusion), kind=kLoop, calls=%fused_computation.31 | loop fusion | flops 12441600 | bytes 8297280 | tf_op jit(solution)/shard_map/mul | solution.py:43
  40.9 19.7 %sine_negate_fusion = (f32[1440,720]{1,0:T(8,128)}, f32[1440,720]{1,0:T(8,128)}) fusion(), kind=kLoop, calls=%fused_computation.25 | loop fusion | flops 10368000 | bytes 8294400 | tf_op jit(solution)/shard_map/neg | solution.py:43
  66.5 10.8 %fusion.2 = f32[1440,192]{0,1:S(1)} fusion(f32[1440,192]{0,1:T(8,128)} %bitcast.144, f32[1440,720]{1,0:T(8,128)} %get-tuple-element.21, f32[1440,720]{1,0:T(8,128)} %get-tuple-element.22), kind=kOutput, calls=%fused_computation.4 | convolution fusion | flops 4779648000 | bytes 10506240
  102.3 12.4 %fusion.29 = f32[2,720,96,3]{2,3,1,0:T(4,128)S(1)} fusion(f32[2,3,96,720]{2,1,3,0:T(4,128)} %copy.42, f32[2,3,3,1,720]{1,2,4,0,3:T(4,128)} %copy.69), kind=kOutput, calls=%fused_computation.47 | convolution fusion | flops 14929920 | bytes 3369600 | tf_op jit(solution)/shard_map/rdkm,rdcm->rkcm/dot_general | solution.py:68
  114.7 10.4 %fusion.27 = f32[2,720,96,3]{2,3,1,0:T(4,128)S(1)} fusion(f32[2,3,96,720]{2,1,3,0:T(4,128)S(1)} %copy-done.5, f32[2,3,3,1,720]{1,2,4,0,3:T(4,128)S(1)} %copy-done.2), kind=kOutput, calls=%fused_computation.45 | convolution fusion | flops 14929920 | bytes 3369600 | tf_op jit(solution)/shard_map/rdkm,rdcm->rkcm/dot_general | solution.py:71
  125.1 10.2 %subtract_bitcast_fusion = f32[2,3,96,720]{2,1,3,0:T(4,128)S(1)} fusion(f32[2,720,96,3]{2,3,1,0:T(4,128)S(1)} %fusion.29, f32[2,3,96,720]{2,1,3,0:T(4,128)S(1)} %copy-done.5, f32[2,3,3,1,720]{1,2,4,0,3:T(4,128)S(1)} %copy-done.3), kind=kOutput, calls=%fused_computation.58 | convolution fusion | flops 15344640 | bytes 5028480 | tf_op jit(solution)/shard_map/rdkm,rdcm->rkcm/dot_general | solution.py:68
  135.4 10.6 %add_bitcast_fusion = f32[2,3,96,720]{2,1,3,0:T(4,128)S(1)} fusion(f32[2,720,96,3]{2,3,1,0:T(4,128)S(1)} %fusion.27, f32[2,3,96,720]{2,1,3,0:T(4,128)S(1)} %copy-done.4, f32[2,3,3,1,720]{1,2,4,0,3:T(4,128)S(1)} %copy-done.3), kind=kOutput, calls=%fused_computation.57 | convolution fusion | flops 15344640 | bytes 5028480 | tf_op jit(solution)/shard_map/rdkm,rdcm->rkcm/dot_general | solution.py:71
  146.1 5.6 %pad_maximum_fusion.3 = f32[2,3,96,1440]{2,1,3,0:T(4,128)S(1)} fusion(f32[2,3,96,720]{2,1,3,0:T(4,128)S(1)} %add_bitcast_fusion, f32[2,3,96,720]{2,1,3,0:T(4,128)S(1)} %subtract_bitcast_fusion), kind=kLoop, calls=%fused_computation.9 | loop fusion | flops 829440 | bytes 6635520 | tf_op jit(solution)/shard_map/concatenate | solution.py:74
  151.7 18.8 %fusion.4 = f32[1440,2,3,96]{0,3,2,1:T(8,128)S(1)} fusion(f32[720,1440]{1,0:T(8,128)S(1)} %bitcast.149, f32[720,1440]{1,0:T(8,128)S(1)} %bitcast.147, f32[2,3,96,1440]{2,1,3,0:T(4,128)S(1)} %pad_maximum_fusion.3), kind=kOutput, calls=%fused_computation.6 | convolution fusion | flops 14334796800 | bytes 14929920 | tf_op jit(solution)/shard_map/rkcm,mn->nrkc/dot_general | solution.py:78
  172.4 10.7 %convolution_bitcast_fusion = f32[1440,2,384]{2,0,1:T(8,128)} fusion(f32[1440,2,3,96]{0,3,2,1:T(8,128)S(1)} %fusion.4, f32[3,384,384]{2,1,0:T(8,128)S(1)} %copy-done, s32[]{:T(128)S(6)} %select_n.52), kind=kOutput, calls=%fused_computation.37 | convolution fusion | flops 3822059520 | bytes 8404996 | tf_op jit(solution)/shard_map/nrkc,kco->nro/dot_general | solution.py:80
  183.1 8.2 %fusion.11 = f32[3,96,2,1440]{3,1,0,2:T(8,128)S(1)} fusion(f32[2,1440,384]{2,1,0:T(8,128)} %all-gather.2.cloned.1.call-done, f32[3,384,384]{2,1,0:T(8,128)S(1)} %copy-done, s32[]{:T(128)S(6)} %select_n.52), kind=kOutput, calls=%fused_computation.22 | convolution fusion | flops 3822059520 | bytes 8183812 | tf_op jit(solution)/shard_map/rno,kco->rknc/dot_general | solution.py:88
  191.3 20.6 %fusion.3 = f32[2,3,96,1440]{3,2,1,0:T(8,128)S(1)} fusion(f32[720,1440]{1,0:T(8,128)} %get-tuple-element.20, f32[720,1440]{1,0:T(8,128)} %get-tuple-element.19, f32[3,96,2,1440]{3,1,0,2:T(8,128)S(1)} %fusion.11), kind=kOutput, calls=%fused_computation.5 | convolution fusion | flops 14334796800 | bytes 14929920 | tf_op jit(solution)/shard_map/rknc,mn->rkcm/dot_general | solution.py:90
  215.2 14.7 %fusion.33 = f32[2,720,96,3]{2,3,1,0:T(4,128)} fusion(f32[2,3,96,720]{2,1,3,0:T(4,128)} %copy.46, f32[2,3,3,1,720]{1,2,4,0,3:T(4,128)} %copy.68), kind=kOutput, calls=%fused_computation.51 | convolution fusion | flops 14929920 | bytes 3369600 | tf_op jit(solution)/shard_map/rdkm,rkcm->rdcm/dot_general | solution.py:98
  235.5 14.5 %fusion.25 = f32[2,720,96,3]{2,3,1,0:T(4,128)} fusion(f32[2,3,96,720]{2,1,3,0:T(4,128)} %copy.48, f32[2,3,3,1,720]{1,2,4,0,3:T(4,128)} %copy.69), kind=kOutput, calls=%fused_computation.43 | convolution fusion | flops 14929920 | bytes 3369600 | tf_op jit(solution)/shard_map/rdkm,rkcm->rdcm/dot_general | solution.py:98
  254.3 14.7 %fusion.31 = f32[2,720,96,3]{2,3,1,0:T(4,128)} fusion(f32[2,3,96,720]{2,1,3,0:T(4,128)} %copy.48, f32[2,3,3,1,720]{1,2,4,0,3:T(4,128)} %copy.68), kind=kOutput, calls=%fused_computation.49 | convolution fusion | flops 14929920 | bytes 3369600 | tf_op jit(solution)/shard_map/rdkm,rkcm->rdcm/dot_general | solution.py:101
  273.2 14.5 %fusion.23 = f32[2,720,96,3]{2,3,1,0:T(4,128)} fusion(f32[2,3,96,720]{2,1,3,0:T(4,128)} %copy.46, f32[2,3,3,1,720]{1,2,4,0,3:T(4,128)} %copy.69), kind=kOutput, calls=%fused_computation.41 | convolution fusion | flops 14929920 | bytes 3369600 | tf_op jit(solution)/shard_map/rdkm,rkcm->rdcm/dot_general | solution.py:101
  287.7 4.3 copy.57
  297.1 8.4 %collective-permute-start.2 = (f32[1,96,1440]{2,1,0:T(8,128)S(1)}, f32[1,96,1440]{2,1,0:T(8,128)S(1)}, u32[]{:S(2)}, u32[]{:S(2)}) collective-permute-start(f32[1,96,1440]{2,1,0:T(8,128)S(1)} %dynamic-slice_bitcast_fusion), channel_id=1, source_target_pairs={{0,4},{4,8},{8,12},{12,16},{16,20},{20,24},{24,28},{1,5},{5,9},{9,... | collective-permute-start | bytes 1658888 | tf_op jit(solution)/shard_map/ppermute | solution.py:14
  306.8 9.4 %fusion.39 = f32[2,1440,96]{1,2,0:T(8,128)S(1)} fusion(f32[1440,720]{1,0:T(8,128)S(1)} %bitcast.135, f32[1440,720]{1,0:T(8,128)S(1)} %bitcast.137, f32[2,3,96,720]{3,2,1,0:T(8,128)S(1)} %get-tuple-element.24, f32[2,3,96,720]{3,2,1,0:T(8,128)S(1)} %get-tuple-element.23, f32[1,96,1440]{2,1,0:T(8,128)S(1)} %slice_select_fusion, ...), kind=kOutput, calls=%fused_computation.59 | convolution fusion | flops 4781583360 | bytes 14929936 | tf_op jit(solution)/shard_map/rcf,nf->rnc/dot_general | solution.py:125
  318.3 6.7 %all-to-all-start.1 = ((f32[2,1440,96]{2,0,1:T(2,128)}), f32[2,1440,96]{2,0,1:T(2,128)S(1)}, u32[]{:S(2)}, u32[]{:S(2)}) async-start(f32[2,1440,96]{2,0,1:T(2,128)} %copy.58), calls=%async_computation.2 | async-start | bytes 2949120 | tf_op jit(solution)/shard_map/all_to_all | solution.py:126
  325.4 8.3 %fusion.51 = f32[3,384,384]{2,1,0:T(8,128)S(1)} fusion(f32[3,384,384]{2,1,0:T(8,128)S(1)} %broadcast_in_dim.55, s32[]{:T(128)S(6)} %select_n.52, f32[2,1440,384]{2,1,0:T(8,128)} %all-gather.2.cloned.1.call-done, f32[1440,2,3,96]{0,3,2,1:T(8,128)} %copy-done.6), kind=kOutput, calls=%fused_computation.63 | convolution fusion | flops 3822059520 | bytes 8183812 | tf_op jit(solution)/shard_map/rknc,rno->kco/dot_general | solution.py:91
  335.0 25.0 %all-to-all-done.1 = f32[2,1440,96]{2,0,1:T(2,128)S(1)} async-done(((f32[2,1440,96]{2,0,1:T(2,128)}), f32[2,1440,96]{2,0,1:T(2,128)S(1)}, u32[]{:S(2)}, u32[]{:S(2)}) %all-to-all-start.1) | async-done | bytes 1105952 | tf_op jit(solution)/shard_map/all_to_all | solution.py:126
  365.1 121.9 %all-reduce.5.cloned.1.call-done = f32[3,384,384]{2,1,0:T(8,128)} async-done(((f32[3,384,384]{2,1,0:T(8,128)}), f32[3,384,384]{2,1,0:T(8,128)}) %all-reduce.5.cloned.1.call-update) | async-done | bytes 1769488 | tf_op jit(solution)/shard_map/psum | solution.py:95
  (95 shorter events, 74.0 us)
Async XLA Ops:
  7.2 165.3 %copy-start = (f32[3,384,384]{2,1,0:T(8,128)S(1)}, f32[3,384,384]{2,1,0:T(8,128)}, u32[]{:S(2)}) copy-start(f32[3,384,384]{2,1,0:T(8,128)} %param.8) | copy-start | bytes 5308420
  7.2 9.8 %copy-start.9 = (s32[8]{0:T(128)S(1)}, s32[8]{0:T(128)}, u32[]{:S(2)}) copy-start(s32[8]{0:T(128)} %param.6) | copy-start | bytes 100
  10.7 53.3 %all-to-all-start = ((f32[2,360,384]{1,0,2:T(2,128)}), f32[2,360,384]{1,0,2:T(2,128)S(1)}, u32[]{:S(2)}, u32[]{:S(2)}) async-start(f32[2,360,384]{1,0,2:T(2,128)} %copy.36), calls=%async_computation | async-start | bytes 2359296 | tf_op jit(solution)/shard_map/all_to_all | solution.py:55
  17.0 166.1 %all-gather.2.cloned.1.call-start = ((), (), s32[]{:S(2)}) async-start(), calls=%async_computation.4 | async-start | bytes 5529600 | tf_op jit(solution)/shard_map/all_gather | solution.py:87
  20.7 341.9 %reduce-scatter.2.cloned.1.call-start = ((), (), s32[]{:S(2)}) async-start(), calls=%async_computation.3 | async-start | bytes 5529600 | tf_op jit(solution)/shard_map/reduce_scatter | solution.py:79
  78.1 12.6 %collective-permute-start = (f32[1,96,1440]{2,1,0:T(8,128)}, f32[1,96,1440]{2,1,0:T(8,128)}, u32[]{:S(2)}, u32[]{:S(2)}) collective-permute-start(f32[1,96,1440]{2,1,0:T(8,128)} %dynamic-slice_bitcast_fusion.1), channel_id=1, source_target_pairs={{0,4},{4,8},{8,12},{12,16},{16,20},{20,24},{24,28},{1,5},{5,9},{9,... | collective-permute-start | bytes 1658888 | tf_op jit(solution)/shard_map/ppermute | solution.py:14
  81.1 10.9 %collective-permute-start.1 = (f32[1,96,1440]{2,1,0:T(8,128)}, f32[1,96,1440]{2,1,0:T(8,128)}, u32[]{:S(2)}, u32[]{:S(2)}) collective-permute-start(f32[1,96,1440]{2,1,0:T(8,128)} %get-tuple-element.15), channel_id=1, source_target_pairs={{4,0},{8,4},{12,8},{16,12},{20,16},{24,20},{28,24},{5,1},{9,5},{13... | collective-permute-start | bytes 1658888 | tf_op jit(solution)/shard_map/ppermute | solution.py:17
  102.3 12.4 %copy-start.2 = (f32[2,3,3,1,720]{1,2,4,0,3:T(4,128)S(1)}, f32[2,3,3,1,720]{1,2,4,0,3:T(4,128)}, u32[]{:S(2)}) copy-start(f32[2,3,3,1,720]{1,2,4,0,3:T(4,128)} %copy.69) | copy-start | bytes 155524
  102.3 12.4 %copy-start.5 = (f32[2,3,96,720]{2,1,3,0:T(4,128)S(1)}, f32[2,3,96,720]{2,1,3,0:T(4,128)}, u32[]{:S(2)}) copy-start(f32[2,3,96,720]{2,1,3,0:T(4,128)} %copy.40) | copy-start | bytes 4976644
  114.7 10.4 %copy-start.3 = (f32[2,3,3,1,720]{1,2,4,0,3:T(4,128)S(1)}, f32[2,3,3,1,720]{1,2,4,0,3:T(4,128)}, u32[]{:S(2)}) copy-start(f32[2,3,3,1,720]{1,2,4,0,3:T(4,128)} %copy.68) | copy-start | bytes 155524
  125.1 10.2 %copy-start.4 = (f32[2,3,96,720]{2,1,3,0:T(4,128)S(1)}, f32[2,3,96,720]{2,1,3,0:T(4,128)}, u32[]{:S(2)}) copy-start(f32[2,3,96,720]{2,1,3,0:T(4,128)} %copy.42) | copy-start | bytes 4976644
  135.4 16.2 %slice-start.4 = ((s8[4423680]{0:T(1024)(128)(4,1)}), s8[4194304]{0:T(1024)(128)(4,1)S(1)}, s32[]{:S(2)}) async-start(s8[4423680]{0:T(1024)(128)(4,1)} %bitcast.146), calls=%async_computation.10 | async-start | bytes 8388608
  135.4 16.2 %slice-start.6 = ((s8[4423680]{0:T(1024)(128)(4,1)}), s8[4194304]{0:T(1024)(128)(4,1)S(1)}, s32[]{:S(2)}) async-start(s8[4423680]{0:T(1024)(128)(4,1)} %bitcast.148), calls=%async_computation.12 | async-start | bytes 8388608
  146.0 5.6 %slice-start.5 = ((s8[4423680]{0:T(1024)(128)(4,1)}), s8[229376]{0:T(1024)(128)(4,1)S(1)}, s32[]{:S(2)}) async-start(s8[4423680]{0:T(1024)(128)(4,1)} %bitcast.146), calls=%async_computation.11 | async-start | bytes 458752
  146.0 5.6 %slice-start.7 = ((s8[4423680]{0:T(1024)(128)(4,1)}), s8[229376]{0:T(1024)(128)(4,1)S(1)}, s32[]{:S(2)}) async-start(s8[4423680]{0:T(1024)(128)(4,1)} %bitcast.148), calls=%async_computation.13 | async-start | bytes 458752
  292.0 14.8 %slice-start = ((s8[4423680]{0:T(1024)(128)(4,1)}), s8[4194304]{0:T(1024)(128)(4,1)S(1)}, s32[]{:S(2)}) async-start(s8[4423680]{0:T(1024)(128)(4,1)} %bitcast.134), calls=%async_computation.6 | async-start | bytes 8388608
  292.0 14.8 %slice-start.2 = ((s8[4423680]{0:T(1024)(128)(4,1)}), s8[4194304]{0:T(1024)(128)(4,1)S(1)}, s32[]{:S(2)}) async-start(s8[4423680]{0:T(1024)(128)(4,1)} %bitcast.136), calls=%async_computation.8 | async-start | bytes 8388608
  295.1 11.7 %slice-start.1 = ((s8[4423680]{0:T(1024)(128)(4,1)}), s8[229376]{0:T(1024)(128)(4,1)S(1)}, s32[]{:S(2)}) async-start(s8[4423680]{0:T(1024)(128)(4,1)} %bitcast.134), calls=%async_computation.7 | async-start | bytes 458752
  295.1 11.7 %slice-start.3 = ((s8[4423680]{0:T(1024)(128)(4,1)}), s8[229376]{0:T(1024)(128)(4,1)S(1)}, s32[]{:S(2)}) async-start(s8[4423680]{0:T(1024)(128)(4,1)} %bitcast.136), calls=%async_computation.9 | async-start | bytes 458752
  295.4 10.2 %collective-permute-start.3 = (f32[1,96,1440]{2,1,0:T(8,128)S(1)}, f32[1,96,1440]{2,1,0:T(8,128)S(1)}, u32[]{:S(2)}, u32[]{:S(2)}) collective-permute-start(f32[1,96,1440]{2,1,0:T(8,128)S(1)} %get-tuple-element.9), channel_id=1, source_target_pairs={{4,0},{8,4},{12,8},{16,12},{20,16},{24,20},{28,24},{5,1},{9,5},{13... | collective-permute-start | bytes 1658888 | tf_op jit(solution)/shard_map/ppermute | solution.py:17
  297.1 9.7 %collective-permute-start.2 = (f32[1,96,1440]{2,1,0:T(8,128)S(1)}, f32[1,96,1440]{2,1,0:T(8,128)S(1)}, u32[]{:S(2)}, u32[]{:S(2)}) collective-permute-start(f32[1,96,1440]{2,1,0:T(8,128)S(1)} %dynamic-slice_bitcast_fusion), channel_id=1, source_target_pairs={{0,4},{4,8},{8,12},{12,16},{16,20},{20,24},{24,28},{1,5},{5,9},{9,... | collective-permute-start | bytes 1658888 | tf_op jit(solution)/shard_map/ppermute | solution.py:14
  318.3 41.7 %all-to-all-start.1 = ((f32[2,1440,96]{2,0,1:T(2,128)}), f32[2,1440,96]{2,0,1:T(2,128)S(1)}, u32[]{:S(2)}, u32[]{:S(2)}) async-start(f32[2,1440,96]{2,0,1:T(2,128)} %copy.58), calls=%async_computation.2 | async-start | bytes 2949120 | tf_op jit(solution)/shard_map/all_to_all | solution.py:126
  325.0 161.9 %all-reduce.5.cloned.1.call-start = ((), (), s32[]{:S(2)}) async-start(), calls=%async_computation.5 | async-start | bytes 3538944 | tf_op jit(solution)/shard_map/psum | solution.py:95
  361.3 128.4 %copy-start.1 = (f32[3,384,384]{2,1,0:T(8,128)S(1)}, f32[3,384,384]{2,1,0:T(8,128)}, u32[]{:S(2)}) copy-start(f32[3,384,384]{2,1,0:T(8,128)} %param.8) | copy-start | bytes 5308420
  (3 other events, 8.5 us)
Sparse Core Ops, SparseCore 0:
  20.8 96.4 all-gather.1
  183.2 87.6 reduce-scatter.1
  335.1 151.7 all-reduce.4
where the time goes:
time: 506 us; the launch traced here: 497 us
  matrix products  189 us (37%)
  waiting for transfers between devices  150 us (30%)
  other arithmetic  58.1 us (11%)
  local copies, waits for them, and re-layouts  56.8 us (11%)
  starting transfers between devices  26.7 us (5%)
  between operations  16.1 us (3%)
    psum x1, waiting for transfers between devices, local(): weight_grad = lax.psum(weight_part, ('lat', 'lon'))  122 us
    all_to_all x1, waiting for transfers between devices, local(): lax.all_to_all(grad_cycles, 'lon', split_axis=1, concat_axis=2, tiled=True)  25 us
    dot_general x1, matrix products, local(): jnp.einsum('rknc,mn->rkcm', piece_grad, columns, precision=exact)  20.6 us
    mul x1, other arithmetic, local(): cosine * scale_row[None, :]  20.1 us
    neg x1, other arithmetic, local(): -sine_table * scale_row[None, :]  19.7 us
    dot_general x1, matrix products, local(): jnp.einsum('rkcm,mn->nrkc', filtered, columns, precision=exact)  18.8 us
    unnamed x41, local copies, waits for them, and re-layouts  17.5 us
    dot_general x1, matrix products, local(): jnp.einsum('rdkm,rkcm->rdcm', real_part, grad_imag, precision=exact)  14.7 us
  transfers between devices with their start and end apart: 9, of which 4 were waited for; matrix products, arithmetic and copies ran while one was open for 59% of the time, Pallas kernels for 0%

commit v1 on v0

v1 whole, which is shorter than its diff:
```python
import math

import jax
import jax.numpy as jnp
import numpy as np
from jax import lax
from jax.sharding import PartitionSpec as P

AXES = ("lat", "lon")
SLOTS = 4
HIGH = lax.Precision.HIGH


class Layout:
    def __init__(self, lat, lon):
        self.lat, self.lon, self.pairs = lat, lon, lat // 2
        self.chips = lon // SLOTS
        self.share = 2 * self.chips

    def device(self, band, z):
        return band * self.lon + z

    def place(self, pair, rho, h):
        v = rho * self.chips + h // 2
        z = v if pair % 2 == 0 else self.lon - 1 - v
        return self.device(2 * pair + h % 2, z)

    def inward(self, t):
        pairs = []
        for band in range(self.lat):
            for z in range(self.lon):
                r = (z // self.share) ^ t
                dst = self.place(band // 2, 2 * (band % 2) + r, z % self.share)
                pairs.append((self.device(band, z), dst))
        return pairs

    def slots(self):
        for pair in range(self.pairs):
            for rho in range(SLOTS):
                for h in range(self.share):
                    yield pair, rho, h

    def within(self, g):
        return [(self.place(p, rho, h), self.place(p, rho, h ^ g)) for p, rho, h in self.slots()]

    def upward(self):
        pairs = []
        for p, rho, h in self.slots():
            q, sigma = (p, rho + 1) if rho + 1 < SLOTS else (p + 1, 0)
            if q < self.pairs:
                pairs.append((self.place(p, rho, h), self.place(q, sigma, h)))
        return pairs


def flipped(pairs):
    return [(b, a) for a, b in pairs]


def tables(length, modes, lon, share):
    n = np.arange(length)
    m = np.arange(modes)
    angle = (n[:, None] * m[None, :] % length) * (2.0 * math.pi / length)
    root = np.sqrt(np.where(m == 0, 1.0, 2.0) / length)
    cosine = (np.cos(angle) * root).reshape(lon, length // lon, modes)
    sine = (-np.sin(angle) * root).reshape(lon, length // lon, modes)
    width = modes // share
    out = []
    for h in range(share):
        order = [b * share + (h ^ g) for g in range(share) for b in range(2)]
        part = slice(h * width, (h + 1) * width)
        out.append(np.concatenate([cosine[order][:, :, part], sine[order][:, :, part]], axis=2).reshape(length, 2 * width))
    return np.stack(out).astype(np.float32)


def make_local(lat, lon):
    lay = Layout(lat, lon)
    share = lay.share

    def send(x, pairs):
        return lax.ppermute(x, AXES, pairs)

    def local(signal, band_rows, filter_modes, mixing, cotangent):
        channels = signal.shape[2]
        part_len = signal.shape[1]
        length = part_len * lon
        modes = filter_modes.shape[-1]
        basis = mixing.shape[0]
        width = modes // share

        band = lax.axis_index("lat")
        z = lax.axis_index("lon")
        core = band % 2
        v = jnp.where((band // 2) % 2 == 0, z, lon - 1 - z)
        rho = v // lay.chips
        h = (v % lay.chips) * 2 + core
        r_held = rho % 2
        live = lax.dynamic_index_in_dim(band_rows, band, 0, keepdims=False)
        full = live == 2
        high_z = z // share

        table = lax.dynamic_index_in_dim(jnp.asarray(tables(length, modes, lon, share)), h, 0, keepdims=False)

        def enter(x):
            got = []
            for t in range(2):
                row = jnp.minimum(high_z ^ t, live - 1)
                got.append(send(lax.dynamic_index_in_dim(x, row, 0, keepdims=False), lay.inward(t)))
            own = jnp.stack([jnp.where(r_held == 0, got[0], got[1]), jnp.where(r_held == 0, got[1], got[0])])
            rows = [own] + [send(own, lay.within(g)) for g in range(1, share)]
            rows = jnp.concatenate(rows, axis=0).reshape(length, channels)
            return jnp.einsum("nf,nc->fc", table, rows, precision=HIGH)

        def leave(spec):
            y = jnp.einsum("nf,fc->nc", table, spec, precision=HIGH).reshape(share, 2, part_len, channels)
            own = y[0]
            for g in range(1, share):
                own = own + send(y[g], lay.within(g))
            got = []
            for t in range(2):
                block = jnp.where((r_held ^ t) == 0, own[0], own[1])
                got.append(send(block, flipped(lay.inward(t))))
            first = jnp.where(high_z == 0, got[0], got[1])
            second = jnp.where(high_z == 0, got[1], got[0])
            return jnp.stack([jnp.where(full, first, first + second), jnp.where(full, second, 0.0)])

        f = filter_modes
        ladder = [(i, i + 1) for i in range(lat - 1)]
        below = lax.ppermute(jnp.where(full, f[1, 2], f[0, 2]), "lat", ladder)
        above = lax.ppermute(f[0, 0], "lat", flipped(ladder))
        nil = jnp.zeros_like(below)
        is_first = r_held == 0
        ahead = [
            jnp.where(is_first, f[0, 0], jnp.where(full, f[1, 0], nil)),
            jnp.where(is_first, f[0, 1], jnp.where(full, f[1, 1], nil)),
            jnp.where(is_first, jnp.where(full, f[0, 2], nil), jnp.where(full, f[1, 2], f[0, 2])),
        ]
        back = [
            jnp.where(is_first, below, jnp.where(full, f[0, 2], nil)),
            jnp.where(is_first, f[0, 1], jnp.where(full, f[1, 1], nil)),
            jnp.where(is_first, jnp.where(full, f[1, 0], nil), above),
        ]
        conj = jnp.array([1.0, -1.0], jnp.float32)[None, None, :, None]
        both = jnp.stack([jnp.stack(ahead), jnp.stack(back) * conj])
        both = both.reshape(2 * 3 * basis * 2, modes)
        swap = [(i, i ^ 1) for i in range(lat)]
        theirs = lax.ppermute(lax.dynamic_slice_in_dim(both, (h ^ 1) * width, width, 1), "lat", swap)
        mine = lax.dynamic_slice_in_dim(both, h * width, width, 1)
        coef = jnp.where(rho // 2 == core, mine, theirs).reshape(2, 3, basis, 2, width)

        def mix(spec, coef, weights):
            lower = send(spec, lay.upward())
            upper = send(spec, flipped(lay.upward()))
            real, imag = [], []
            for k in range(basis):
                re, im = 0.0, 0.0
                for d, row in enumerate((lower, spec, upper)):
                    pr, pi = coef[d, k, 0][:, None], coef[d, k, 1][:, None]
                    xr, xi = row[:width], row[width:]
                    re = re + (pr * xr - pi * xi)
                    im = im + (pr * xi + pi * xr)
                real.append(re)
                imag.append(im)
            filtered = jnp.concatenate([jnp.concatenate(real, axis=1), jnp.concatenate(imag, axis=1)], axis=0)
            return filtered, jnp.einsum("fc,co->fo", filtered, weights, precision=HIGH)

        s_spec = enter(signal)
        g_spec = enter(cotangent)
        filtered, o_spec = mix(s_spec, coef[0], mixing.reshape(basis * channels, channels))
        output = leave(o_spec)
        _, b_spec = mix(g_spec, coef[1], jnp.transpose(mixing, (0, 2, 1)).reshape(basis * channels, channels))
        grad_signal = leave(b_spec)
        term = jnp.einsum("fc,fo->co", filtered, g_spec, precision=HIGH)

        bits = int(math.log2(lat))
        for i in range(bits):
            bit = (band >> i) & 1
            half = term.shape[0] // 2
            term = term.reshape(2, half, channels)
            keep = lax.dynamic_index_in_dim(term, bit, 0, keepdims=False)
            give = lax.dynamic_index_in_dim(term, 1 - bit, 0, keepdims=False)
            term = keep + lax.ppermute(give, "lat", [(a, a ^ (1 << i)) for a in range(lat)])
        shape = term.shape
        parts = term.reshape(lon, -1, 128) if term.size % (lon * 128) == 0 else term.reshape(lon, 1, -1)
        total = lax.dynamic_index_in_dim(parts, z, 0, keepdims=False)
        for g in range(1, lon):
            piece = lax.dynamic_index_in_dim(parts, z ^ g, 0, keepdims=False)
            total = total + lax.ppermute(piece, "lon", [(a, a ^ g) for a in range(lon)])
        gathered = jnp.zeros_like(parts)
        gathered = lax.dynamic_update_index_in_dim(gathered, total, z, 0)
        for g in range(1, lon):
            piece = lax.ppermute(total, "lon", [(a, a ^ g) for a in range(lon)])
            gathered = lax.dynamic_update_index_in_dim(gathered, piece, z ^ g, 0)
        term = gathered.reshape(shape)
        for i in reversed(range(bits)):
            bit = (band >> i) & 1
            other = lax.ppermute(term, "lat", [(a, a ^ (1 << i)) for a in range(lat)])
            term = jnp.concatenate([jnp.where(bit == 0, term, other), jnp.where(bit == 0, other, term)], axis=0)
        weight_grad = term.reshape(mixing.shape)
        return output, grad_signal, weight_grad

    return local


def solution(mesh):
    lat, lon = mesh.shape["lat"], mesh.shape["lon"]
    grid = P("lat", "lon", None)
    return jax.shard_map(
        make_local(lat, lon),
        mesh=mesh,
        in_specs=(grid, P(), P("lat", None, None, None, None), P(), grid),
        out_specs=(grid, grid, P()),
        check_vma=False,
    )
```

time: 506 us -> 235 us (0.46)
  the two profiles are of different devices: /device:TPU:0 before, /device:TPU:2 now
where the time goes in v1:
time: 235 us; the launch traced here: 234 us
  waiting for transfers between devices  109 us (46%)
  starting transfers between devices  53.8 us (23%)
  matrix products  30.9 us (13%)
  other arithmetic  23.6 us (10%)
  local copies, waits for them, and re-layouts  13 us (6%)
  between operations  2.7 us (1%)
    ppermute x16, waiting for transfers between devices, send(): return lax.ppermute(x, AXES, pairs)  87.4 us
    ppermute x16, starting transfers between devices, send(): return lax.ppermute(x, AXES, pairs)  35.9 us
    dot_general x2, matrix products, enter(): return jnp.einsum('nf,nc->fc', table, rows, precision=HIGH)  12.8 us
    ppermute x3, waiting for transfers between devices, local(): lax.ppermute(give, 'lat', [(a, a ^ 1 << i) for a in range(lat)])  11.3 us
    dot_general x2, matrix products, leave(): jnp.einsum('nf,fc->nc', table, spec, precision=HIGH)  9.19 us
    ppermute x3, waiting for transfers between devices, local(): other = lax.ppermute(term, 'lat', [(a, a ^ 1 << i) for a in range(lat)])  5.94 us
    dot_general x2, matrix products, mix(): jnp.einsum('fc,co->fo', filtered, weights, precision=HIGH)  5.89 us
    ppermute x3, waiting for transfers between devices, local(): piece = lax.ppermute(total, 'lon', [(a, a ^ g) for a in range(lon)])  4.79 us
  transfers between devices with their start and end apart: 31, of which 14 were waited for; matrix products, arithmetic and copies ran while one was open for 26% of the time, Pallas kernels for 0%

profile of v1, /device:TPU:2, one launch (start us, length us, event | category | flops | bytes accessed | tf_op | source)
XLA Modules:
  0.0 233.5 jit_solution(6920685998385585389)
XLA Ops:
  4.8 5.5 %collective-permute-start.3 = (f32[360,384]{1,0:T(8,128)}, f32[360,384]{1,0:T(8,128)S(1)}, u32[]{:S(2)}, u32[]{:S(2)}) collective-permute-start(f32[360,384]{1,0:T(8,128)} %get-tuple-element.73), channel_id=1, source_target_pairs={{0,0},{1,4},{2,1},{3,5},{4,2},{5,6},{6,3},{7,7},{8,11},{9,15},{10,... | collective-permute-start | bytes 1658888 | tf_op jit(solution)/shard_map/ppermute | solution.py:80
  16.6 3.3 %collective-permute-start.11 = (f32[360,384]{1,0:T(8,128)}, f32[360,384]{1,0:T(8,128)S(1)}, u32[]{:S(2)}, u32[]{:S(2)}) collective-permute-start(f32[360,384]{1,0:T(8,128)} %get-tuple-element.65), channel_id=1, source_target_pairs={{0,0},{1,4},{2,1},{3,5},{4,2},{5,6},{6,3},{7,7},{8,11},{9,15},{10,... | collective-permute-start | bytes 1658888 | tf_op jit(solution)/shard_map/ppermute | solution.py:80
  19.9 3.2 %collective-permute-done.3 = f32[360,384]{1,0:T(8,128)S(1)} collective-permute-done((f32[360,384]{1,0:T(8,128)}, f32[360,384]{1,0:T(8,128)S(1)}, u32[]{:S(2)}, u32[]{:S(2)}) %collective-permute-start.3) | collective-permute-done | bytes 552992 | tf_op jit(solution)/shard_map/ppermute | solution.py:80
  23.1 8.7 %collective-permute-done.4 = f32[360,384]{1,0:T(8,128)S(1)} collective-permute-done((f32[360,384]{1,0:T(8,128)S(1)}, f32[360,384]{1,0:T(8,128)S(1)}, u32[]{:S(2)}, u32[]{:S(2)}) %collective-permute-start.4) | collective-permute-done | bytes 552992 | tf_op jit(solution)/shard_map/ppermute | solution.py:80
  36.7 15.5 %collective-permute-done.11 = f32[360,384]{1,0:T(8,128)S(1)} collective-permute-done((f32[360,384]{1,0:T(8,128)}, f32[360,384]{1,0:T(8,128)S(1)}, u32[]{:S(2)}, u32[]{:S(2)}) %collective-permute-start.11) | collective-permute-done | bytes 552992 | tf_op jit(solution)/shard_map/ppermute | solution.py:80
  56.1 6.4 %fusion.6 = f32[720,384]{1,0:T(8,128)S(1)} fusion(f32[1440,384]{1,0:T(8,128)S(1)} %bitcast.122, f32[2,1440,720]{2,1,0:T(8,128)} %constant.152.clone, s32[]{:T(128)S(6)} %select_n.364), kind=kOutput, calls=%fused_computation.6 | convolution fusion | flops 2388787200 | bytes 7741444 | tf_op jit(solution)/shard_map/nf,nc->fc/dot_general | solution.py:111
  62.6 8.7 %collective-permute-start.7 = (f32[720,384]{1,0:T(8,128)S(1)}, f32[720,384]{1,0:T(8,128)S(1)}, u32[]{:S(2)}, u32[]{:S(2)}) collective-permute-start(f32[720,384]{1,0:T(8,128)S(1)} %fusion.6), channel_id=1, source_target_pairs={{1,0},{5,4},{2,1},{6,5},{3,2},{7,6},{11,3},{15,7},{10,11},{14,15},... | collective-permute-start | bytes 3317768 | tf_op jit(solution)/shard_map/ppermute | solution.py:80
  71.3 3.4 %collective-permute-start.6 = (f32[720,384]{1,0:T(8,128)S(1)}, f32[720,384]{1,0:T(8,128)S(1)}, u32[]{:S(2)}, u32[]{:S(2)}) collective-permute-start(f32[720,384]{1,0:T(8,128)S(1)} %fusion.6), channel_id=1, source_target_pairs={{0,1},{4,5},{1,2},{5,6},{2,3},{6,7},{3,11},{7,15},{11,10},{15,14},... | collective-permute-start | bytes 3317768 | tf_op jit(solution)/shard_map/ppermute | solution.py:80
  76.7 6.4 %fusion.2 = f32[720,384]{1,0:T(8,128)S(1)} fusion(f32[1440,384]{1,0:T(8,128)S(1)} %bitcast.123, f32[2,1440,720]{2,1,0:T(8,128)} %constant.152.clone, s32[]{:T(128)S(6)} %select_n.364), kind=kOutput, calls=%fused_computation.2 | convolution fusion | flops 2388787200 | bytes 7741444 | tf_op jit(solution)/shard_map/nf,nc->fc/dot_general | solution.py:111
  85.8 4.2 %collective-permute-start.14 = (f32[720,384]{1,0:T(8,128)S(1)}, f32[720,384]{1,0:T(8,128)S(1)}, u32[]{:S(2)}, u32[]{:S(2)}) collective-permute-start(f32[720,384]{1,0:T(8,128)S(1)} %fusion.2), channel_id=1, source_target_pairs={{0,1},{4,5},{1,2},{5,6},{2,3},{6,7},{3,11},{7,15},{11,10},{15,14},... | collective-permute-start | bytes 3317768 | tf_op jit(solution)/shard_map/ppermute | solution.py:80
  90.1 7.9 %collective-permute-done.7 = f32[720,384]{1,0:T(8,128)S(1)} collective-permute-done((f32[720,384]{1,0:T(8,128)S(1)}, f32[720,384]{1,0:T(8,128)S(1)}, u32[]{:S(2)}, u32[]{:S(2)}) %collective-permute-start.7) | collective-permute-done | bytes 1105952 | tf_op jit(solution)/shard_map/ppermute | solution.py:80
  102.2 3.1 %fusion.24 = f32[1152,384]{1,0:T(8,128)S(1)} fusion(f32[720,384]{1,0:T(8,128)S(1)} %fusion.2, f32[360,384]{1,0:T(8,128)S(1)} %get-tuple-element.52, f32[360,384]{1,0:T(8,128)S(1)} %get-tuple-element.50, f32[360,384]{1,0:T(8,128)S(1)} %get-tuple-element.48, f32[360,384]{1,0:T(8,128)S(1)} %get-tuple-element.51, f32[360,384]{1,0:T(8,128)S(1)} %get-tuple-element.49, ...), kind=kOutput, calls=%fused_computation.28 | convolution fusion | flops 1915176960 | bytes 6193152 | tf_op jit(solution)/shard_map/fc,fo->co/dot_general | solution.py:172
  106.7 3.0 %fusion.25 = f32[720,384]{1,0:T(8,128)S(1)} fusion(f32[1152,384]{1,0:T(8,128)S(1)} %bitcast.128, f32[360,384]{1,0:T(8,128)S(1)} %get-tuple-element.52, f32[360,384]{1,0:T(8,128)S(1)} %get-tuple-element.50, f32[360,384]{1,0:T(8,128)S(1)} %get-tuple-element.48, f32[360,384]{1,0:T(8,128)S(1)} %get-tuple-element.51, f32[360,384]{1,0:T(8,128)S(1)} %get-tuple-element.49, ...), kind=kOutput, calls=%fused_computation.29 | convolution fusion | flops 1915176960 | bytes 6193152 | tf_op jit(solution)/shard_map/fc,co->fo/dot_general | solution.py:164
  109.8 3.8 %fusion.4 = f32[1440,384]{1,0:T(8,128)S(1)} fusion(f32[720,384]{1,0:T(8,128)S(1)} %fusion.25, f32[2,1440,720]{2,1,0:T(8,128)S(1)} %bitcast.121, s32[]{:T(128)S(6)} %select_n.364), kind=kOutput, calls=%fused_computation.4 | convolution fusion | flops 2388787200 | bytes 7741444 | tf_op jit(solution)/shard_map/nf,fc->nc/dot_general | solution.py:114
  114.7 6.7 %collective-permute-done.15 = f32[720,384]{1,0:T(8,128)S(1)} collective-permute-done((f32[720,384]{1,0:T(8,128)S(1)}, f32[720,384]{1,0:T(8,128)S(1)}, u32[]{:S(2)}, u32[]{:S(2)}) %collective-permute-start.15) | collective-permute-done | bytes 1105952 | tf_op jit(solution)/shard_map/ppermute | solution.py:80
  125.4 10.1 %collective-permute-done.20 = f32[288,384]{1,0:T(8,128)S(1)} collective-permute-done((f32[288,384]{1,0:T(8,128)S(1)}, f32[288,384]{1,0:T(8,128)S(1)}, u32[]{:S(2)}, u32[]{:S(2)}) %collective-permute-start.20) | collective-permute-done | bytes 442400 | tf_op jit(solution)/shard_map/ppermute | solution.py:181
  137.4 2.9 %fusion.12 = f32[720,384]{1,0:T(8,128)S(1)} fusion(f32[1152,384]{1,0:T(8,128)S(1)} %bitcast.129, f32[360,384]{1,0:T(8,128)S(1)} %get-tuple-element.46, f32[360,384]{1,0:T(8,128)S(1)} %get-tuple-element.44, f32[360,384]{1,0:T(8,128)S(1)} %get-tuple-element.42, f32[360,384]{1,0:T(8,128)S(1)} %get-tuple-element.45, f32[360,384]{1,0:T(8,128)S(1)} %get-tuple-element.43, ...), kind=kOutput, calls=%fused_computation.13 | convolution fusion | flops 1915176960 | bytes 6193152 | tf_op jit(solution)/shard_map/fc,co->fo/dot_general | solution.py:164
  146.8 5.4 %fusion = f32[1440,384]{1,0:T(8,128)S(1)} fusion(f32[720,384]{1,0:T(8,128)S(1)} %fusion.12, f32[2,1440,720]{2,1,0:T(8,128)} %constant.152.clone, s32[]{:T(128)S(6)} %select_n.364), kind=kOutput, calls=%fused_computation | convolution fusion | flops 2388787200 | bytes 7741444 | tf_op jit(solution)/shard_map/nf,fc->nc/dot_general | solution.py:114
  159.1 4.8 %collective-permute-done.26 = f32[108,128]{1,0:T(8,128)S(1)} collective-permute-done((f32[108,128]{1,0:T(8,128)S(1)}, f32[108,128]{1,0:T(8,128)S(1)}, u32[]{:S(2)}, u32[]{:S(2)}) %collective-permute-start.26) | collective-permute-done | bytes 55328 | tf_op jit(solution)/shard_map/ppermute | solution.py:191
  166.4 5.9 %collective-permute-done.28 = f32[144,384]{1,0:T(8,128)} collective-permute-done((f32[144,384]{1,0:T(8,128)}, f32[144,384]{1,0:T(8,128)}, u32[]{:S(2)}, u32[]{:S(2)}) %collective-permute-start.28) | collective-permute-done | bytes 221216 | tf_op jit(solution)/shard_map/ppermute | solution.py:196
  180.6 4.6 %collective-permute-start.17 = (f32[360,384]{1,0:T(8,128)}, f32[360,384]{1,0:T(8,128)S(1)}, u32[]{:S(2)}, u32[]{:S(2)}) collective-permute-start(f32[360,384]{1,0:T(8,128)} %get-tuple-element.61), channel_id=1, source_target_pairs={{0,0},{4,1},{1,2},{5,3},{2,4},{6,5},{3,6},{7,7},{11,8},{15,9},{10,... | collective-permute-start | bytes 1658888 | tf_op jit(solution)/shard_map/ppermute | solution.py:80
  186.7 8.7 %collective-permute-done.9 = f32[360,384]{1,0:T(8,128)} collective-permute-done((f32[360,384]{1,0:T(8,128)}, f32[360,384]{1,0:T(8,128)}, u32[]{:S(2)}, u32[]{:S(2)}) %collective-permute-start.9) | collective-permute-done | bytes 552992 | tf_op jit(solution)/shard_map/ppermute | solution.py:80
  195.4 23.5 %collective-permute-done.10 = f32[360,384]{1,0:T(8,128)} collective-permute-done((f32[360,384]{1,0:T(8,128)}, f32[360,384]{1,0:T(8,128)}, u32[]{:S(2)}, u32[]{:S(2)}) %collective-permute-start.10) | collective-permute-done | bytes 552992 | tf_op jit(solution)/shard_map/ppermute | solution.py:80
  221.4 8.4 %collective-permute-done.18 = f32[360,384]{1,0:T(8,128)} collective-permute-done((f32[360,384]{1,0:T(8,128)}, f32[360,384]{1,0:T(8,128)}, u32[]{:S(2)}, u32[]{:S(2)}) %collective-permute-start.18) | collective-permute-done | bytes 552992 | tf_op jit(solution)/shard_map/ppermute | solution.py:80
  (131 shorter events, 66.6 us)
Async XLA Ops:
  4.8 18.3 %collective-permute-start.3 = (f32[360,384]{1,0:T(8,128)}, f32[360,384]{1,0:T(8,128)S(1)}, u32[]{:S(2)}, u32[]{:S(2)}) collective-permute-start(f32[360,384]{1,0:T(8,128)} %get-tuple-element.73), channel_id=1, source_target_pairs={{0,0},{1,4},{2,1},{3,5},{4,2},{5,6},{6,3},{7,7},{8,11},{9,15},{10,... | collective-permute-start | bytes 1658888 | tf_op jit(solution)/shard_map/ppermute | solution.py:80
  10.3 21.5 %collective-permute-start.4 = (f32[360,384]{1,0:T(8,128)S(1)}, f32[360,384]{1,0:T(8,128)S(1)}, u32[]{:S(2)}, u32[]{:S(2)}) collective-permute-start(f32[360,384]{1,0:T(8,128)S(1)} %get-tuple-element.74), channel_id=1, source_target_pairs={{0,1},{1,5},{2,0},{3,4},{4,3},{5,7},{6,2},{7,6},{8,10},{9,14},{10,... | collective-permute-start | bytes 1658888 | tf_op jit(solution)/shard_map/ppermute | solution.py:80
  11.1 24.4 %collective-permute-start.1 = (f32[3,2,720]{2,1,0:T(2,128)S(1)}, f32[3,2,720]{2,1,0:T(2,128)}, u32[]{:S(2)}, u32[]{:S(2)}) collective-permute-start(f32[3,2,720]{2,1,0:T(2,128)S(1)} %get-tuple-element.83), channel_id=1, source_target_pairs={{4,0},{8,4},{12,8},{16,12},{20,16},{24,20},{28,24},{5,1},{9,5},{13... | collective-permute-start | bytes 51848 | tf_op jit(solution)/shard_map/ppermute | solution.py:129
  13.2 22.3 %collective-permute-start = (f32[3,2,720]{2,1,0:T(2,128)S(1)}, f32[3,2,720]{2,1,0:T(2,128)}, u32[]{:S(2)}, u32[]{:S(2)}) collective-permute-start(f32[3,2,720]{2,1,0:T(2,128)S(1)} %get-tuple-element.84), channel_id=1, source_target_pairs={{0,4},{4,8},{8,12},{12,16},{16,20},{20,24},{24,28},{1,5},{5,9},{9,... | collective-permute-start | bytes 51848 | tf_op jit(solution)/shard_map/ppermute | solution.py:128
  16.6 35.7 %collective-permute-start.11 = (f32[360,384]{1,0:T(8,128)}, f32[360,384]{1,0:T(8,128)S(1)}, u32[]{:S(2)}, u32[]{:S(2)}) collective-permute-start(f32[360,384]{1,0:T(8,128)} %get-tuple-element.65), channel_id=1, source_target_pairs={{0,0},{1,4},{2,1},{3,5},{4,2},{5,6},{6,3},{7,7},{8,11},{9,15},{10,... | collective-permute-start | bytes 1658888 | tf_op jit(solution)/shard_map/ppermute | solution.py:80
  23.1 29.2 %collective-permute-start.12 = (f32[360,384]{1,0:T(8,128)}, f32[360,384]{1,0:T(8,128)}, u32[]{:S(2)}, u32[]{:S(2)}) collective-permute-start(f32[360,384]{1,0:T(8,128)} %get-tuple-element.66), channel_id=1, source_target_pairs={{0,1},{1,5},{2,0},{3,4},{4,3},{5,7},{6,2},{7,6},{8,10},{9,14},{10,... | collective-permute-start | bytes 1658888 | tf_op jit(solution)/shard_map/ppermute | solution.py:80
  33.0 21.8 %collective-permute-start.5 = (f32[2,360,384]{2,1,0:T(8,128)}, f32[2,360,384]{2,1,0:T(8,128)}, u32[]{:S(2)}, u32[]{:S(2)}) collective-permute-start(f32[2,360,384]{2,1,0:T(8,128)} %pad_maximum_fusion.3), channel_id=1, source_target_pairs={{0,4},{4,0},{1,5},{5,1},{2,6},{6,2},{3,7},{7,3},{11,15},{15,11},{1... | collective-permute-start | bytes 3317768 | tf_op jit(solution)/shard_map/ppermute | solution.py:80
  36.6 38.0 %collective-permute-start.2 = (f32[36,360]{1,0:T(8,128)S(1)}, f32[36,360]{1,0:T(8,128)S(1)}, u32[]{:S(2)}, u32[]{:S(2)}) collective-permute-start(f32[36,360]{1,0:T(8,128)S(1)} %constant_dynamic-slice_fusion), channel_id=1, source_target_pairs={{0,4},{4,0},{8,12},{12,8},{16,20},{20,16},{24,28},{28,24},{1,5},{5... | collective-permute-start | bytes 155528 | tf_op jit(solution)/shard_map/ppermute | solution.py:146
  54.7 20.4 %collective-permute-start.13 = (f32[2,360,384]{2,1,0:T(8,128)}, f32[2,360,384]{2,1,0:T(8,128)}, u32[]{:S(2)}, u32[]{:S(2)}) collective-permute-start(f32[2,360,384]{2,1,0:T(8,128)} %pad_maximum_fusion.5), channel_id=1, source_target_pairs={{0,4},{4,0},{1,5},{5,1},{2,6},{6,2},{3,7},{7,3},{11,15},{15,11},{1... | collective-permute-start | bytes 3317768 | tf_op jit(solution)/shard_map/ppermute | solution.py:80
  62.6 35.4 %collective-permute-start.7 = (f32[720,384]{1,0:T(8,128)S(1)}, f32[720,384]{1,0:T(8,128)S(1)}, u32[]{:S(2)}, u32[]{:S(2)}) collective-permute-start(f32[720,384]{1,0:T(8,128)S(1)} %fusion.6), channel_id=1, source_target_pairs={{1,0},{5,4},{2,1},{6,5},{3,2},{7,6},{11,3},{15,7},{10,11},{14,15},... | collective-permute-start | bytes 3317768 | tf_op jit(solution)/shard_map/ppermute | solution.py:80
  71.3 29.4 %collective-permute-start.6 = (f32[720,384]{1,0:T(8,128)S(1)}, f32[720,384]{1,0:T(8,128)S(1)}, u32[]{:S(2)}, u32[]{:S(2)}) collective-permute-start(f32[720,384]{1,0:T(8,128)S(1)} %fusion.6), channel_id=1, source_target_pairs={{0,1},{4,5},{1,2},{5,6},{2,3},{6,7},{3,11},{7,15},{11,10},{15,14},... | collective-permute-start | bytes 3317768 | tf_op jit(solution)/shard_map/ppermute | solution.py:80
  83.1 38.3 %collective-permute-start.15 = (f32[720,384]{1,0:T(8,128)S(1)}, f32[720,384]{1,0:T(8,128)S(1)}, u32[]{:S(2)}, u32[]{:S(2)}) collective-permute-start(f32[720,384]{1,0:T(8,128)S(1)} %fusion.2), channel_id=1, source_target_pairs={{1,0},{5,4},{2,1},{6,5},{3,2},{7,6},{11,3},{15,7},{10,11},{14,15},... | collective-permute-start | bytes 3317768 | tf_op jit(solution)/shard_map/ppermute | solution.py:80
  85.8 37.6 %collective-permute-start.14 = (f32[720,384]{1,0:T(8,128)S(1)}, f32[720,384]{1,0:T(8,128)S(1)}, u32[]{:S(2)}, u32[]{:S(2)}) collective-permute-start(f32[720,384]{1,0:T(8,128)S(1)} %fusion.2), channel_id=1, source_target_pairs={{0,1},{4,5},{1,2},{5,6},{2,3},{6,7},{3,11},{7,15},{11,10},{15,14},... | collective-permute-start | bytes 3317768 | tf_op jit(solution)/shard_map/ppermute | solution.py:80
  105.3 18.6 %collective-permute-start.19 = (f32[576,384]{1,0:T(8,128)S(1)}, f32[576,384]{1,0:T(8,128)S(1)}, u32[]{:S(2)}, u32[]{:S(2)}) collective-permute-start(f32[576,384]{1,0:T(8,128)S(1)} %dynamic-slice_bitcast_fusion), channel_id=1, source_target_pairs={{0,4},{4,0},{8,12},{12,8},{16,20},{20,16},{24,28},{28,24},{1,5},{5... | collective-permute-start | bytes 2654216 | tf_op jit(solution)/shard_map/ppermute | solution.py:181
  114.7 51.6 %collective-permute-start.8 = (f32[2,360,384]{2,1,0:T(8,128)}, f32[2,360,384]{2,1,0:T(8,128)S(1)}, u32[]{:S(2)}, u32[]{:S(2)}) collective-permute-start(f32[2,360,384]{2,1,0:T(8,128)} %bitcast.20), channel_id=1, source_target_pairs={{0,4},{4,0},{1,5},{5,1},{2,6},{6,2},{3,7},{7,3},{11,15},{15,11},{1... | collective-permute-start | bytes 3317768 | tf_op jit(solution)/shard_map/ppermute | solution.py:80
  124.1 11.4 %collective-permute-start.20 = (f32[288,384]{1,0:T(8,128)S(1)}, f32[288,384]{1,0:T(8,128)S(1)}, u32[]{:S(2)}, u32[]{:S(2)}) collective-permute-start(f32[288,384]{1,0:T(8,128)S(1)} %dynamic-slice_bitcast_fusion.5), channel_id=1, source_target_pairs={{0,8},{4,12},{8,0},{12,4},{16,24},{20,28},{24,16},{28,20},{1,9},{5... | collective-permute-start | bytes 1327112 | tf_op jit(solution)/shard_map/ppermute | solution.py:181
  143.3 9.0 %collective-permute-start.22 = (f32[108,128]{1,0:T(8,128)S(1)}, f32[108,128]{1,0:T(8,128)S(1)}, u32[]{:S(2)}, u32[]{:S(2)}) collective-permute-start(f32[108,128]{1,0:T(8,128)S(1)} %get-tuple-element.79), channel_id=1, source_target_pairs={{0,1},{1,0},{2,3},{3,2},{4,5},{5,4},{6,7},{7,6},{8,9},{9,8},{10,11... | collective-permute-start | bytes 165896 | tf_op jit(solution)/shard_map/ppermute | solution.py:187
  156.7 21.4 %collective-permute-start.16 = (f32[2,360,384]{2,1,0:T(8,128)}, f32[2,360,384]{2,1,0:T(8,128)}, u32[]{:S(2)}, u32[]{:S(2)}) collective-permute-start(f32[2,360,384]{2,1,0:T(8,128)} %bitcast.33), channel_id=1, source_target_pairs={{0,4},{4,0},{1,5},{5,1},{2,6},{6,2},{3,7},{7,3},{11,15},{15,11},{1... | collective-permute-start | bytes 3317768 | tf_op jit(solution)/shard_map/ppermute | solution.py:80
  173.4 13.1 %collective-permute-start.29 = (f32[288,384]{1,0:T(8,128)S(1)}, f32[288,384]{1,0:T(8,128)S(1)}, u32[]{:S(2)}, u32[]{:S(2)}) collective-permute-start(f32[288,384]{1,0:T(8,128)S(1)} %pad_maximum_fusion.8), channel_id=1, source_target_pairs={{0,8},{4,12},{8,0},{12,4},{16,24},{20,28},{24,16},{28,20},{1,9},{5... | collective-permute-start | bytes 1327112 | tf_op jit(solution)/shard_map/ppermute | solution.py:196
  175.9 19.5 %collective-permute-start.9 = (f32[360,384]{1,0:T(8,128)}, f32[360,384]{1,0:T(8,128)}, u32[]{:S(2)}, u32[]{:S(2)}) collective-permute-start(f32[360,384]{1,0:T(8,128)} %get-tuple-element.69), channel_id=1, source_target_pairs={{0,0},{4,1},{1,2},{5,3},{2,4},{6,5},{3,6},{7,7},{11,8},{15,9},{10,... | collective-permute-start | bytes 1658888 | tf_op jit(solution)/shard_map/ppermute | solution.py:80
  178.0 40.9 %collective-permute-start.10 = (f32[360,384]{1,0:T(8,128)}, f32[360,384]{1,0:T(8,128)}, u32[]{:S(2)}, u32[]{:S(2)}) collective-permute-start(f32[360,384]{1,0:T(8,128)} %get-tuple-element.70), channel_id=1, source_target_pairs={{1,0},{5,1},{0,2},{4,3},{3,4},{7,5},{2,6},{6,7},{10,8},{14,9},{11,... | collective-permute-start | bytes 1658888 | tf_op jit(solution)/shard_map/ppermute | solution.py:80
  180.6 40.8 %collective-permute-start.17 = (f32[360,384]{1,0:T(8,128)}, f32[360,384]{1,0:T(8,128)S(1)}, u32[]{:S(2)}, u32[]{:S(2)}) collective-permute-start(f32[360,384]{1,0:T(8,128)} %get-tuple-element.61), channel_id=1, source_target_pairs={{0,0},{4,1},{1,2},{5,3},{2,4},{6,5},{3,6},{7,7},{11,8},{15,9},{10,... | collective-permute-start | bytes 1658888 | tf_op jit(solution)/shard_map/ppermute | solution.py:80
  185.2 44.6 %collective-permute-start.18 = (f32[360,384]{1,0:T(8,128)}, f32[360,384]{1,0:T(8,128)}, u32[]{:S(2)}, u32[]{:S(2)}) collective-permute-start(f32[360,384]{1,0:T(8,128)} %get-tuple-element.62), channel_id=1, source_target_pairs={{1,0},{5,1},{0,2},{4,3},{3,4},{7,5},{2,6},{6,7},{10,8},{14,9},{11,... | collective-permute-start | bytes 1658888 | tf_op jit(solution)/shard_map/ppermute | solution.py:80
  186.6 45.5 %collective-permute-start.30 = (f32[576,384]{1,0:T(8,128)S(1)}, f32[576,384]{1,0:T(8,128)S(1)}, u32[]{:S(2)}, u32[]{:S(2)}) collective-permute-start(f32[576,384]{1,0:T(8,128)S(1)} %pad_maximum_fusion.7), channel_id=1, source_target_pairs={{0,4},{4,0},{8,12},{12,8},{16,20},{20,16},{24,28},{28,24},{1,5},{5... | collective-permute-start | bytes 2654216 | tf_op jit(solution)/shard_map/ppermute | solution.py:196
  (20 other events, 128.2 us)

commit v2 on v1

v2 whole, which is shorter than its diff:
```python
import math

import jax
import jax.numpy as jnp
import numpy as np
from jax import lax
from jax.experimental import pallas as pl
from jax.experimental.pallas import tpu as pltpu
from jax.sharding import PartitionSpec as P

AXES = ("lat", "lon")
SLOTS = 4
VMEM = 48 * 2**20
BF16 = jnp.bfloat16


class Layout:
    def __init__(self, lat, lon):
        self.lat, self.lon, self.pairs = lat, lon, lat // 2
        self.chips = lon // SLOTS
        self.share = 2 * self.chips

    def device(self, band, z):
        return band * self.lon + z

    def place(self, pair, rho, h):
        v = rho * self.chips + h // 2
        z = v if pair % 2 == 0 else self.lon - 1 - v
        return self.device(2 * pair + h % 2, z)

    def inward(self, t):
        pairs = []
        for band in range(self.lat):
            for z in range(self.lon):
                r = (z // self.share) ^ t
                dst = self.place(band // 2, 2 * (band % 2) + r, z % self.share)
                pairs.append((self.device(band, z), dst))
        return pairs

    def slots(self):
        for pair in range(self.pairs):
            for rho in range(SLOTS):
                for h in range(self.share):
                    yield pair, rho, h

    def within(self, g):
        return [(self.place(p, rho, h), self.place(p, rho, h ^ g)) for p, rho, h in self.slots()]

    def upward(self):
        pairs = []
        for p, rho, h in self.slots():
            q, sigma = (p, rho + 1) if rho + 1 < SLOTS else (p + 1, 0)
            if q < self.pairs:
                pairs.append((self.place(p, rho, h), self.place(q, sigma, h)))
        return pairs


def after(x, *others):
    return lax.optimization_barrier((x,) + others)[0]


def flipped(pairs):
    return [(b, a) for a, b in pairs]


def tables(length, modes, lon, share):
    n = np.arange(length)
    m = np.arange(modes)
    angle = (n[:, None] * m[None, :] % length) * (2.0 * math.pi / length)
    root = np.sqrt(np.where(m == 0, 1.0, 2.0) / length)
    part_len, width = length // lon, modes // share
    wide = -(-width // 16) * 16
    parts = np.stack([(f * root).reshape(lon, part_len, share, width) for f in (np.cos(angle), -np.sin(angle))])
    out = np.zeros((share, 2, 2 * share, wide, 2 * wide), np.float32)
    for h in range(share):
        for g in range(share):
            for b in range(2):
                for half in range(2):
                    block = parts[half, b * share + (h ^ g), :, h]
                    out[h, 0, half * share + g, :width, b * part_len : (b + 1) * part_len] = block.T
                    out[h, 1, 2 * g + b, :part_len, half * wide : half * wide + width] = block
    return np.stack(split(out)), wide


def split(x):
    high = x.astype(BF16)
    return high, (x - high.astype(np.float32)).astype(BF16)


def split_outside(x):
    high = lax.reduce_precision(x, 8, 7)
    return high.astype(BF16), (x - high).astype(BF16)


def dot3(a, b, dims=(((1,), (0,)), ((), ()))):
    out = lax.dot_general(a[0], b[0], dims, preferred_element_type=jnp.float32)
    out += lax.dot_general(a[0], b[1], dims, preferred_element_type=jnp.float32)
    return out + lax.dot_general(a[1], b[0], dims, preferred_element_type=jnp.float32)


WHOLE = pl.BlockSpec(memory_space=pltpu.VMEM)
REMAIN = pl.BlockSpec(memory_space=pltpu.HBM)
CHEAP = pl.CostEstimate(flops=1, bytes_accessed=1, transcendentals=0)


def kernel_call(body, grid, in_specs, out_specs, out_shape, scratch=()):
    return pl.pallas_call(
        body,
        grid_spec=pltpu.PrefetchScalarGridSpec(
            num_scalar_prefetch=1, grid=grid, in_specs=in_specs, out_specs=out_specs, scratch_shapes=list(scratch)
        ),
        out_shape=out_shape,
        compiler_params=pltpu.CompilerParams(vmem_limit_bytes=VMEM),
        cost_estimate=CHEAP,
    )


def copies(table, blocks, buffers, sems):
    started = []
    for i, block in enumerate(blocks):
        pair = [pltpu.make_async_copy(table.at[(term, *block)], buffers.at[term, i], sems.at[term, i]) for term in range(2)]
        for copy in pair:
            copy.start()
        started.append(pair)
    return started


def fetched(refs, buffer, sems):
    started = [pltpu.make_async_copy(ref, buffer.at[i], sems.at[i]) for i, ref in enumerate(refs)]
    for copy in started:
        copy.start()
    return started


def arrived(pair):
    for copy in pair:
        copy.wait()


def transform(place, blocks, table):
    share, wide, wide2 = table.shape[1], *table.shape[-2:]
    channels = blocks[0].shape[-1]
    count = len(blocks)

    def body(place, *refs):
        ins, (table, out, x, v, sems, held, held_sems) = refs[:count], refs[count:]
        loads = fetched(ins, held, held_sems)
        pairs = copies(table, [(place[0], 0, i) for i in range(2 * share)], v, sems)
        for g in range(share):
            if count == 1:
                if g == 0:
                    arrived(loads)
                x[0, g], x[1, g] = split(held[0, g])
                continue
            arrived(loads[2 * g : 2 * g + 2])
            a, b = held[2 * g], held[2 * g + 1]
            swap = place[1] == 1
            size = 2 * a.shape[0]
            pair = jnp.concatenate([jnp.where(swap, b, a), jnp.where(swap, a, b)], axis=0)
            x[0, g, :size, :], x[1, g, :size, :] = split(pair)
            for term in range(2):
                x[term, g, size:, :] = jnp.zeros((wide2 - size, channels), BF16)
        for half in range(2):
            total = 0.0
            for g in range(share):
                i = half * share + g
                arrived(pairs[i])
                total += dot3((v[0, i], v[1, i]), (x[0, g], x[1, g]))
            out[half * wide : (half + 1) * wide, :] = total

    return kernel_call(
        body,
        (),
        [REMAIN] * (count + 1),
        WHOLE,
        jax.ShapeDtypeStruct((wide2, channels), jnp.float32),
        [
            pltpu.VMEM((2, share, wide2, channels), BF16),
            pltpu.VMEM((2, 2 * share, wide, wide2), BF16),
            pltpu.SemaphoreType.DMA((2, 2 * share)),
            pltpu.VMEM((count, *blocks[0].shape), jnp.float32),
            pltpu.SemaphoreType.DMA((count,)),
        ],
    )(place, *blocks, table)


def mix(place, rows, coef, weights, table, part_len, gradient=None):
    share, wide, wide2 = table.shape[1], *table.shape[-2:]
    channels = weights[0].shape[1]
    deep = weights[0].shape[0]
    basis = deep // channels
    chunk = 16
    count = 2 * share
    rows = [*rows] + ([] if gradient is None else [gradient])
    n_rows = len(rows)
    n_in = n_rows + 4

    def body(place, *refs):
        coef, wh, wl, table = refs[n_rows:n_in]
        ys, rest = refs[n_in : n_in + count], refs[n_in + count :]
        if gradient is not None:
            out, gh, gl, *rest = rest
        fh, fl, oh, ol, v, sems, held, held_sems, w, w_sems = rest
        loads = fetched(refs[:n_rows], held, held_sems)
        w_loads = fetched((wh, wl), w, w_sems)
        blocks = [(place[0], 1, 2 * (i // 2) + (place[1] ^ (i % 2))) for i in range(count)]
        pairs = copies(table, blocks, v, sems)
        arrived(loads)

        @pl.loop(0, wide // chunk)
        def _(i):
            re_at = pl.ds(pl.multiple_of(i * chunk, chunk), chunk)
            im_at = pl.ds(pl.multiple_of(wide + i * chunk, chunk), chunk)
            c = coef[re_at, :]
            data = [(held[d, re_at, :], held[d, im_at, :]) for d in range(3)]
            for k in range(basis):
                re, im = 0.0, 0.0
                for d, (xr, xi) in enumerate(data):
                    at = (d * basis + k) * 2
                    pr, pi = c[:, at : at + 1], c[:, at + 1 : at + 2]
                    re += pr * xr - pi * xi
                    im += pr * xi + pi * xr
                cols = pl.ds(k * channels, channels)
                fh[re_at, cols], fl[re_at, cols] = split(re)
                fh[im_at, cols], fl[im_at, cols] = split(im)

        arrived(w_loads)
        oh[...], ol[...] = split(dot3((fh[...], fl[...]), (w[0], w[1])))
        for i, y in enumerate(ys):
            arrived(pairs[i])
            y[...] = dot3((v[0, i], v[1, i]), (oh[...], ol[...]))[:part_len]
        if gradient is not None:
            gh[...], gl[...] = split(held[3])
            for k in range(basis):
                at = pl.ds(k * channels, channels)
                out[at, :] = dot3((fh[:, at], fl[:, at]), (gh[...], gl[...]), (((0,), (0,)), ((), ())))

    y_shape = jax.ShapeDtypeStruct((part_len, channels), jnp.float32)
    extra, scratch = [], []
    if gradient is not None:
        extra = [jax.ShapeDtypeStruct((deep, channels), jnp.float32)]
        scratch = [pltpu.VMEM((wide2, channels), BF16)] * 2
    return kernel_call(
        body,
        (),
        [REMAIN] * n_rows + [WHOLE] + [REMAIN] * 3,
        [WHOLE] * (count + len(extra)),
        [y_shape] * count + extra,
        scratch
        + [pltpu.VMEM((wide2, deep), BF16)] * 2
        + [pltpu.VMEM((wide2, channels), BF16)] * 2
        + [pltpu.VMEM((2, count, wide, wide2), BF16), pltpu.SemaphoreType.DMA((2, count))]
        + [pltpu.VMEM((n_rows, wide2, channels), jnp.float32), pltpu.SemaphoreType.DMA((n_rows,))]
        + [pltpu.VMEM((2, deep, channels), BF16), pltpu.SemaphoreType.DMA((2,))],
    )(place, *rows, coef, *weights, table)


def arrange(flags, got):
    part_len, channels = got[0].shape

    def body(flags, a, b, out):
        swap, full = flags[0] == 1, flags[1] == 1
        x, y = a[...], b[...]
        first, second = jnp.where(swap, y, x), jnp.where(swap, x, y)
        out[0] = jnp.where(full, first, first + second)
        out[1] = jnp.where(full, second, 0.0)

    return kernel_call(
        body,
        (),
        [WHOLE, WHOLE],
        WHOLE,
        jax.ShapeDtypeStruct((2, part_len, channels), jnp.float32),
    )(flags, *got)


def shares_sent(x, axis, me, ways, stride):
    parts = x.reshape(ways, -1, x.shape[-1])
    size = lax.axis_size(axis)
    pieces = [lax.dynamic_index_in_dim(parts, me, 0, keepdims=False)]
    for g in range(1, ways):
        piece = lax.dynamic_index_in_dim(parts, me ^ g, 0, keepdims=False)
        pieces.append(lax.ppermute(piece, axis, [(a, a ^ (g * stride)) for a in range(size)]))
    return pieces


def shares_summed(pieces):
    total = pieces[0]
    for piece in pieces[1:]:
        total = total + piece
    return total


def shares_joined(x, axis, me, ways, stride):
    size = lax.axis_size(axis)
    whole = jnp.zeros((ways,) + x.shape, x.dtype)
    whole = lax.dynamic_update_index_in_dim(whole, x, me, 0)
    for g in range(1, ways):
        piece = lax.ppermute(x, axis, [(a, a ^ (g * stride)) for a in range(size)])
        whole = lax.dynamic_update_index_in_dim(whole, piece, me ^ g, 0)
    return whole.reshape((-1,) + x.shape[1:])


def make_local(lat, lon):
    lay = Layout(lat, lon)
    share = lay.share

    def send(x, pairs):
        return lax.ppermute(x, AXES, pairs)

    def local(signal, band_rows, filter_modes, mixing, cotangent):
        channels = signal.shape[2]
        part_len = signal.shape[1]
        length = part_len * lon
        modes = filter_modes.shape[-1]
        basis = mixing.shape[0]
        width = modes // share

        band = lax.axis_index("lat")
        z = lax.axis_index("lon")
        core = band % 2
        v = jnp.where((band // 2) % 2 == 0, z, lon - 1 - z)
        rho = v // lay.chips
        h = (v % lay.chips) * 2 + core
        r_held = rho % 2
        live = lax.dynamic_index_in_dim(band_rows, band, 0, keepdims=False)
        full = live == 2
        high_z = z // share

        table, wide = tables(length, modes, lon, share)
        table = jnp.asarray(table)
        place = jnp.stack([h, r_held]).astype(jnp.int32)
        flags = jnp.stack([high_z, full.astype(jnp.int32)]).astype(jnp.int32)

        def fetch(x, then=None):
            got = []
            for t in range(2):
                row = jnp.minimum(high_z ^ t, live - 1)
                message = lax.dynamic_index_in_dim(x, row, 0, keepdims=False)
                if then is not None:
                    message = after(message, *then)
                got.append(send(message, lay.inward(t)))
            return got

        def enter(got):
            blocks = list(got)
            for g in range(1, share):
                blocks += [send(x, lay.within(g)) for x in got]
            if part_len % 8:
                pairs = []
                for x, y in zip(blocks[::2], blocks[1::2]):
                    pairs += [jnp.where(r_held == 0, x, y), jnp.where(r_held == 0, y, x)]
                blocks = jnp.concatenate(pairs, axis=0).reshape(share, 2 * part_len, channels)
                blocks = [jnp.pad(blocks, ((0, 0), (0, 2 * (wide - part_len)), (0, 0)))]
            return transform(place, blocks, table)

        def exchange(y):
            return [[send(y[2 * g + t], lay.within(g)) for t in range(2)] for g in range(1, share)]

        def total(own, others):
            return [own[t] + sum(other[t] for other in others) for t in range(2)]

        def deliver(block, t):
            return send(block, flipped(lay.inward(t)))

        def halo(spec):
            return send(spec, lay.upward()), send(spec, flipped(lay.upward()))

        s_got = fetch(signal)
        f = after(filter_modes, *s_got)
        ladder = [(i, i + 1) for i in range(lat - 1)]
        below = lax.ppermute(jnp.where(full, f[1, 2], f[0, 2]), "lat", ladder)
        above = lax.ppermute(f[0, 0], "lat", flipped(ladder))
        nil = jnp.zeros_like(below)
        is_first = r_held == 0
        ahead = [
            jnp.where(is_first, f[0, 0], jnp.where(full, f[1, 0], nil)),
            jnp.where(is_first, f[0, 1], jnp.where(full, f[1, 1], nil)),
            jnp.where(is_first, jnp.where(full, f[0, 2], nil), jnp.where(full, f[1, 2], f[0, 2])),
        ]
        back = [
            jnp.where(is_first, below, jnp.where(full, f[0, 2], nil)),
            jnp.where(is_first, f[0, 1], jnp.where(full, f[1, 1], nil)),
            jnp.where(is_first, jnp.where(full, f[1, 0], nil), above),
        ]
        conj = jnp.array([1.0, -1.0], jnp.float32)[None, None, :, None]
        both = jnp.stack([jnp.stack(ahead), jnp.stack(back) * conj])
        both = both.reshape(2 * 3 * basis * 2, modes)
        swap = [(i, i ^ 1) for i in range(lat)]
        theirs = lax.ppermute(lax.dynamic_slice_in_dim(both, (h ^ 1) * width, width, 1), "lat", swap)
        mine = lax.dynamic_slice_in_dim(both, h * width, width, 1)
        coef = jnp.where(rho // 2 == core, mine, theirs).reshape(2, 3 * basis * 2, width)
        coef = jnp.pad(jnp.transpose(coef, (0, 2, 1)), ((0, 0), (0, wide - width), (0, 0)))

        flat = (basis * channels, channels)
        ahead_weights = split_outside(mixing.reshape(flat))
        back_weights = split_outside(jnp.transpose(mixing, (0, 2, 1)).reshape(flat))

        pair = band // 2
        even = (basis * channels // lat) * channels % (lon * 128) == 0

        def swap_core(x):
            return lax.ppermute(x, "lat", swap)

        s_got = [after(x, *ahead_weights, *back_weights) for x in s_got]
        g_got = fetch(cotangent, s_got)
        s_spec = enter(s_got)
        g_got = [after(x, s_spec, coef) for x in g_got]
        s_halo = halo(after(s_spec, *g_got))
        g_spec = enter(g_got)
        s_halo = [after(x, g_spec) for x in s_halo]
        g_halo = halo(g_spec)
        *y, term = mix(place, (s_halo[0], s_spec, s_halo[1]), coef[0], ahead_weights, table, part_len, g_spec)
        g_halo = [after(x, *y) for x in g_halo]
        others = exchange([after(x, *g_halo) for x in y])
        halves = term.reshape(2, -1, channels)
        give = after(lax.dynamic_index_in_dim(halves, 1 - core, 0, keepdims=False), *g_halo)
        given = swap_core(give)
        o_blocks = total(y, others)

        o_got = [deliver(x, t) for t, x in enumerate(o_blocks)]
        term = lax.dynamic_index_in_dim(halves, core, 0, keepdims=False) + after(given, *o_blocks)
        pieces = shares_sent(term, "lat", pair, lay.pairs, 2)
        g_halo = [after(x, *o_blocks, term) for x in g_halo]
        y = mix(place, (g_halo[0], g_spec, g_halo[1]), coef[1], back_weights, table, part_len)
        o_got = [after(x, *y) for x in o_got]
        y = [after(x, *o_got) for x in y]
        others = exchange(y)
        term = shares_summed([after(x, *o_got) for x in pieces])
        term_shape = term.shape
        term = term.reshape((-1, 128) if even else (lon, -1))
        pieces = shares_sent(term, "lon", z, lon, 1)
        b_blocks = total(y, others)
        term = shares_summed([after(x, *b_blocks) for x in pieces])
        b_got = [deliver(after(x, term), t) for t, x in enumerate(b_blocks)]
        term = shares_joined(term, "lon", z, lon, 1).reshape(term_shape)
        output = arrange(flags, o_got)
        b_got = [after(x, output) for x in b_got]
        term = shares_joined(term, "lat", pair, lay.pairs, 2)
        b_got = [after(x, term) for x in b_got]
        other = swap_core(after(term, *b_got))
        grad_signal = arrange(flags, b_got)
        term = jnp.concatenate([jnp.where(core == 0, term, other), jnp.where(core == 0, other, term)], axis=0)
        weight_grad = term.reshape(mixing.shape)
        return output, grad_signal, weight_grad

    return local


def solution(mesh):
    lat, lon = mesh.shape["lat"], mesh.shape["lon"]
    grid = P("lat", "lon", None)
    return jax.shard_map(
        make_local(lat, lon),
        mesh=mesh,
        in_specs=(grid, P(), P("lat", None, None, None, None), P(), grid),
        out_specs=(grid, grid, P()),
        check_vma=False,
    )
```

time: 235 us -> 210 us (0.89)
  the two profiles are of different devices: /device:TPU:2 before, /device:TPU:0 now
where the time goes in v2:
time: 210 us; the launch traced here: 207 us
  starting transfers between devices  63.7 us (30%)
  waiting for transfers between devices  61.2 us (29%)
  Pallas kernels  47 us (22%)
  local copies, waits for them, and re-layouts  21.2 us (10%)
  other arithmetic  11.4 us (5%)
  between operations  2.39 us (1%)
    ppermute x20, waiting for transfers between devices, send(): return lax.ppermute(x, AXES, pairs)  40 us
    ppermute x20, starting transfers between devices, send(): return lax.ppermute(x, AXES, pairs)  34.4 us
    pallas_call x2, Pallas kernels, mix(): kernel_call(body, (), [REMAIN] * n_rows + [WHOLE] + [REMAIN] * 3, [WHOLE]...  31.3 us
    ppermute x6, waiting for transfers between devices, shares_joined(): piece = lax.ppermute(x, axis, [(a, a ^ g * stride) for a in range(size)])  15.4 us
    pallas_call x2, Pallas kernels, transform(): kernel_call(body, (), [REMAIN] * (count + 1), WHOLE, jax.ShapeDtypeStruct...  12.4 us
    ppermute x6, starting transfers between devices, shares_joined(): piece = lax.ppermute(x, axis, [(a, a ^ g * stride) for a in range(size)])  9.35 us
    ppermute x2, starting transfers between devices, swap_core(): return lax.ppermute(x, 'lat', swap)  8.84 us
    ppermute x6, starting transfers between devices, shares_sent(): lax.ppermute(piece, axis, [(a, a ^ g * stride) for a in range(size)])  8.26 us
  transfers between devices with their start and end apart: 37, of which 15 were waited for; matrix products, arithmetic and copies ran while one was open for 10% of the time, Pallas kernels for 23%

profile of v2, /device:TPU:0, one launch (start us, length us, event | category | flops | bytes accessed | tf_op | source)
XLA Modules:
  0.0 206.9 jit_solution(3721270759048897753)
XLA Ops:
  2.7 2.3 %dynamic-slice_bitcast_fusion.3 = (f32[360,384]{1,0:T(8,128)}, f32[360,384]{1,0:T(8,128)}) fusion(f32[2,360,384]{2,1,0:T(8,128)} %param.7, s32[]{:T(128)S(6)} %select_n.249, s32[]{:T(128)S(6)} %select_n.248), kind=kLoop, calls=%fused_computation.11 | loop fusion | bytes 2211848 | tf_op jit(solution)/shard_map/jit(dynamic_index_in_dim)/squeeze | solution.py:339
  6.7 3.3 %collective-permute-start.1 = (f32[360,384]{1,0:T(8,128)}, f32[360,384]{1,0:T(8,128)S(1)}, u32[]{:S(2)}, u32[]{:S(2)}) collective-permute-start(f32[360,384]{1,0:T(8,128)} %get-tuple-element.109), channel_id=1, source_target_pairs={{0,1},{1,5},{2,0},{3,4},{4,3},{5,7},{6,2},{7,6},{8,10},{9,14},{10,... | collective-permute-start | bytes 1658888 | tf_op jit(solution)/shard_map/ppermute | solution.py:309
  12.5 2.4 %dynamic-slice_bitcast_fusion.1 = (f32[360,384]{1,0:T(8,128)}, f32[360,384]{1,0:T(8,128)}) fusion(f32[2,360,384]{2,1,0:T(8,128)} %param.11, s32[]{:T(128)S(6)} %select_n.249, s32[]{:T(128)S(6)} %select_n.248), kind=kLoop, calls=%fused_computation.9 | loop fusion | bytes 2211848 | tf_op jit(solution)/shard_map/jit(dynamic_index_in_dim)/squeeze | solution.py:339
  14.9 3.9 %fusion = (bf16[1152,384]{1,0:T(8,128)(2,1)}, bf16[1152,384]{1,0:T(8,128)(2,1)}, bf16[1152,384]{1,0:T(8,128)(2,1)S(1)}, bf16[1152,384]{1,0:T(8,128)(2,1)}) fusion(f32[3,384,384]{2,1,0:T(8,128)} %param.10, f32[3,384,384]{2,1,0:T(8,128)} %copy.11), kind=kLoop, calls=%fused_computation.4 | loop fusion | flops 3538944 | bytes 7077888 | tf_op jit(solution)/shard_map/convert_element_type | solution.py:92
  18.8 18.0 %collective-permute-done.1.refs_1_ = f32[360,384]{1,0:T(8,128)S(1)} collective-permute-done((f32[360,384]{1,0:T(8,128)}, f32[360,384]{1,0:T(8,128)S(1)}, u32[]{:S(2)}, u32[]{:S(2)}) %collective-permute-start.1) | collective-permute-done | bytes 552992 | tf_op jit(solution)/shard_map/ppermute | solution.py:309
  37.3 5.9 %collective-permute-start.4 = (f32[360,384]{1,0:T(8,128)}, f32[360,384]{1,0:T(8,128)}, u32[]{:S(2)}, u32[]{:S(2)}) collective-permute-start(f32[360,384]{1,0:T(8,128)} %get-tuple-element.53), channel_id=1, source_target_pairs={{0,0},{1,4},{2,1},{3,5},{4,2},{5,6},{6,3},{7,7},{8,11},{9,15},{10,... | collective-permute-start | bytes 1658888 | tf_op jit(solution)/shard_map/ppermute | solution.py:309
  54.1 6.1 %shard_map.94.refs_1_ = f32[736,384]{1,0:T(8,128)S(1)} custom-call(s32[2]{0:T(128)S(1)} %pad_add_fusion.1.place, f32[360,384]{1,0:T(8,128)S(1)} %collective-permute-done.refs_0_, f32[360,384]{1,0:T(8,128)S(1)} %collective-permute-done.1.refs_1_, f32[360,384]{1,0:T(8,128)S(1)} %copy-done.6, f32[360,384]{1,0:T(8,128)S(1)} %copy-done.8, ...), custom_call_target="tpu_custom_call" | custom-call | flops 1 | bytes 1 | tf_op jit(solution)/shard_map/pallas_call | solution.py:171
  60.2 4.2 %collective-permute-done.8.refs_1_ = f32[360,384]{1,0:T(8,128)} collective-permute-done((f32[360,384]{1,0:T(8,128)}, f32[360,384]{1,0:T(8,128)}, u32[]{:S(2)}, u32[]{:S(2)}) %collective-permute-start.8) | collective-permute-done | bytes 552992 | tf_op jit(solution)/shard_map/ppermute | solution.py:309
  65.0 2.3 %collective-permute-start.9 = (f32[736,384]{1,0:T(8,128)S(1)}, f32[736,384]{1,0:T(8,128)}, u32[]{:S(2)}, u32[]{:S(2)}) collective-permute-start(f32[736,384]{1,0:T(8,128)S(1)} %shard_map.94.refs_1_), channel_id=1, source_target_pairs={{0,1},{4,5},{1,2},{5,6},{2,3},{6,7},{3,11},{7,15},{11,10},{15,14},... | collective-permute-start | bytes 3391496 | tf_op jit(solution)/shard_map/ppermute | solution.py:309
  68.6 6.3 %shard_map.95.refs_3_.refs_1_ = f32[736,384]{1,0:T(8,128)S(1)} custom-call(s32[2]{0:T(128)S(1)} %pad_add_fusion.1.place, f32[360,384]{1,0:T(8,128)} %collective-permute-done.4.refs_0_, f32[360,384]{1,0:T(8,128)} %collective-permute-done.8.refs_1_, f32[360,384]{1,0:T(8,128)S(1)} %collective-permute-done.10.refs_2_, ...), custom_call_target="tpu_custom_call" | custom-call | flops 1 | bytes 1 | tf_op jit(solution)/shard_map/pallas_call | solution.py:171
  74.9 5.6 %collective-permute-start.13 = (f32[736,384]{1,0:T(8,128)S(1)}, f32[736,384]{1,0:T(8,128)}, u32[]{:S(2)}, u32[]{:S(2)}) collective-permute-start(f32[736,384]{1,0:T(8,128)S(1)} %shard_map.95.refs_3_.refs_1_), channel_id=1, source_target_pairs={{0,1},{4,5},{1,2},{5,6},{2,3},{6,7},{3,11},{7,15},{11,10},{15,14},... | collective-permute-start | bytes 3391496 | tf_op jit(solution)/shard_map/ppermute | solution.py:309
  83.0 8.5 %collective-permute-done.9.refs_0_ = f32[736,384]{1,0:T(8,128)} collective-permute-done((f32[736,384]{1,0:T(8,128)S(1)}, f32[736,384]{1,0:T(8,128)}, u32[]{:S(2)}, u32[]{:S(2)}) %collective-permute-start.9) | collective-permute-done | bytes 1130528 | tf_op jit(solution)/shard_map/ppermute | solution.py:309
  91.5 5.6 %collective-permute-done.12.refs_2_ = f32[736,384]{1,0:T(8,128)} collective-permute-done((f32[736,384]{1,0:T(8,128)S(1)}, f32[736,384]{1,0:T(8,128)}, u32[]{:S(2)}, u32[]{:S(2)}) %collective-permute-start.12) | collective-permute-done | bytes 1130528 | tf_op jit(solution)/shard_map/ppermute | solution.py:309
  99.4 17.4 %shard_map.96 = (f32[360,384]{1,0:T(8,128)S(1)}, f32[360,384]{1,0:T(8,128)S(1)}, f32[360,384]{1,0:T(8,128)S(1)}, f32[360,384]{1,0:T(8,128)S(1)}, f32[1152,384]{1,0:T(8,128)}) custom-call(s32[2]{0:T(128)S(1)} %pad_add_fusion.1.place, f32[736,384]{1,0:T(8,128)} %collective-permute-done.9.refs_0_, f32[736,384]{1,0:T(8,128)} %copy-done.1, ...), custom_call_target="tpu_custom_call" | custom-call | flops 1 | bytes 1 | tf_op jit(solution)/shard_map/pallas_call | solution.py:243
  120.8 2.3 %collective-permute-done.15 = f32[360,384]{1,0:T(8,128)S(1)} collective-permute-done((f32[360,384]{1,0:T(8,128)S(1)}, f32[360,384]{1,0:T(8,128)S(1)}, u32[]{:S(2)}, u32[]{:S(2)}) %collective-permute-start.15) | collective-permute-done | bytes 552992 | tf_op jit(solution)/shard_map/ppermute | solution.py:309
  126.6 3.1 %collective-permute-start.19 = (f32[360,384]{1,0:T(8,128)}, f32[360,384]{1,0:T(8,128)S(1)}, u32[]{:S(2)}, u32[]{:S(2)}) collective-permute-start(f32[360,384]{1,0:T(8,128)} %add.125), channel_id=1, source_target_pairs={{1,0},{5,1},{0,2},{4,3},{3,4},{7,5},{2,6},{6,7},{10,8},{14,9},{11,... | collective-permute-start | bytes 1658888 | tf_op jit(solution)/shard_map/ppermute | solution.py:309
  132.5 2.9 %collective-permute-start.22 = (f32[144,384]{1,0:T(8,128)}, f32[144,384]{1,0:T(8,128)}, u32[]{:S(2)}, u32[]{:S(2)}) collective-permute-start(f32[144,384]{1,0:T(8,128)} %get-tuple-element.113), channel_id=1, source_target_pairs={{0,16},{4,20},{8,24},{12,28},{16,0},{20,4},{24,8},{28,12},{1,17},{... | collective-permute-start | bytes 663560 | tf_op jit(solution)/shard_map/ppermute | solution.py:283
  135.9 13.9 %shard_map.97 = (f32[360,384]{1,0:T(8,128)S(1)}, f32[360,384]{1,0:T(8,128)S(1)}, f32[360,384]{1,0:T(8,128)}, f32[360,384]{1,0:T(8,128)}) custom-call(s32[2]{0:T(128)S(1)} %pad_add_fusion.1.place, f32[736,384]{1,0:T(8,128)} %collective-permute-done.13.refs_0_, f32[736,384]{1,0:T(8,128)} %copy-done, f32[736,384]{1,0:T(8,128)} %collective-permute-done.14.refs_2_, ...), custom_call_target="tpu_custom_call" | custom-call | flops 1 | bytes 1 | tf_op jit(solution)/shard_map/pallas_call | solution.py:243
  149.8 3.6 %collective-permute-start.20 = (f32[360,384]{1,0:T(8,128)}, f32[360,384]{1,0:T(8,128)S(1)}, u32[]{:S(2)}, u32[]{:S(2)}) collective-permute-start(f32[360,384]{1,0:T(8,128)} %get-tuple-element.81), channel_id=1, source_target_pairs={{0,4},{4,0},{1,5},{5,1},{2,6},{6,2},{3,7},{7,3},{11,15},{15,11},{1... | collective-permute-start | bytes 1658888 | tf_op jit(solution)/shard_map/ppermute | solution.py:309
  156.2 3.0 %collective-permute-start.25 = (f32[108,128]{1,0:T(8,128)S(1)}, f32[108,128]{1,0:T(8,128)S(1)}, u32[]{:S(2)}, u32[]{:S(2)}) collective-permute-start(f32[108,128]{1,0:T(8,128)S(1)} %get-tuple-element.117), channel_id=1, source_target_pairs={{0,1},{1,0},{2,3},{3,2},{4,5},{5,4},{6,7},{7,6},{8,9},{9,8},{10,11... | collective-permute-start | bytes 165896 | tf_op jit(solution)/shard_map/ppermute | solution.py:283
  167.8 2.6 %collective-permute-done.30 = f32[108,128]{1,0:T(8,128)S(1)} collective-permute-done((f32[108,128]{1,0:T(8,128)S(1)}, f32[108,128]{1,0:T(8,128)S(1)}, u32[]{:S(2)}, u32[]{:S(2)}) %collective-permute-start.30) | collective-permute-done | bytes 55328 | tf_op jit(solution)/shard_map/ppermute | solution.py:299
  172.4 4.2 %collective-permute-start.32 = (f32[144,384]{1,0:T(8,128)}, f32[144,384]{1,0:T(8,128)}, u32[]{:S(2)}, u32[]{:S(2)}) collective-permute-start(f32[144,384]{1,0:T(8,128)} %reshape_reshape.7), channel_id=1, source_target_pairs={{0,8},{4,12},{8,0},{12,4},{16,24},{20,28},{24,16},{28,20},{1,9},{5... | collective-permute-start | bytes 663560 | tf_op jit(solution)/shard_map/ppermute | solution.py:299
  183.1 11.4 %collective-permute-done.33 = f32[144,384]{1,0:T(8,128)S(1)} collective-permute-done((f32[144,384]{1,0:T(8,128)}, f32[144,384]{1,0:T(8,128)S(1)}, u32[]{:S(2)}, u32[]{:S(2)}) %collective-permute-start.33) | collective-permute-done | bytes 221216 | tf_op jit(solution)/shard_map/ppermute | solution.py:299
  194.6 8.8 %collective-permute-start.36 = (f32[576,384]{1,0:T(8,128)S(1)}, f32[576,384]{1,0:T(8,128)S(1)}, u32[]{:S(2)}, u32[]{:S(2)}) collective-permute-start(f32[576,384]{1,0:T(8,128)S(1)} %bitcast.90), channel_id=1, source_target_pairs={{0,4},{4,0},{8,12},{12,8},{16,20},{20,16},{24,28},{28,24},{1,5},{5... | collective-permute-start | bytes 2654216 | tf_op jit(solution)/shard_map/ppermute | solution.py:403
  (122 shorter events, 56.9 us)
Async XLA Ops:
  5.0 13.8 %collective-permute-start = (f32[360,384]{1,0:T(8,128)}, f32[360,384]{1,0:T(8,128)S(1)}, u32[]{:S(2)}, u32[]{:S(2)}) collective-permute-start(f32[360,384]{1,0:T(8,128)} %get-tuple-element.110), channel_id=1, source_target_pairs={{0,0},{1,4},{2,1},{3,5},{4,2},{5,6},{6,3},{7,7},{8,11},{9,15},{10,... | collective-permute-start | bytes 1658888 | tf_op jit(solution)/shard_map/ppermute | solution.py:309
  6.7 30.1 %collective-permute-start.1 = (f32[360,384]{1,0:T(8,128)}, f32[360,384]{1,0:T(8,128)S(1)}, u32[]{:S(2)}, u32[]{:S(2)}) collective-permute-start(f32[360,384]{1,0:T(8,128)} %get-tuple-element.109), channel_id=1, source_target_pairs={{0,1},{1,5},{2,0},{3,4},{4,3},{5,7},{6,2},{7,6},{8,10},{9,14},{10,... | collective-permute-start | bytes 1658888 | tf_op jit(solution)/shard_map/ppermute | solution.py:309
  36.8 13.5 %collective-permute-start.2 = (f32[360,384]{1,0:T(8,128)S(1)}, f32[360,384]{1,0:T(8,128)S(1)}, u32[]{:S(2)}, u32[]{:S(2)}) collective-permute-start(f32[360,384]{1,0:T(8,128)S(1)} %collective-permute-done.refs_0_), channel_id=1, source_target_pairs={{0,4},{4,0},{1,5},{5,1},{2,6},{6,2},{3,7},{7,3},{11,15},{15,11},{1... | collective-permute-start | bytes 1658888 | tf_op jit(solution)/shard_map/ppermute | solution.py:309
  36.8 14.3 %collective-permute-start.3 = (f32[360,384]{1,0:T(8,128)S(1)}, f32[360,384]{1,0:T(8,128)S(1)}, u32[]{:S(2)}, u32[]{:S(2)}) collective-permute-start(f32[360,384]{1,0:T(8,128)S(1)} %collective-permute-done.1.refs_1_), channel_id=1, source_target_pairs={{0,4},{4,0},{1,5},{5,1},{2,6},{6,2},{3,7},{7,3},{11,15},{15,11},{1... | collective-permute-start | bytes 1658888 | tf_op jit(solution)/shard_map/ppermute | solution.py:309
  37.3 22.9 %collective-permute-start.4 = (f32[360,384]{1,0:T(8,128)}, f32[360,384]{1,0:T(8,128)}, u32[]{:S(2)}, u32[]{:S(2)}) collective-permute-start(f32[360,384]{1,0:T(8,128)} %get-tuple-element.53), channel_id=1, source_target_pairs={{0,0},{1,4},{2,1},{3,5},{4,2},{5,6},{6,3},{7,7},{8,11},{9,15},{10,... | collective-permute-start | bytes 1658888 | tf_op jit(solution)/shard_map/ppermute | solution.py:309
  45.9 18.6 %collective-permute-start.8 = (f32[360,384]{1,0:T(8,128)}, f32[360,384]{1,0:T(8,128)}, u32[]{:S(2)}, u32[]{:S(2)}) collective-permute-start(f32[360,384]{1,0:T(8,128)} %get-tuple-element.56), channel_id=1, source_target_pairs={{0,1},{1,5},{2,0},{3,4},{4,3},{5,7},{6,2},{7,6},{8,10},{9,14},{10,... | collective-permute-start | bytes 1658888 | tf_op jit(solution)/shard_map/ppermute | solution.py:309
  65.0 26.5 %collective-permute-start.9 = (f32[736,384]{1,0:T(8,128)S(1)}, f32[736,384]{1,0:T(8,128)}, u32[]{:S(2)}, u32[]{:S(2)}) collective-permute-start(f32[736,384]{1,0:T(8,128)S(1)} %shard_map.94.refs_1_), channel_id=1, source_target_pairs={{0,1},{4,5},{1,2},{5,6},{2,3},{6,7},{3,11},{7,15},{11,10},{15,14},... | collective-permute-start | bytes 3391496 | tf_op jit(solution)/shard_map/ppermute | solution.py:309
  67.3 29.8 %collective-permute-start.12 = (f32[736,384]{1,0:T(8,128)S(1)}, f32[736,384]{1,0:T(8,128)}, u32[]{:S(2)}, u32[]{:S(2)}) collective-permute-start(f32[736,384]{1,0:T(8,128)S(1)} %shard_map.94.refs_1_), channel_id=1, source_target_pairs={{1,0},{5,4},{2,1},{6,5},{3,2},{7,6},{11,3},{15,7},{10,11},{14,15},... | collective-permute-start | bytes 3391496 | tf_op jit(solution)/shard_map/ppermute | solution.py:309
  74.9 44.0 %collective-permute-start.13 = (f32[736,384]{1,0:T(8,128)S(1)}, f32[736,384]{1,0:T(8,128)}, u32[]{:S(2)}, u32[]{:S(2)}) collective-permute-start(f32[736,384]{1,0:T(8,128)S(1)} %shard_map.95.refs_3_.refs_1_), channel_id=1, source_target_pairs={{0,1},{4,5},{1,2},{5,6},{2,3},{6,7},{3,11},{7,15},{11,10},{15,14},... | collective-permute-start | bytes 3391496 | tf_op jit(solution)/shard_map/ppermute | solution.py:309
  80.5 39.8 %collective-permute-start.14 = (f32[736,384]{1,0:T(8,128)S(1)}, f32[736,384]{1,0:T(8,128)}, u32[]{:S(2)}, u32[]{:S(2)}) collective-permute-start(f32[736,384]{1,0:T(8,128)S(1)} %shard_map.95.refs_3_.refs_1_), channel_id=1, source_target_pairs={{1,0},{5,4},{2,1},{6,5},{3,2},{7,6},{11,3},{15,7},{10,11},{14,15},... | collective-permute-start | bytes 3391496 | tf_op jit(solution)/shard_map/ppermute | solution.py:309
  120.3 9.4 %collective-permute-start.18 = (f32[576,384]{1,0:T(8,128)}, f32[576,384]{1,0:T(8,128)S(1)}, u32[]{:S(2)}, u32[]{:S(2)}) collective-permute-start(f32[576,384]{1,0:T(8,128)} %dynamic-slice_bitcast_fusion), channel_id=1, source_target_pairs={{0,4},{4,0},{8,12},{12,8},{16,20},{20,16},{24,28},{28,24},{1,5},{5... | collective-permute-start | bytes 2654216 | tf_op jit(solution)/shard_map/ppermute | solution.py:403
  124.0 25.7 %collective-permute-start.16 = (f32[360,384]{1,0:T(8,128)}, f32[360,384]{1,0:T(8,128)S(1)}, u32[]{:S(2)}, u32[]{:S(2)}) collective-permute-start(f32[360,384]{1,0:T(8,128)} %add.124), channel_id=1, source_target_pairs={{0,0},{4,1},{1,2},{5,3},{2,4},{6,5},{3,6},{7,7},{11,8},{15,9},{10,... | collective-permute-start | bytes 1658888 | tf_op jit(solution)/shard_map/ppermute | solution.py:309
  126.6 23.2 %collective-permute-start.19 = (f32[360,384]{1,0:T(8,128)}, f32[360,384]{1,0:T(8,128)S(1)}, u32[]{:S(2)}, u32[]{:S(2)}) collective-permute-start(f32[360,384]{1,0:T(8,128)} %add.125), channel_id=1, source_target_pairs={{1,0},{5,1},{0,2},{4,3},{3,4},{7,5},{2,6},{6,7},{10,8},{14,9},{11,... | collective-permute-start | bytes 1658888 | tf_op jit(solution)/shard_map/ppermute | solution.py:309
  132.0 21.3 %collective-permute-start.23 = (f32[144,384]{1,0:T(8,128)}, f32[144,384]{1,0:T(8,128)}, u32[]{:S(2)}, u32[]{:S(2)}) collective-permute-start(f32[144,384]{1,0:T(8,128)} %get-tuple-element.112), channel_id=1, source_target_pairs={{0,24},{4,28},{8,16},{12,20},{16,8},{20,12},{24,0},{28,4},{1,25},{... | collective-permute-start | bytes 663560 | tf_op jit(solution)/shard_map/ppermute | solution.py:283
  132.5 20.9 %collective-permute-start.22 = (f32[144,384]{1,0:T(8,128)}, f32[144,384]{1,0:T(8,128)}, u32[]{:S(2)}, u32[]{:S(2)}) collective-permute-start(f32[144,384]{1,0:T(8,128)} %get-tuple-element.113), channel_id=1, source_target_pairs={{0,16},{4,20},{8,24},{12,28},{16,0},{20,4},{24,8},{28,12},{1,17},{... | collective-permute-start | bytes 663560 | tf_op jit(solution)/shard_map/ppermute | solution.py:283
  135.4 18.0 %collective-permute-start.21 = (f32[144,384]{1,0:T(8,128)}, f32[144,384]{1,0:T(8,128)}, u32[]{:S(2)}, u32[]{:S(2)}) collective-permute-start(f32[144,384]{1,0:T(8,128)} %get-tuple-element.111), channel_id=1, source_target_pairs={{0,8},{4,12},{8,0},{12,4},{16,24},{20,28},{24,16},{28,20},{1,9},{5... | collective-permute-start | bytes 663560 | tf_op jit(solution)/shard_map/ppermute | solution.py:283
  149.8 9.4 %collective-permute-start.20 = (f32[360,384]{1,0:T(8,128)}, f32[360,384]{1,0:T(8,128)S(1)}, u32[]{:S(2)}, u32[]{:S(2)}) collective-permute-start(f32[360,384]{1,0:T(8,128)} %get-tuple-element.81), channel_id=1, source_target_pairs={{0,4},{4,0},{1,5},{5,1},{2,6},{6,2},{3,7},{7,3},{11,15},{15,11},{1... | collective-permute-start | bytes 1658888 | tf_op jit(solution)/shard_map/ppermute | solution.py:309
  163.5 6.9 %collective-permute-start.30 = (f32[108,128]{1,0:T(8,128)S(1)}, f32[108,128]{1,0:T(8,128)S(1)}, u32[]{:S(2)}, u32[]{:S(2)}) collective-permute-start(f32[108,128]{1,0:T(8,128)S(1)} %get-tuple-element.100), channel_id=1, source_target_pairs={{0,2},{1,3},{2,0},{3,1},{4,6},{5,7},{6,4},{7,5},{8,10},{9,11},{10,... | collective-permute-start | bytes 165896 | tf_op jit(solution)/shard_map/ppermute | solution.py:299
  172.4 9.7 %collective-permute-start.32 = (f32[144,384]{1,0:T(8,128)}, f32[144,384]{1,0:T(8,128)}, u32[]{:S(2)}, u32[]{:S(2)}) collective-permute-start(f32[144,384]{1,0:T(8,128)} %reshape_reshape.7), channel_id=1, source_target_pairs={{0,8},{4,12},{8,0},{12,4},{16,24},{20,28},{24,16},{28,20},{1,9},{5... | collective-permute-start | bytes 663560 | tf_op jit(solution)/shard_map/ppermute | solution.py:299
  178.3 16.3 %collective-permute-start.28 = (f32[360,384]{1,0:T(8,128)S(1)}, f32[360,384]{1,0:T(8,128)S(1)}, u32[]{:S(2)}, u32[]{:S(2)}) collective-permute-start(f32[360,384]{1,0:T(8,128)S(1)} %add.129), channel_id=1, source_target_pairs={{0,0},{4,1},{1,2},{5,3},{2,4},{6,5},{3,6},{7,7},{11,8},{15,9},{10,... | collective-permute-start | bytes 1658888 | tf_op jit(solution)/shard_map/ppermute | solution.py:309
  179.0 15.6 %collective-permute-start.35 = (f32[360,384]{1,0:T(8,128)S(1)}, f32[360,384]{1,0:T(8,128)S(1)}, u32[]{:S(2)}, u32[]{:S(2)}) collective-permute-start(f32[360,384]{1,0:T(8,128)S(1)} %add.138), channel_id=1, source_target_pairs={{1,0},{5,1},{0,2},{4,3},{3,4},{7,5},{2,6},{6,7},{10,8},{14,9},{11,... | collective-permute-start | bytes 1658888 | tf_op jit(solution)/shard_map/ppermute | solution.py:309
  181.3 13.2 %collective-permute-start.33 = (f32[144,384]{1,0:T(8,128)}, f32[144,384]{1,0:T(8,128)S(1)}, u32[]{:S(2)}, u32[]{:S(2)}) collective-permute-start(f32[144,384]{1,0:T(8,128)} %reshape_reshape.7), channel_id=1, source_target_pairs={{0,16},{4,20},{8,24},{12,28},{16,0},{20,4},{24,8},{28,12},{1,17},{... | collective-permute-start | bytes 663560 | tf_op jit(solution)/shard_map/ppermute | solution.py:299
  181.4 13.2 %collective-permute-start.34 = (f32[144,384]{1,0:T(8,128)}, f32[144,384]{1,0:T(8,128)S(1)}, u32[]{:S(2)}, u32[]{:S(2)}) collective-permute-start(f32[144,384]{1,0:T(8,128)} %reshape_reshape.7), channel_id=1, source_target_pairs={{0,24},{4,28},{8,16},{12,20},{16,8},{20,12},{24,0},{28,4},{1,25},{... | collective-permute-start | bytes 663560 | tf_op jit(solution)/shard_map/ppermute | solution.py:299
  194.6 10.9 %collective-permute-start.36 = (f32[576,384]{1,0:T(8,128)S(1)}, f32[576,384]{1,0:T(8,128)S(1)}, u32[]{:S(2)}, u32[]{:S(2)}) collective-permute-start(f32[576,384]{1,0:T(8,128)S(1)} %bitcast.90), channel_id=1, source_target_pairs={{0,4},{4,0},{8,12},{12,8},{16,20},{20,16},{24,28},{28,24},{1,5},{5... | collective-permute-start | bytes 2654216 | tf_op jit(solution)/shard_map/ppermute | solution.py:403
  (25 other events, 180.3 us)

commit v3 on v2

--- a/solution.py
+++ b/solution.py
@@ -89,13 +89,18 @@
 
 def split_outside(x):
     high = lax.reduce_precision(x, 8, 7)
-    return high.astype(BF16), (x - high).astype(BF16)
+    return jnp.concatenate([high.astype(BF16), (x - high).astype(BF16)], axis=1)
 
 
 def dot3(a, b, dims=(((1,), (0,)), ((), ()))):
-    out = lax.dot_general(a[0], b[0], dims, preferred_element_type=jnp.float32)
-    out += lax.dot_general(a[0], b[1], dims, preferred_element_type=jnp.float32)
-    return out + lax.dot_general(a[1], b[0], dims, preferred_element_type=jnp.float32)
+    columns = b.shape[1] // 2
+    both = lax.dot_general(a[0], b, dims, preferred_element_type=jnp.float32)
+    rest = lax.dot_general(a[1], b[:, :columns], dims, preferred_element_type=jnp.float32)
+    return both[:, :columns] + both[:, columns:] + rest
+
+
+def side_by_side(x):
+    return jnp.concatenate(split(x), axis=1)
 
 
 WHOLE = pl.BlockSpec(memory_space=pltpu.VMEM)
@@ -150,22 +155,21 @@
             if count == 1:
                 if g == 0:
                     arrived(loads)
-                x[0, g], x[1, g] = split(held[0, g])
+                x[g] = side_by_side(held[0, g])
                 continue
             arrived(loads[2 * g : 2 * g + 2])
             a, b = held[2 * g], held[2 * g + 1]
             swap = place[1] == 1
             size = 2 * a.shape[0]
             pair = jnp.concatenate([jnp.where(swap, b, a), jnp.where(swap, a, b)], axis=0)
-            x[0, g, :size, :], x[1, g, :size, :] = split(pair)
-            for term in range(2):
-                x[term, g, size:, :] = jnp.zeros((wide2 - size, channels), BF16)
+            x[g, :size, :] = side_by_side(pair)
+            x[g, size:, :] = jnp.zeros((wide2 - size, 2 * channels), BF16)
         for half in range(2):
             total = 0.0
             for g in range(share):
                 i = half * share + g
                 arrived(pairs[i])
-                total += dot3((v[0, i], v[1, i]), (x[0, g], x[1, g]))
+                total += dot3((v[0, i], v[1, i]), x[g])
             out[half * wide : (half + 1) * wide, :] = total
 
     return kernel_call(
@@ -175,7 +179,7 @@
         WHOLE,
         jax.ShapeDtypeStruct((wide2, channels), jnp.float32),
         [
-            pltpu.VMEM((2, share, wide2, channels), BF16),
+            pltpu.VMEM((share, wide2, 2 * channels), BF16),
             pltpu.VMEM((2, 2 * share, wide, wide2), BF16),
             pltpu.SemaphoreType.DMA((2, 2 * share)),
             pltpu.VMEM((count, *blocks[0].shape), jnp.float32),
@@ -186,28 +190,27 @@
 
 def mix(place, rows, coef, weights, table, part_len, gradient=None):
     share, wide, wide2 = table.shape[1], *table.shape[-2:]
-    channels = weights[0].shape[1]
-    deep = weights[0].shape[0]
+    deep, channels = weights.shape[0], weights.shape[1] // 2
     basis = deep // channels
     chunk = 16
     count = 2 * share
     rows = [*rows] + ([] if gradient is None else [gradient])
     n_rows = len(rows)
-    n_in = n_rows + 4
+    n_in = n_rows + 3
 
     def body(place, *refs):
-        coef, wh, wl, table = refs[n_rows:n_in]
+        coef, weights, table = refs[n_rows:n_in]
         ys, rest = refs[n_in : n_in + count], refs[n_in + count :]
         if gradient is not None:
-            out, gh, gl, *rest = rest
-        fh, fl, oh, ol, v, sems, held, held_sems, w, w_sems = rest
+            out, both, *rest = rest
+        fh, fl, mixed, v, sems, held, held_sems, w, w_sems = rest
         loads = fetched(refs[:n_rows], held, held_sems)
-        w_loads = fetched((wh, wl), w, w_sems)
+        arrived(loads)
+        w_loads = fetched((weights,), w, w_sems)
         blocks = [(place[0], 1, 2 * (i // 2) + (place[1] ^ (i % 2))) for i in range(count)]
         pairs = copies(table, blocks, v, sems)
-        arrived(loads)
-
-        @pl.loop(0, wide // chunk)
+
+        @pl.loop(0, wide // chunk, unroll=True)
         def _(i):
             re_at = pl.ds(pl.multiple_of(i * chunk, chunk), chunk)
             im_at = pl.ds(pl.multiple_of(wide + i * chunk, chunk), chunk)
@@ -225,34 +228,34 @@
                 fh[im_at, cols], fl[im_at, cols] = split(im)
 
         arrived(w_loads)
-        oh[...], ol[...] = split(dot3((fh[...], fl[...]), (w[0], w[1])))
+        mixed[...] = side_by_side(dot3((fh[...], fl[...]), w[0]))
         for i, y in enumerate(ys):
             arrived(pairs[i])
-            y[...] = dot3((v[0, i], v[1, i]), (oh[...], ol[...]))[:part_len]
+            y[...] = dot3((v[0, i], v[1, i]), mixed[...])[:part_len]
         if gradient is not None:
-            gh[...], gl[...] = split(held[3])
+            both[...] = side_by_side(held[3])
             for k in range(basis):
                 at = pl.ds(k * channels, channels)
-                out[at, :] = dot3((fh[:, at], fl[:, at]), (gh[...], gl[...]), (((0,), (0,)), ((), ())))
+                out[at, :] = dot3((fh[:, at], fl[:, at]), both[...], (((0,), (0,)), ((), ())))
 
     y_shape = jax.ShapeDtypeStruct((part_len, channels), jnp.float32)
     extra, scratch = [], []
     if gradient is not None:
         extra = [jax.ShapeDtypeStruct((deep, channels), jnp.float32)]
-        scratch = [pltpu.VMEM((wide2, channels), BF16)] * 2
+        scratch = [pltpu.VMEM((wide2, 2 * channels), BF16)]
     return kernel_call(
         body,
         (),
-        [REMAIN] * n_rows + [WHOLE] + [REMAIN] * 3,
+        [REMAIN] * n_rows + [WHOLE] + [REMAIN] * 2,
         [WHOLE] * (count + len(extra)),
         [y_shape] * count + extra,
         scratch
         + [pltpu.VMEM((wide2, deep), BF16)] * 2
-        + [pltpu.VMEM((wide2, channels), BF16)] * 2
+        + [pltpu.VMEM((wide2, 2 * channels), BF16)]
         + [pltpu.VMEM((2, count, wide, wide2), BF16), pltpu.SemaphoreType.DMA((2, count))]
         + [pltpu.VMEM((n_rows, wide2, channels), jnp.float32), pltpu.SemaphoreType.DMA((n_rows,))]
-        + [pltpu.VMEM((2, deep, channels), BF16), pltpu.SemaphoreType.DMA((2,))],
-    )(place, *rows, coef, *weights, table)
+        + [pltpu.VMEM((1, deep, 2 * channels), BF16), pltpu.SemaphoreType.DMA((1,))],
+    )(place, *rows, coef, weights, table)
 
 
 def arrange(flags, got):
@@ -291,14 +294,17 @@
     return total
 
 
-def shares_joined(x, axis, me, ways, stride):
+def share_shown(x, axis, ways, stride):
     size = lax.axis_size(axis)
-    whole = jnp.zeros((ways,) + x.shape, x.dtype)
-    whole = lax.dynamic_update_index_in_dim(whole, x, me, 0)
-    for g in range(1, ways):
-        piece = lax.ppermute(x, axis, [(a, a ^ (g * stride)) for a in range(size)])
+    return [x] + [lax.ppermute(x, axis, [(a, a ^ (g * stride)) for a in range(size)]) for g in range(1, ways)]
+
+
+def shares_joined(pieces, me):
+    ways = len(pieces)
+    whole = jnp.zeros((ways,) + pieces[0].shape, pieces[0].dtype)
+    for g, piece in enumerate(pieces):
         whole = lax.dynamic_update_index_in_dim(whole, piece, me ^ g, 0)
-    return whole.reshape((-1,) + x.shape[1:])
+    return whole.reshape((-1,) + pieces[0].shape[1:])
 
 
 def make_local(lat, lon):
@@ -402,17 +408,17 @@
         def swap_core(x):
             return lax.ppermute(x, "lat", swap)
 
-        s_got = [after(x, *ahead_weights, *back_weights) for x in s_got]
+        s_got = [after(x, ahead_weights, back_weights) for x in s_got]
         g_got = fetch(cotangent, s_got)
         s_spec = enter(s_got)
         g_got = [after(x, s_spec, coef) for x in g_got]
-        s_halo = halo(after(s_spec, *g_got))
+        s_halo = halo(s_spec)
         g_spec = enter(g_got)
         s_halo = [after(x, g_spec) for x in s_halo]
         g_halo = halo(g_spec)
         *y, term = mix(place, (s_halo[0], s_spec, s_halo[1]), coef[0], ahead_weights, table, part_len, g_spec)
         g_halo = [after(x, *y) for x in g_halo]
-        others = exchange([after(x, *g_halo) for x in y])
+        others = [[after(x, *g_halo) for x in other] for other in exchange(y)]
         halves = term.reshape(2, -1, channels)
         give = after(lax.dynamic_index_in_dim(halves, 1 - core, 0, keepdims=False), *g_halo)
         given = swap_core(give)
@@ -424,21 +430,21 @@
         g_halo = [after(x, *o_blocks, term) for x in g_halo]
         y = mix(place, (g_halo[0], g_spec, g_halo[1]), coef[1], back_weights, table, part_len)
         o_got = [after(x, *y) for x in o_got]
-        y = [after(x, *o_got) for x in y]
-        others = exchange(y)
-        term = shares_summed([after(x, *o_got) for x in pieces])
+        y = [after(x, o_got[0]) for x in y]
+        others = [[after(x, *o_got) for x in other] for other in exchange(y)]
+        term = shares_summed([after(x, *y) for x in pieces])
         term_shape = term.shape
         term = term.reshape((-1, 128) if even else (lon, -1))
         pieces = shares_sent(term, "lon", z, lon, 1)
         b_blocks = total(y, others)
         term = shares_summed([after(x, *b_blocks) for x in pieces])
         b_got = [deliver(after(x, term), t) for t, x in enumerate(b_blocks)]
-        term = shares_joined(term, "lon", z, lon, 1).reshape(term_shape)
+        term = shares_joined(share_shown(term, "lon", lon, 1), z).reshape(term_shape)
         output = arrange(flags, o_got)
         b_got = [after(x, output) for x in b_got]
-        term = shares_joined(term, "lat", pair, lay.pairs, 2)
-        b_got = [after(x, term) for x in b_got]
-        other = swap_core(after(term, *b_got))
+        term = shares_joined([after(x, b_got[0]) for x in share_shown(term, "lat", lay.pairs, 2)], pair)
+        b_got[1] = after(b_got[1], term)
+        other = swap_core(after(term, b_got[1]))
         grad_signal = arrange(flags, b_got)
         term = jnp.concatenate([jnp.where(core == 0, term, other), jnp.where(core == 0, other, term)], axis=0)
         weight_grad = term.reshape(mixing.shape)

time: 210 us -> 200 us (0.952); the launches traced: 207 us -> 199 us
  waiting for transfers between devices: 61.2 us -> 52.6 us
  other arithmetic: 11.4 us -> 18 us
  local copies, waits for them, and re-layouts: 21.2 us -> 16.2 us
    ppermute x6, waiting for transfers between devices: 15.4 us -> 0.72 us  [share_shown(): lax.ppermute(x, axis, [(a, a ^ g * stride) for a in range(size)])]
    ppermute x20, waiting for transfers between devices: 40 us -> 48.9 us  [send(): return lax.ppermute(x, AXES, pairs)]
    ppermute x20, starting transfers between devices: 34.4 us -> 27.4 us  [send(): return lax.ppermute(x, AXES, pairs)]
    unnamed x24 -> x26, local copies, waits for them, and re-layouts: 6.08 us -> 1.9 us
    concatenate x0 -> x1, other arithmetic: none -> 3.64 us  [split_outside(): return jnp.concatenate([high.astype(BF16), (x - high).astype(BF16)], axis=1)]
    add x4, other arithmetic: 2.9 us -> 5.03 us  [total(): return [own[t] + sum((other[t] for other in others)) for t in range(2)]]
    ppermute x6, starting transfers between devices: 8.26 us -> 10.4 us  [shares_sent(): lax.ppermute(piece, axis, [(a, a ^ g * stride) for a in range(size)])]
    convert_element_type x1 -> x2, other arithmetic: 3.95 us -> 4.41 us  [split_outside(): return jnp.concatenate([high.astype(BF16), (x - high).astype(BF16)], axis=1)]
  transfers between devices with their start and end apart: 37 -> 37, of which waited for: 15 -> 13; matrix products, arithmetic and copies ran while one was open for 10% -> 14% of each run, Pallas kernels for 23% -> 24%
where the time goes in v3:
time: 200 us; the launch traced here: 199 us
  starting transfers between devices  62 us (31%)
  waiting for transfers between devices  52.6 us (26%)
  Pallas kernels  48 us (24%)
  other arithmetic  18 us (9%)
  local copies, waits for them, and re-layouts  16.2 us (8%)
  between operations  2.64 us (1%)
    ppermute x20, waiting for transfers between devices, send(): return lax.ppermute(x, AXES, pairs)  48.9 us
    pallas_call x2, Pallas kernels, mix(): kernel_call(body, (), [REMAIN] * n_rows + [WHOLE] + [REMAIN] * 2, [WHOLE]...  32.2 us
    ppermute x20, starting transfers between devices, send(): return lax.ppermute(x, AXES, pairs)  27.4 us
    pallas_call x2, Pallas kernels, transform(): kernel_call(body, (), [REMAIN] * (count + 1), WHOLE, jax.ShapeDtypeStruct...  12.4 us
    ppermute x2, starting transfers between devices, swap_core(): return lax.ppermute(x, 'lat', swap)  10.5 us
    ppermute x6, starting transfers between devices, shares_sent(): lax.ppermute(piece, axis, [(a, a ^ g * stride) for a in range(size)])  10.4 us
    ppermute x6, starting transfers between devices, share_shown(): lax.ppermute(x, axis, [(a, a ^ g * stride) for a in range(size)])  8 us
    add x4, other arithmetic, total(): return [own[t] + sum((other[t] for other in others)) for t in range(2)]  5.03 us
  transfers between devices with their start and end apart: 37, of which 13 were waited for; matrix products, arithmetic and copies ran while one was open for 14% of the time, Pallas kernels for 24%

profile of v3, /device:TPU:0, one launch (start us, length us, event | category | flops | bytes accessed | tf_op | source)
XLA Modules:
  0.0 199.4 jit_solution(11349429278961717310)
XLA Ops:
  6.7 3.3 %collective-permute-start.1 = (f32[360,384]{1,0:T(8,128)S(1)}, f32[360,384]{1,0:T(8,128)S(1)}, u32[]{:S(2)}, u32[]{:S(2)}) collective-permute-start(f32[360,384]{1,0:T(8,128)S(1)} %get-tuple-element.117), channel_id=1, source_target_pairs={{0,1},{1,5},{2,0},{3,4},{4,3},{5,7},{6,2},{7,6},{8,10},{9,14},{10,... | collective-permute-start | bytes 1658888 | tf_op jit(solution)/shard_map/ppermute | solution.py:315
  13.3 2.9 %reduce-precision_convert_fusion = (bf16[1152,384]{1,0:T(8,128)(2,1)}, bf16[1152,384]{1,0:T(8,128)(2,1)}) fusion(f32[3,384,384]{2,1,0:T(8,128)} %copy.11), kind=kLoop, calls=%fused_computation.1 | loop fusion | flops 1769472 | bytes 3538944 | tf_op jit(solution)/shard_map/convert_element_type | solution.py:92
  17.1 2.3 %dynamic-slice_bitcast_fusion.1 = (f32[360,384]{1,0:T(8,128)}, f32[360,384]{1,0:T(8,128)}) fusion(f32[2,360,384]{2,1,0:T(8,128)} %param.11, s32[]{:T(128)S(6)} %select_n.249, s32[]{:T(128)S(6)} %select_n.248), kind=kLoop, calls=%fused_computation.11 | loop fusion | bytes 2211848 | tf_op jit(solution)/shard_map/jit(dynamic_index_in_dim)/squeeze | solution.py:345
  19.5 3.6 %pad_maximum_fusion = (bf16[1152,768]{1,0:T(8,128)(2,1)}, bf16[1152,768]{1,0:T(8,128)(2,1)}) fusion(bf16[1152,384]{1,0:T(8,128)(2,1)S(1)} %copy-done.10, bf16[1152,384]{1,0:T(8,128)(2,1)S(1)} %copy-done.9, bf16[1152,384]{1,0:T(8,128)(2,1)} %get-tuple-element.112, bf16[1152,384]{1,0:T(8,128)(2,1)} %get-tuple-element.111), kind=kLoop, calls=%fused_computation.6 | loop fusion | flops 7077888 | bytes 7077888 | tf_op jit(solution)/shard_map/concatenate | solution.py:92
  23.1 13.7 %collective-permute-done.1.refs_1_ = f32[360,384]{1,0:T(8,128)S(1)} collective-permute-done((f32[360,384]{1,0:T(8,128)S(1)}, f32[360,384]{1,0:T(8,128)S(1)}, u32[]{:S(2)}, u32[]{:S(2)}) %collective-permute-start.1) | collective-permute-done | bytes 552992 | tf_op jit(solution)/shard_map/ppermute | solution.py:315
  50.7 6.1 %shard_map.94.refs_1_ = f32[736,384]{1,0:T(8,128)S(1)} custom-call(s32[2]{0:T(128)S(1)} %pad_add_fusion.1.place, f32[360,384]{1,0:T(8,128)S(1)} %collective-permute-done.refs_0_, f32[360,384]{1,0:T(8,128)S(1)} %collective-permute-done.1.refs_1_, f32[360,384]{1,0:T(8,128)S(1)} %collective-permute-done.2.refs_2_, f32[360,384]{1,0:T(8,128)S(1)} %copy-done.4, ...), custom_call_target="tpu_custom_call" | custom-call | flops 1 | bytes 1 | tf_op jit(solution)/shard_map/pallas_call | solution.py:175
  56.8 7.6 %collective-permute-done.9.refs_1_ = f32[360,384]{1,0:T(8,128)} collective-permute-done((f32[360,384]{1,0:T(8,128)}, f32[360,384]{1,0:T(8,128)}, u32[]{:S(2)}, u32[]{:S(2)}) %collective-permute-start.9) | collective-permute-done | bytes 552992 | tf_op jit(solution)/shard_map/ppermute | solution.py:315
  68.5 6.3 %shard_map.95.refs_3_.refs_1_ = f32[736,384]{1,0:T(8,128)S(1)} custom-call(s32[2]{0:T(128)S(1)} %pad_add_fusion.1.place, f32[360,384]{1,0:T(8,128)S(1)} %collective-permute-done.5.refs_0_, f32[360,384]{1,0:T(8,128)} %collective-permute-done.9.refs_1_, f32[360,384]{1,0:T(8,128)S(1)} %collective-permute-done.10.refs_2_, ...), custom_call_target="tpu_custom_call" | custom-call | flops 1 | bytes 1 | tf_op jit(solution)/shard_map/pallas_call | solution.py:175
  74.8 4.6 %collective-permute-start.14 = (f32[736,384]{1,0:T(8,128)S(1)}, f32[736,384]{1,0:T(8,128)S(1)}, u32[]{:S(2)}, u32[]{:S(2)}) collective-permute-start(f32[736,384]{1,0:T(8,128)S(1)} %shard_map.95.refs_3_.refs_1_), channel_id=1, source_target_pairs={{0,1},{4,5},{1,2},{5,6},{2,3},{6,7},{3,11},{7,15},{11,10},{15,14},... | collective-permute-start | bytes 3391496 | tf_op jit(solution)/shard_map/ppermute | solution.py:315
  82.6 8.8 %collective-permute-done.4.refs_0_ = f32[736,384]{1,0:T(8,128)} collective-permute-done((f32[736,384]{1,0:T(8,128)S(1)}, f32[736,384]{1,0:T(8,128)}, u32[]{:S(2)}, u32[]{:S(2)}) %collective-permute-start.4) | collective-permute-done | bytes 1130528 | tf_op jit(solution)/shard_map/ppermute | solution.py:315
  91.4 5.5 %collective-permute-done.12.refs_2_ = f32[736,384]{1,0:T(8,128)} collective-permute-done((f32[736,384]{1,0:T(8,128)S(1)}, f32[736,384]{1,0:T(8,128)}, u32[]{:S(2)}, u32[]{:S(2)}) %collective-permute-start.12) | collective-permute-done | bytes 1130528 | tf_op jit(solution)/shard_map/ppermute | solution.py:315
  96.9 17.7 %shard_map.96 = (f32[360,384]{1,0:T(8,128)S(1)}, f32[360,384]{1,0:T(8,128)S(1)}, f32[360,384]{1,0:T(8,128)}, f32[360,384]{1,0:T(8,128)}, f32[1152,384]{1,0:T(8,128)}) custom-call(s32[2]{0:T(128)S(1)} %pad_add_fusion.1.place, f32[736,384]{1,0:T(8,128)} %collective-permute-done.4.refs_0_, f32[736,384]{1,0:T(8,128)S(1)} %shard_map.94.refs_1_, ...), custom_call_target="tpu_custom_call" | custom-call | flops 1 | bytes 1 | tf_op jit(solution)/shard_map/pallas_call | solution.py:246
  114.6 2.5 %dynamic-slice_bitcast_fusion = f32[576,384]{1,0:T(8,128)} fusion(f32[2,576,384]{2,1,0:T(8,128)} %bitcast.94, s32[]{:T(128)S(6)} %select_n.274), kind=kLoop, calls=%fused_computation.10 | loop fusion | bytes 1769476 | tf_op jit(solution)/shard_map/jit(dynamic_index_in_dim)/squeeze | solution.py:423
  117.2 3.0 %collective-permute-done.15.refs_2_ = f32[736,384]{1,0:T(8,128)} collective-permute-done((f32[736,384]{1,0:T(8,128)S(1)}, f32[736,384]{1,0:T(8,128)}, u32[]{:S(2)}, u32[]{:S(2)}) %collective-permute-start.15) | collective-permute-done | bytes 1130528 | tf_op jit(solution)/shard_map/ppermute | solution.py:315
  120.8 2.8 %collective-permute-done.13 = f32[360,384]{1,0:T(8,128)S(1)} collective-permute-done((f32[360,384]{1,0:T(8,128)}, f32[360,384]{1,0:T(8,128)S(1)}, u32[]{:S(2)}, u32[]{:S(2)}) %collective-permute-start.13) | collective-permute-done | bytes 552992 | tf_op jit(solution)/shard_map/ppermute | solution.py:315
  128.9 2.5 %collective-permute-start.23 = (f32[144,384]{1,0:T(8,128)S(1)}, f32[144,384]{1,0:T(8,128)}, u32[]{:S(2)}, u32[]{:S(2)}) collective-permute-start(f32[144,384]{1,0:T(8,128)S(1)} %get-tuple-element.120), channel_id=1, source_target_pairs={{0,24},{4,28},{8,16},{12,20},{16,8},{20,12},{24,0},{28,4},{1,25},{... | collective-permute-start | bytes 663560 | tf_op jit(solution)/shard_map/ppermute | solution.py:286
  131.4 3.5 %collective-permute-start.22 = (f32[144,384]{1,0:T(8,128)}, f32[144,384]{1,0:T(8,128)}, u32[]{:S(2)}, u32[]{:S(2)}) collective-permute-start(f32[144,384]{1,0:T(8,128)} %get-tuple-element.121), channel_id=1, source_target_pairs={{0,16},{4,20},{8,24},{12,28},{16,0},{20,4},{24,8},{28,12},{1,17},{... | collective-permute-start | bytes 663560 | tf_op jit(solution)/shard_map/ppermute | solution.py:286
  136.3 14.6 %shard_map.97 = (f32[360,384]{1,0:T(8,128)S(1)}, f32[360,384]{1,0:T(8,128)S(1)}, f32[360,384]{1,0:T(8,128)}, f32[360,384]{1,0:T(8,128)}) custom-call(s32[2]{0:T(128)S(1)} %pad_add_fusion.1.place, f32[736,384]{1,0:T(8,128)S(1)} %collective-permute-done.14.refs_0_, f32[736,384]{1,0:T(8,128)S(1)} %copy-done.1, f32[736,384]{1,0:T(8,128)} %collective-permute-done.15.refs_2_, ...), custom_call_target="tpu_custom_call" | custom-call | flops 1 | bytes 1 | tf_op jit(solution)/shard_map/pallas_call | solution.py:246
  150.9 2.6 %collective-permute-start.20 = (f32[360,384]{1,0:T(8,128)}, f32[360,384]{1,0:T(8,128)}, u32[]{:S(2)}, u32[]{:S(2)}) collective-permute-start(f32[360,384]{1,0:T(8,128)} %get-tuple-element.84), channel_id=1, source_target_pairs={{0,4},{4,0},{1,5},{5,1},{2,6},{6,2},{3,7},{7,3},{11,15},{15,11},{1... | collective-permute-start | bytes 1658888 | tf_op jit(solution)/shard_map/ppermute | solution.py:315
  156.8 2.6 %collective-permute-start.25 = (f32[108,128]{1,0:T(8,128)S(1)}, f32[108,128]{1,0:T(8,128)S(1)}, u32[]{:S(2)}, u32[]{:S(2)}) collective-permute-start(f32[108,128]{1,0:T(8,128)S(1)} %get-tuple-element.125), channel_id=1, source_target_pairs={{0,1},{1,0},{2,3},{3,2},{4,5},{5,4},{6,7},{7,6},{8,9},{9,8},{10,11... | collective-permute-start | bytes 165896 | tf_op jit(solution)/shard_map/ppermute | solution.py:286
  163.6 2.5 %collective-permute-start.31 = (f32[108,128]{1,0:T(8,128)S(1)}, f32[108,128]{1,0:T(8,128)S(1)}, u32[]{:S(2)}, u32[]{:S(2)}) collective-permute-start(f32[108,128]{1,0:T(8,128)S(1)} %get-tuple-element.108), channel_id=1, source_target_pairs={{0,2},{1,3},{2,0},{3,1},{4,6},{5,7},{6,4},{7,5},{8,10},{9,11},{10,... | collective-permute-start | bytes 165896 | tf_op jit(solution)/shard_map/ppermute | solution.py:299
  168.7 3.0 %collective-permute-start.29 = (f32[360,384]{1,0:T(8,128)}, f32[360,384]{1,0:T(8,128)S(1)}, u32[]{:S(2)}, u32[]{:S(2)}) collective-permute-start(f32[360,384]{1,0:T(8,128)} %add.138), channel_id=1, source_target_pairs={{1,0},{5,1},{0,2},{4,3},{3,4},{7,5},{2,6},{6,7},{10,8},{14,9},{11,... | collective-permute-start | bytes 1658888 | tf_op jit(solution)/shard_map/ppermute | solution.py:315
  177.6 7.4 %collective-permute-done.29.b = f32[360,384]{1,0:T(8,128)S(1)} collective-permute-done((f32[360,384]{1,0:T(8,128)}, f32[360,384]{1,0:T(8,128)S(1)}, u32[]{:S(2)}, u32[]{:S(2)}) %collective-permute-start.29) | collective-permute-done | bytes 552992 | tf_op jit(solution)/shard_map/ppermute | solution.py:315
  185.4 10.5 %collective-permute-start.36 = (f32[576,384]{1,0:T(8,128)S(1)}, f32[576,384]{1,0:T(8,128)S(1)}, u32[]{:S(2)}, u32[]{:S(2)}) collective-permute-start(f32[576,384]{1,0:T(8,128)S(1)} %bitcast.92), channel_id=1, source_target_pairs={{0,4},{4,0},{8,12},{12,8},{16,20},{20,16},{24,28},{28,24},{1,5},{5... | collective-permute-start | bytes 2654216 | tf_op jit(solution)/shard_map/ppermute | solution.py:409
  (125 shorter events, 56.8 us)
Async XLA Ops:
  5.0 18.1 %collective-permute-start = (f32[360,384]{1,0:T(8,128)}, f32[360,384]{1,0:T(8,128)S(1)}, u32[]{:S(2)}, u32[]{:S(2)}) collective-permute-start(f32[360,384]{1,0:T(8,128)} %get-tuple-element.118), channel_id=1, source_target_pairs={{0,0},{1,4},{2,1},{3,5},{4,2},{5,6},{6,3},{7,7},{8,11},{9,15},{10,... | collective-permute-start | bytes 1658888 | tf_op jit(solution)/shard_map/ppermute | solution.py:315
  6.7 30.1 %collective-permute-start.1 = (f32[360,384]{1,0:T(8,128)S(1)}, f32[360,384]{1,0:T(8,128)S(1)}, u32[]{:S(2)}, u32[]{:S(2)}) collective-permute-start(f32[360,384]{1,0:T(8,128)S(1)} %get-tuple-element.117), channel_id=1, source_target_pairs={{0,1},{1,5},{2,0},{3,4},{4,3},{5,7},{6,2},{7,6},{8,10},{9,14},{10,... | collective-permute-start | bytes 1658888 | tf_op jit(solution)/shard_map/ppermute | solution.py:315
  36.8 12.0 %collective-permute-start.2 = (f32[360,384]{1,0:T(8,128)S(1)}, f32[360,384]{1,0:T(8,128)S(1)}, u32[]{:S(2)}, u32[]{:S(2)}) collective-permute-start(f32[360,384]{1,0:T(8,128)S(1)} %collective-permute-done.refs_0_), channel_id=1, source_target_pairs={{0,4},{4,0},{1,5},{5,1},{2,6},{6,2},{3,7},{7,3},{11,15},{15,11},{1... | collective-permute-start | bytes 1658888 | tf_op jit(solution)/shard_map/ppermute | solution.py:315
  36.8 12.0 %collective-permute-start.3 = (f32[360,384]{1,0:T(8,128)S(1)}, f32[360,384]{1,0:T(8,128)S(1)}, u32[]{:S(2)}, u32[]{:S(2)}) collective-permute-start(f32[360,384]{1,0:T(8,128)S(1)} %collective-permute-done.1.refs_1_), channel_id=1, source_target_pairs={{0,4},{4,0},{1,5},{5,1},{2,6},{6,2},{3,7},{7,3},{11,15},{15,11},{1... | collective-permute-start | bytes 1658888 | tf_op jit(solution)/shard_map/ppermute | solution.py:315
  37.4 19.5 %collective-permute-start.5 = (f32[360,384]{1,0:T(8,128)}, f32[360,384]{1,0:T(8,128)S(1)}, u32[]{:S(2)}, u32[]{:S(2)}) collective-permute-start(f32[360,384]{1,0:T(8,128)} %get-tuple-element.57), channel_id=1, source_target_pairs={{0,0},{1,4},{2,1},{3,5},{4,2},{5,6},{6,3},{7,7},{8,11},{9,15},{10,... | collective-permute-start | bytes 1658888 | tf_op jit(solution)/shard_map/ppermute | solution.py:315
  42.6 21.8 %collective-permute-start.9 = (f32[360,384]{1,0:T(8,128)}, f32[360,384]{1,0:T(8,128)}, u32[]{:S(2)}, u32[]{:S(2)}) collective-permute-start(f32[360,384]{1,0:T(8,128)} %get-tuple-element.60), channel_id=1, source_target_pairs={{0,1},{1,5},{2,0},{3,4},{4,3},{5,7},{6,2},{7,6},{8,10},{9,14},{10,... | collective-permute-start | bytes 1658888 | tf_op jit(solution)/shard_map/ppermute | solution.py:315
  64.9 26.5 %collective-permute-start.4 = (f32[736,384]{1,0:T(8,128)S(1)}, f32[736,384]{1,0:T(8,128)}, u32[]{:S(2)}, u32[]{:S(2)}) collective-permute-start(f32[736,384]{1,0:T(8,128)S(1)} %shard_map.94.refs_1_), channel_id=1, source_target_pairs={{0,1},{4,5},{1,2},{5,6},{2,3},{6,7},{3,11},{7,15},{11,10},{15,14},... | collective-permute-start | bytes 3391496 | tf_op jit(solution)/shard_map/ppermute | solution.py:315
  67.2 29.8 %collective-permute-start.12 = (f32[736,384]{1,0:T(8,128)S(1)}, f32[736,384]{1,0:T(8,128)}, u32[]{:S(2)}, u32[]{:S(2)}) collective-permute-start(f32[736,384]{1,0:T(8,128)S(1)} %shard_map.94.refs_1_), channel_id=1, source_target_pairs={{1,0},{5,4},{2,1},{6,5},{3,2},{7,6},{11,3},{15,7},{10,11},{14,15},... | collective-permute-start | bytes 3391496 | tf_op jit(solution)/shard_map/ppermute | solution.py:315
  74.8 42.4 %collective-permute-start.14 = (f32[736,384]{1,0:T(8,128)S(1)}, f32[736,384]{1,0:T(8,128)S(1)}, u32[]{:S(2)}, u32[]{:S(2)}) collective-permute-start(f32[736,384]{1,0:T(8,128)S(1)} %shard_map.95.refs_3_.refs_1_), channel_id=1, source_target_pairs={{0,1},{4,5},{1,2},{5,6},{2,3},{6,7},{3,11},{7,15},{11,10},{15,14},... | collective-permute-start | bytes 3391496 | tf_op jit(solution)/shard_map/ppermute | solution.py:315
  79.4 40.8 %collective-permute-start.15 = (f32[736,384]{1,0:T(8,128)S(1)}, f32[736,384]{1,0:T(8,128)}, u32[]{:S(2)}, u32[]{:S(2)}) collective-permute-start(f32[736,384]{1,0:T(8,128)S(1)} %shard_map.95.refs_3_.refs_1_), channel_id=1, source_target_pairs={{1,0},{5,4},{2,1},{6,5},{3,2},{7,6},{11,3},{15,7},{10,11},{14,15},... | collective-permute-start | bytes 3391496 | tf_op jit(solution)/shard_map/ppermute | solution.py:315
  124.8 26.1 %collective-permute-start.16 = (f32[360,384]{1,0:T(8,128)S(1)}, f32[360,384]{1,0:T(8,128)S(1)}, u32[]{:S(2)}, u32[]{:S(2)}) collective-permute-start(f32[360,384]{1,0:T(8,128)S(1)} %add.124), channel_id=1, source_target_pairs={{0,0},{4,1},{1,2},{5,3},{2,4},{6,5},{3,6},{7,7},{11,8},{15,9},{10,... | collective-permute-start | bytes 1658888 | tf_op jit(solution)/shard_map/ppermute | solution.py:315
  128.9 24.5 %collective-permute-start.23 = (f32[144,384]{1,0:T(8,128)S(1)}, f32[144,384]{1,0:T(8,128)}, u32[]{:S(2)}, u32[]{:S(2)}) collective-permute-start(f32[144,384]{1,0:T(8,128)S(1)} %get-tuple-element.120), channel_id=1, source_target_pairs={{0,24},{4,28},{8,16},{12,20},{16,8},{20,12},{24,0},{28,4},{1,25},{... | collective-permute-start | bytes 663560 | tf_op jit(solution)/shard_map/ppermute | solution.py:286
  131.4 22.2 %collective-permute-start.22 = (f32[144,384]{1,0:T(8,128)}, f32[144,384]{1,0:T(8,128)}, u32[]{:S(2)}, u32[]{:S(2)}) collective-permute-start(f32[144,384]{1,0:T(8,128)} %get-tuple-element.121), channel_id=1, source_target_pairs={{0,16},{4,20},{8,24},{12,28},{16,0},{20,4},{24,8},{28,12},{1,17},{... | collective-permute-start | bytes 663560 | tf_op jit(solution)/shard_map/ppermute | solution.py:286
  134.8 18.7 %collective-permute-start.21 = (f32[144,384]{1,0:T(8,128)}, f32[144,384]{1,0:T(8,128)}, u32[]{:S(2)}, u32[]{:S(2)}) collective-permute-start(f32[144,384]{1,0:T(8,128)} %get-tuple-element.119), channel_id=1, source_target_pairs={{0,8},{4,12},{8,0},{12,4},{16,24},{20,28},{24,16},{28,20},{1,9},{5... | collective-permute-start | bytes 663560 | tf_op jit(solution)/shard_map/ppermute | solution.py:286
  134.8 21.9 %collective-permute-start.19 = (f32[360,384]{1,0:T(8,128)}, f32[360,384]{1,0:T(8,128)S(1)}, u32[]{:S(2)}, u32[]{:S(2)}) collective-permute-start(f32[360,384]{1,0:T(8,128)} %add.125), channel_id=1, source_target_pairs={{1,0},{5,1},{0,2},{4,3},{3,4},{7,5},{2,6},{6,7},{10,8},{14,9},{11,... | collective-permute-start | bytes 1658888 | tf_op jit(solution)/shard_map/ppermute | solution.py:315
  150.9 8.5 %collective-permute-start.20 = (f32[360,384]{1,0:T(8,128)}, f32[360,384]{1,0:T(8,128)}, u32[]{:S(2)}, u32[]{:S(2)}) collective-permute-start(f32[360,384]{1,0:T(8,128)} %get-tuple-element.84), channel_id=1, source_target_pairs={{0,4},{4,0},{1,5},{5,1},{2,6},{6,2},{3,7},{7,3},{11,15},{15,11},{1... | collective-permute-start | bytes 1658888 | tf_op jit(solution)/shard_map/ppermute | solution.py:315
  163.5 8.1 %collective-permute-start.30 = (f32[108,128]{1,0:T(8,128)S(1)}, f32[108,128]{1,0:T(8,128)S(1)}, u32[]{:S(2)}, u32[]{:S(2)}) collective-permute-start(f32[108,128]{1,0:T(8,128)S(1)} %get-tuple-element.108), channel_id=1, source_target_pairs={{0,1},{1,0},{2,3},{3,2},{4,5},{5,4},{6,7},{7,6},{8,9},{9,8},{10,11... | collective-permute-start | bytes 165896 | tf_op jit(solution)/shard_map/ppermute | solution.py:299
  163.6 8.0 %collective-permute-start.31 = (f32[108,128]{1,0:T(8,128)S(1)}, f32[108,128]{1,0:T(8,128)S(1)}, u32[]{:S(2)}, u32[]{:S(2)}) collective-permute-start(f32[108,128]{1,0:T(8,128)S(1)} %get-tuple-element.108), channel_id=1, source_target_pairs={{0,2},{1,3},{2,0},{3,1},{4,6},{5,7},{6,4},{7,5},{8,10},{9,11},{10,... | collective-permute-start | bytes 165896 | tf_op jit(solution)/shard_map/ppermute | solution.py:299
  168.0 9.6 %collective-permute-start.28 = (f32[360,384]{1,0:T(8,128)S(1)}, f32[360,384]{1,0:T(8,128)S(1)}, u32[]{:S(2)}, u32[]{:S(2)}) collective-permute-start(f32[360,384]{1,0:T(8,128)S(1)} %add.129), channel_id=1, source_target_pairs={{0,0},{4,1},{1,2},{5,3},{2,4},{6,5},{3,6},{7,7},{11,8},{15,9},{10,... | collective-permute-start | bytes 1658888 | tf_op jit(solution)/shard_map/ppermute | solution.py:315
  168.7 16.3 %collective-permute-start.29 = (f32[360,384]{1,0:T(8,128)}, f32[360,384]{1,0:T(8,128)S(1)}, u32[]{:S(2)}, u32[]{:S(2)}) collective-permute-start(f32[360,384]{1,0:T(8,128)} %add.138), channel_id=1, source_target_pairs={{1,0},{5,1},{0,2},{4,3},{3,4},{7,5},{2,6},{6,7},{10,8},{14,9},{11,... | collective-permute-start | bytes 1658888 | tf_op jit(solution)/shard_map/ppermute | solution.py:315
  172.3 12.7 %collective-permute-start.33 = (f32[144,384]{1,0:T(8,128)S(1)}, f32[144,384]{1,0:T(8,128)S(1)}, u32[]{:S(2)}, u32[]{:S(2)}) collective-permute-start(f32[144,384]{1,0:T(8,128)S(1)} %reshape_reshape.7), channel_id=1, source_target_pairs={{0,8},{4,12},{8,0},{12,4},{16,24},{20,28},{24,16},{28,20},{1,9},{5... | collective-permute-start | bytes 663560 | tf_op jit(solution)/shard_map/ppermute | solution.py:299
  172.4 12.6 %collective-permute-start.34 = (f32[144,384]{1,0:T(8,128)S(1)}, f32[144,384]{1,0:T(8,128)S(1)}, u32[]{:S(2)}, u32[]{:S(2)}) collective-permute-start(f32[144,384]{1,0:T(8,128)S(1)} %reshape_reshape.7), channel_id=1, source_target_pairs={{0,16},{4,20},{8,24},{12,28},{16,0},{20,4},{24,8},{28,12},{1,17},{... | collective-permute-start | bytes 663560 | tf_op jit(solution)/shard_map/ppermute | solution.py:299
  173.9 11.3 %collective-permute-start.35 = (f32[144,384]{1,0:T(8,128)S(1)}, f32[144,384]{1,0:T(8,128)S(1)}, u32[]{:S(2)}, u32[]{:S(2)}) collective-permute-start(f32[144,384]{1,0:T(8,128)S(1)} %reshape_reshape.7), channel_id=1, source_target_pairs={{0,24},{4,28},{8,16},{12,20},{16,8},{20,12},{24,0},{28,4},{1,25},{... | collective-permute-start | bytes 663560 | tf_op jit(solution)/shard_map/ppermute | solution.py:299
  185.4 12.6 %collective-permute-start.36 = (f32[576,384]{1,0:T(8,128)S(1)}, f32[576,384]{1,0:T(8,128)S(1)}, u32[]{:S(2)}, u32[]{:S(2)}) collective-permute-start(f32[576,384]{1,0:T(8,128)S(1)} %bitcast.92), channel_id=1, source_target_pairs={{0,4},{4,0},{8,12},{12,8},{16,20},{20,16},{24,28},{28,24},{1,5},{5... | collective-permute-start | bytes 2654216 | tf_op jit(solution)/shard_map/ppermute | solution.py:409
  (26 other events, 186.8 us)

commit v4 on v3

--- a/solution.py
+++ b/solution.py
@@ -418,9 +418,9 @@
         g_halo = halo(g_spec)
         *y, term = mix(place, (s_halo[0], s_spec, s_halo[1]), coef[0], ahead_weights, table, part_len, g_spec)
         g_halo = [after(x, *y) for x in g_halo]
-        others = [[after(x, *g_halo) for x in other] for other in exchange(y)]
+        others = exchange(y)
         halves = term.reshape(2, -1, channels)
-        give = after(lax.dynamic_index_in_dim(halves, 1 - core, 0, keepdims=False), *g_halo)
+        give = after(lax.dynamic_index_in_dim(halves, 1 - core, 0, keepdims=False), *g_halo, *[x for other in others for x in other])
         given = swap_core(give)
         o_blocks = total(y, others)
 

time: 200 us -> 198 us (0.990)
  waiting for transfers between devices: 52.6 us -> 27.8 us
  starting transfers between devices: 62 us -> 82.2 us
    ppermute x20, waiting for transfers between devices: 48.9 us -> 14.3 us  [send(): return lax.ppermute(x, AXES, pairs)]
    ppermute x20, starting transfers between devices: 27.4 us -> 45.7 us  [send(): return lax.ppermute(x, AXES, pairs)]
    ppermute x6, waiting for transfers between devices: 0.72 us -> 9.75 us  [share_shown(): lax.ppermute(x, axis, [(a, a ^ g * stride) for a in range(size)])]
    ppermute x6, starting transfers between devices: 10.4 us -> 14.5 us  [shares_sent(): lax.ppermute(piece, axis, [(a, a ^ g * stride) for a in range(size)])]
  transfers between devices with their start and end apart: 37 -> 37, of which waited for: 13 -> 12; matrix products, arithmetic and copies ran while one was open for 14% -> 14% of each run, Pallas kernels for 24% -> 24%
where the time goes in v4:
time: 198 us; the launch traced here: 196 us
  starting transfers between devices  82.2 us (42%)
  Pallas kernels  47.6 us (24%)
  waiting for transfers between devices  27.8 us (14%)
  other arithmetic  18.5 us (9%)
  local copies, waits for them, and re-layouts  17.6 us (9%)
  between operations  2.63 us (1%)
    ppermute x20, starting transfers between devices, send(): return lax.ppermute(x, AXES, pairs)  45.7 us
    pallas_call x2, Pallas kernels, mix(): kernel_call(body, (), [REMAIN] * n_rows + [WHOLE] + [REMAIN] * 2, [WHOLE]...  31 us
    ppermute x6, starting transfers between devices, shares_sent(): lax.ppermute(piece, axis, [(a, a ^ g * stride) for a in range(size)])  14.5 us
    ppermute x20, waiting for transfers between devices, send(): return lax.ppermute(x, AXES, pairs)  14.3 us
    pallas_call x2, Pallas kernels, transform(): kernel_call(body, (), [REMAIN] * (count + 1), WHOLE, jax.ShapeDtypeStruct...  12.2 us
    ppermute x6, waiting for transfers between devices, share_shown(): lax.ppermute(x, axis, [(a, a ^ g * stride) for a in range(size)])  9.75 us
    ppermute x6, starting transfers between devices, share_shown(): lax.ppermute(x, axis, [(a, a ^ g * stride) for a in range(size)])  8.71 us
    ppermute x2, starting transfers between devices, swap_core(): return lax.ppermute(x, 'lat', swap)  8.56 us
  transfers between devices with their start and end apart: 37, of which 12 were waited for; matrix products, arithmetic and copies ran while one was open for 14% of the time, Pallas kernels for 24%

profile of v4, /device:TPU:0, one launch (start us, length us, event | category | flops | bytes accessed | tf_op | source)
XLA Modules:
  0.0 196.4 jit_solution(2555177817960227417)
XLA Ops:
  4.9 3.0 %collective-permute-start.1 = (f32[360,384]{1,0:T(8,128)}, f32[360,384]{1,0:T(8,128)S(1)}, u32[]{:S(2)}, u32[]{:S(2)}) collective-permute-start(f32[360,384]{1,0:T(8,128)} %get-tuple-element.113), channel_id=1, source_target_pairs={{0,1},{1,5},{2,0},{3,4},{4,3},{5,7},{6,2},{7,6},{8,10},{9,14},{10,... | collective-permute-start | bytes 1658888 | tf_op jit(solution)/shard_map/ppermute | solution.py:315
  11.9 2.9 %reduce-precision_convert_fusion = (bf16[1152,384]{1,0:T(8,128)(2,1)}, bf16[1152,384]{1,0:T(8,128)(2,1)}) fusion(f32[3,384,384]{2,1,0:T(8,128)} %copy.11), kind=kLoop, calls=%fused_computation.1 | loop fusion | flops 1769472 | bytes 3538944 | tf_op jit(solution)/shard_map/convert_element_type | solution.py:92
  15.6 2.3 %dynamic-slice_bitcast_fusion.1 = (f32[360,384]{1,0:T(8,128)}, f32[360,384]{1,0:T(8,128)}) fusion(f32[2,360,384]{2,1,0:T(8,128)} %param.11, s32[]{:T(128)S(6)} %select_n.249, s32[]{:T(128)S(6)} %select_n.248), kind=kLoop, calls=%fused_computation.11 | loop fusion | bytes 2211848 | tf_op jit(solution)/shard_map/jit(dynamic_index_in_dim)/squeeze | solution.py:345
  18.0 3.6 %pad_maximum_fusion = (bf16[1152,768]{1,0:T(8,128)(2,1)}, bf16[1152,768]{1,0:T(8,128)(2,1)}) fusion(bf16[1152,384]{1,0:T(8,128)(2,1)S(1)} %copy-done.10, bf16[1152,384]{1,0:T(8,128)(2,1)S(1)} %copy-done.9, bf16[1152,384]{1,0:T(8,128)(2,1)} %get-tuple-element.108, bf16[1152,384]{1,0:T(8,128)(2,1)} %get-tuple-element.107), kind=kLoop, calls=%fused_computation.6 | loop fusion | flops 7077888 | bytes 7077888 | tf_op jit(solution)/shard_map/concatenate | solution.py:92
  21.7 6.6 %collective-permute-start.3 = (f32[360,384]{1,0:T(8,128)S(1)}, f32[360,384]{1,0:T(8,128)S(1)}, u32[]{:S(2)}, u32[]{:S(2)}) collective-permute-start(f32[360,384]{1,0:T(8,128)S(1)} %collective-permute-done.1.refs_1_), channel_id=1, source_target_pairs={{0,4},{4,0},{1,5},{5,1},{2,6},{6,2},{3,7},{7,3},{11,15},{15,11},{1... | collective-permute-start | bytes 1658888 | tf_op jit(solution)/shard_map/ppermute | solution.py:315
  28.3 13.1 %collective-permute-start.9 = (f32[360,384]{1,0:T(8,128)}, f32[360,384]{1,0:T(8,128)S(1)}, u32[]{:S(2)}, u32[]{:S(2)}) collective-permute-start(f32[360,384]{1,0:T(8,128)} %get-tuple-element.58), channel_id=1, source_target_pairs={{0,1},{1,5},{2,0},{3,4},{4,3},{5,7},{6,2},{7,6},{8,10},{9,14},{10,... | collective-permute-start | bytes 1658888 | tf_op jit(solution)/shard_map/ppermute | solution.py:315
  54.2 6.1 %shard_map.94.refs_1_ = f32[736,384]{1,0:T(8,128)S(1)} custom-call(s32[2]{0:T(128)S(1)} %pad_add_fusion.1.place, f32[360,384]{1,0:T(8,128)S(1)} %collective-permute-done.refs_0_, f32[360,384]{1,0:T(8,128)S(1)} %collective-permute-done.1.refs_1_, f32[360,384]{1,0:T(8,128)S(1)} %collective-permute-done.2.refs_2_, ...), custom_call_target="tpu_custom_call" | custom-call | flops 1 | bytes 1 | tf_op jit(solution)/shard_map/pallas_call | solution.py:175
  63.1 4.3 %collective-permute-start.4 = (f32[736,384]{1,0:T(8,128)S(1)}, f32[736,384]{1,0:T(8,128)S(1)}, u32[]{:S(2)}, u32[]{:S(2)}) collective-permute-start(f32[736,384]{1,0:T(8,128)S(1)} %shard_map.94.refs_1_), channel_id=1, source_target_pairs={{0,1},{4,5},{1,2},{5,6},{2,3},{6,7},{3,11},{7,15},{11,10},{15,14},... | collective-permute-start | bytes 3391496 | tf_op jit(solution)/shard_map/ppermute | solution.py:315
  67.5 6.1 %shard_map.95.refs_3_.refs_1_ = f32[736,384]{1,0:T(8,128)S(1)} custom-call(s32[2]{0:T(128)S(1)} %pad_add_fusion.1.place, f32[360,384]{1,0:T(8,128)S(1)} %collective-permute-done.5.refs_0_, f32[360,384]{1,0:T(8,128)S(1)} %collective-permute-done.9.refs_1_, f32[360,384]{1,0:T(8,128)S(1)} %collective-permute-done.10.refs_2_, ...), custom_call_target="tpu_custom_call" | custom-call | flops 1 | bytes 1 | tf_op jit(solution)/shard_map/pallas_call | solution.py:175
  74.9 4.8 %collective-permute-start.15 = (f32[736,384]{1,0:T(8,128)S(1)}, f32[736,384]{1,0:T(8,128)S(1)}, u32[]{:S(2)}, u32[]{:S(2)}) collective-permute-start(f32[736,384]{1,0:T(8,128)S(1)} %shard_map.95.refs_3_.refs_1_), channel_id=1, source_target_pairs={{0,1},{4,5},{1,2},{5,6},{2,3},{6,7},{3,11},{7,15},{11,10},{15,14},... | collective-permute-start | bytes 3391496 | tf_op jit(solution)/shard_map/ppermute | solution.py:315
  80.5 9.5 %collective-permute-done.12.refs_2_ = f32[736,384]{1,0:T(8,128)S(1)} collective-permute-done((f32[736,384]{1,0:T(8,128)S(1)}, f32[736,384]{1,0:T(8,128)S(1)}, u32[]{:S(2)}, u32[]{:S(2)}) %collective-permute-start.12) | collective-permute-done | bytes 1130528 | tf_op jit(solution)/shard_map/ppermute | solution.py:315
  89.9 2.6 %collective-permute-done.4.refs_0_ = f32[736,384]{1,0:T(8,128)S(1)} collective-permute-done((f32[736,384]{1,0:T(8,128)S(1)}, f32[736,384]{1,0:T(8,128)S(1)}, u32[]{:S(2)}, u32[]{:S(2)}) %collective-permute-start.4) | collective-permute-done | bytes 1130528 | tf_op jit(solution)/shard_map/ppermute | solution.py:315
  92.6 17.5 %shard_map.96 = (f32[360,384]{1,0:T(8,128)S(1)}, f32[360,384]{1,0:T(8,128)S(1)}, f32[360,384]{1,0:T(8,128)}, f32[360,384]{1,0:T(8,128)}, f32[1152,384]{1,0:T(8,128)}) custom-call(s32[2]{0:T(128)S(1)} %pad_add_fusion.1.place, f32[736,384]{1,0:T(8,128)S(1)} %collective-permute-done.4.refs_0_, f32[736,384]{1,0:T(8,128)S(1)} %shard_map.94.refs_1_, ...), custom_call_target="tpu_custom_call" | custom-call | flops 1 | bytes 1 | tf_op jit(solution)/shard_map/pallas_call | solution.py:246
  112.2 2.1 %dynamic-slice_bitcast_fusion = f32[576,384]{1,0:T(8,128)} fusion(f32[2,576,384]{2,1,0:T(8,128)} %bitcast.94, s32[]{:T(128)S(6)} %select_n.274), kind=kLoop, calls=%fused_computation.10 | loop fusion | bytes 1769476 | tf_op jit(solution)/shard_map/jit(dynamic_index_in_dim)/squeeze | solution.py:423
  122.8 8.6 %collective-permute-start.21 = (f32[144,384]{1,0:T(8,128)S(1)}, f32[144,384]{1,0:T(8,128)}, u32[]{:S(2)}, u32[]{:S(2)}) collective-permute-start(f32[144,384]{1,0:T(8,128)S(1)} %get-tuple-element.115), channel_id=1, source_target_pairs={{0,8},{4,12},{8,0},{12,4},{16,24},{20,28},{24,16},{28,20},{1,9},{5... | collective-permute-start | bytes 663560 | tf_op jit(solution)/shard_map/ppermute | solution.py:286
  132.9 3.5 %collective-permute-start.19 = (f32[360,384]{1,0:T(8,128)}, f32[360,384]{1,0:T(8,128)}, u32[]{:S(2)}, u32[]{:S(2)}) collective-permute-start(f32[360,384]{1,0:T(8,128)} %add.125), channel_id=1, source_target_pairs={{1,0},{5,1},{0,2},{4,3},{3,4},{7,5},{2,6},{6,7},{10,8},{14,9},{11,... | collective-permute-start | bytes 1658888 | tf_op jit(solution)/shard_map/ppermute | solution.py:315
  136.4 13.5 %shard_map.97 = (f32[360,384]{1,0:T(8,128)S(1)}, f32[360,384]{1,0:T(8,128)S(1)}, f32[360,384]{1,0:T(8,128)}, f32[360,384]{1,0:T(8,128)}) custom-call(s32[2]{0:T(128)S(1)} %pad_add_fusion.1.place, f32[736,384]{1,0:T(8,128)S(1)} %collective-permute-done.15.refs_0_, f32[736,384]{1,0:T(8,128)S(1)} %copy-done.1, f32[736,384]{1,0:T(8,128)S(1)} %collective-permute-done.17.refs_2_, ...), custom_call_target="tpu_custom_call" | custom-call | flops 1 | bytes 1 | tf_op jit(solution)/shard_map/pallas_call | solution.py:246
  153.6 3.5 %collective-permute-start.27 = (f32[108,128]{1,0:T(8,128)S(1)}, f32[108,128]{1,0:T(8,128)S(1)}, u32[]{:S(2)}, u32[]{:S(2)}) collective-permute-start(f32[108,128]{1,0:T(8,128)S(1)} %get-tuple-element.122), channel_id=1, source_target_pairs={{0,3},{1,2},{2,1},{3,0},{4,7},{5,6},{6,5},{7,4},{8,11},{9,10},{10,... | collective-permute-start | bytes 165896 | tf_op jit(solution)/shard_map/ppermute | solution.py:286
  158.4 2.2 %collective-permute-done.26 = f32[108,128]{1,0:T(8,128)S(1)} collective-permute-done((f32[108,128]{1,0:T(8,128)S(1)}, f32[108,128]{1,0:T(8,128)S(1)}, u32[]{:S(2)}, u32[]{:S(2)}) %collective-permute-start.26) | collective-permute-done | bytes 55328 | tf_op jit(solution)/shard_map/ppermute | solution.py:286
  170.4 2.4 %collective-permute-start.34 = (f32[144,384]{1,0:T(8,128)S(1)}, f32[144,384]{1,0:T(8,128)S(1)}, u32[]{:S(2)}, u32[]{:S(2)}) collective-permute-start(f32[144,384]{1,0:T(8,128)S(1)} %reshape_reshape.7), channel_id=1, source_target_pairs={{0,16},{4,20},{8,24},{12,28},{16,0},{20,4},{24,8},{28,12},{1,17},{... | collective-permute-start | bytes 663560 | tf_op jit(solution)/shard_map/ppermute | solution.py:299
  174.3 2.7 %shard_map.98 = f32[2,360,384]{2,1,0:T(8,128)} custom-call(s32[2]{0:T(128)S(1)} %pad_add_fusion.flags, f32[360,384]{1,0:T(8,128)S(1)} %copy-done.7, f32[360,384]{1,0:T(8,128)} %collective-permute-done.19.b), custom_call_target="tpu_custom_call" | custom-call | flops 1 | bytes 1 | tf_op jit(solution)/shard_map/pallas_call | solution.py:271
  177.0 2.2 %collective-permute-done.35 = f32[144,384]{1,0:T(8,128)S(1)} collective-permute-done((f32[144,384]{1,0:T(8,128)S(1)}, f32[144,384]{1,0:T(8,128)S(1)}, u32[]{:S(2)}, u32[]{:S(2)}) %collective-permute-start.35) | collective-permute-done | bytes 221216 | tf_op jit(solution)/shard_map/ppermute | solution.py:299
  179.3 3.6 %collective-permute-done.34 = f32[144,384]{1,0:T(8,128)S(1)} collective-permute-done((f32[144,384]{1,0:T(8,128)S(1)}, f32[144,384]{1,0:T(8,128)S(1)}, u32[]{:S(2)}, u32[]{:S(2)}) %collective-permute-start.34) | collective-permute-done | bytes 221216 | tf_op jit(solution)/shard_map/ppermute | solution.py:299
  184.4 8.5 %collective-permute-start.36 = (f32[576,384]{1,0:T(8,128)S(1)}, f32[576,384]{1,0:T(8,128)S(1)}, u32[]{:S(2)}, u32[]{:S(2)}) collective-permute-start(f32[576,384]{1,0:T(8,128)S(1)} %bitcast.92), channel_id=1, source_target_pairs={{0,4},{4,0},{8,12},{12,8},{16,20},{20,16},{24,28},{28,24},{1,5},{5... | collective-permute-start | bytes 2654216 | tf_op jit(solution)/shard_map/ppermute | solution.py:409
  (129 shorter events, 58.2 us)
Async XLA Ops:
  4.9 16.8 %collective-permute-start.1 = (f32[360,384]{1,0:T(8,128)}, f32[360,384]{1,0:T(8,128)S(1)}, u32[]{:S(2)}, u32[]{:S(2)}) collective-permute-start(f32[360,384]{1,0:T(8,128)} %get-tuple-element.113), channel_id=1, source_target_pairs={{0,1},{1,5},{2,0},{3,4},{4,3},{5,7},{6,2},{7,6},{8,10},{9,14},{10,... | collective-permute-start | bytes 1658888 | tf_op jit(solution)/shard_map/ppermute | solution.py:315
  7.9 13.8 %collective-permute-start = (f32[360,384]{1,0:T(8,128)S(1)}, f32[360,384]{1,0:T(8,128)S(1)}, u32[]{:S(2)}, u32[]{:S(2)}) collective-permute-start(f32[360,384]{1,0:T(8,128)S(1)} %get-tuple-element.114), channel_id=1, source_target_pairs={{0,0},{1,4},{2,1},{3,5},{4,2},{5,6},{6,3},{7,7},{8,11},{9,15},{10,... | collective-permute-start | bytes 1658888 | tf_op jit(solution)/shard_map/ppermute | solution.py:315
  21.7 32.5 %collective-permute-start.3 = (f32[360,384]{1,0:T(8,128)S(1)}, f32[360,384]{1,0:T(8,128)S(1)}, u32[]{:S(2)}, u32[]{:S(2)}) collective-permute-start(f32[360,384]{1,0:T(8,128)S(1)} %collective-permute-done.1.refs_1_), channel_id=1, source_target_pairs={{0,4},{4,0},{1,5},{5,1},{2,6},{6,2},{3,7},{7,3},{11,15},{15,11},{1... | collective-permute-start | bytes 1658888 | tf_op jit(solution)/shard_map/ppermute | solution.py:315
  28.3 25.9 %collective-permute-start.2 = (f32[360,384]{1,0:T(8,128)S(1)}, f32[360,384]{1,0:T(8,128)S(1)}, u32[]{:S(2)}, u32[]{:S(2)}) collective-permute-start(f32[360,384]{1,0:T(8,128)S(1)} %collective-permute-done.refs_0_), channel_id=1, source_target_pairs={{0,4},{4,0},{1,5},{5,1},{2,6},{6,2},{3,7},{7,3},{11,15},{15,11},{1... | collective-permute-start | bytes 1658888 | tf_op jit(solution)/shard_map/ppermute | solution.py:315
  28.3 33.5 %collective-permute-start.9 = (f32[360,384]{1,0:T(8,128)}, f32[360,384]{1,0:T(8,128)S(1)}, u32[]{:S(2)}, u32[]{:S(2)}) collective-permute-start(f32[360,384]{1,0:T(8,128)} %get-tuple-element.58), channel_id=1, source_target_pairs={{0,1},{1,5},{2,0},{3,4},{4,3},{5,7},{6,2},{7,6},{8,10},{9,14},{10,... | collective-permute-start | bytes 1658888 | tf_op jit(solution)/shard_map/ppermute | solution.py:315
  44.1 18.9 %collective-permute-start.5 = (f32[360,384]{1,0:T(8,128)}, f32[360,384]{1,0:T(8,128)S(1)}, u32[]{:S(2)}, u32[]{:S(2)}) collective-permute-start(f32[360,384]{1,0:T(8,128)} %get-tuple-element.55), channel_id=1, source_target_pairs={{0,0},{1,4},{2,1},{3,5},{4,2},{5,6},{6,3},{7,7},{8,11},{9,15},{10,... | collective-permute-start | bytes 1658888 | tf_op jit(solution)/shard_map/ppermute | solution.py:315
  60.3 29.6 %collective-permute-start.12 = (f32[736,384]{1,0:T(8,128)S(1)}, f32[736,384]{1,0:T(8,128)S(1)}, u32[]{:S(2)}, u32[]{:S(2)}) collective-permute-start(f32[736,384]{1,0:T(8,128)S(1)} %shard_map.94.refs_1_), channel_id=1, source_target_pairs={{1,0},{5,4},{2,1},{6,5},{3,2},{7,6},{11,3},{15,7},{10,11},{14,15},... | collective-permute-start | bytes 3391496 | tf_op jit(solution)/shard_map/ppermute | solution.py:315
  63.1 29.5 %collective-permute-start.4 = (f32[736,384]{1,0:T(8,128)S(1)}, f32[736,384]{1,0:T(8,128)S(1)}, u32[]{:S(2)}, u32[]{:S(2)}) collective-permute-start(f32[736,384]{1,0:T(8,128)S(1)} %shard_map.94.refs_1_), channel_id=1, source_target_pairs={{0,1},{4,5},{1,2},{5,6},{2,3},{6,7},{3,11},{7,15},{11,10},{15,14},... | collective-permute-start | bytes 3391496 | tf_op jit(solution)/shard_map/ppermute | solution.py:315
  73.6 40.7 %collective-permute-start.17 = (f32[736,384]{1,0:T(8,128)S(1)}, f32[736,384]{1,0:T(8,128)S(1)}, u32[]{:S(2)}, u32[]{:S(2)}) collective-permute-start(f32[736,384]{1,0:T(8,128)S(1)} %shard_map.95.refs_3_.refs_1_), channel_id=1, source_target_pairs={{1,0},{5,4},{2,1},{6,5},{3,2},{7,6},{11,3},{15,7},{10,11},{14,15},... | collective-permute-start | bytes 3391496 | tf_op jit(solution)/shard_map/ppermute | solution.py:315
  74.9 41.5 %collective-permute-start.15 = (f32[736,384]{1,0:T(8,128)S(1)}, f32[736,384]{1,0:T(8,128)S(1)}, u32[]{:S(2)}, u32[]{:S(2)}) collective-permute-start(f32[736,384]{1,0:T(8,128)S(1)} %shard_map.95.refs_3_.refs_1_), channel_id=1, source_target_pairs={{0,1},{4,5},{1,2},{5,6},{2,3},{6,7},{3,11},{7,15},{11,10},{15,14},... | collective-permute-start | bytes 3391496 | tf_op jit(solution)/shard_map/ppermute | solution.py:315
  117.9 32.0 %collective-permute-start.14 = (f32[360,384]{1,0:T(8,128)S(1)}, f32[360,384]{1,0:T(8,128)S(1)}, u32[]{:S(2)}, u32[]{:S(2)}) collective-permute-start(f32[360,384]{1,0:T(8,128)S(1)} %add.124), channel_id=1, source_target_pairs={{0,0},{4,1},{1,2},{5,3},{2,4},{6,5},{3,6},{7,7},{11,8},{15,9},{10,... | collective-permute-start | bytes 1658888 | tf_op jit(solution)/shard_map/ppermute | solution.py:315
  122.8 28.0 %collective-permute-start.21 = (f32[144,384]{1,0:T(8,128)S(1)}, f32[144,384]{1,0:T(8,128)}, u32[]{:S(2)}, u32[]{:S(2)}) collective-permute-start(f32[144,384]{1,0:T(8,128)S(1)} %get-tuple-element.115), channel_id=1, source_target_pairs={{0,8},{4,12},{8,0},{12,4},{16,24},{20,28},{24,16},{28,20},{1,9},{5... | collective-permute-start | bytes 663560 | tf_op jit(solution)/shard_map/ppermute | solution.py:286
  131.4 19.8 %collective-permute-start.22 = (f32[144,384]{1,0:T(8,128)}, f32[144,384]{1,0:T(8,128)}, u32[]{:S(2)}, u32[]{:S(2)}) collective-permute-start(f32[144,384]{1,0:T(8,128)} %get-tuple-element.117), channel_id=1, source_target_pairs={{0,16},{4,20},{8,24},{12,28},{16,0},{20,4},{24,8},{28,12},{1,17},{... | collective-permute-start | bytes 663560 | tf_op jit(solution)/shard_map/ppermute | solution.py:286
  131.4 19.8 %collective-permute-start.23 = (f32[144,384]{1,0:T(8,128)}, f32[144,384]{1,0:T(8,128)}, u32[]{:S(2)}, u32[]{:S(2)}) collective-permute-start(f32[144,384]{1,0:T(8,128)} %get-tuple-element.116), channel_id=1, source_target_pairs={{0,24},{4,28},{8,16},{12,20},{16,8},{20,12},{24,0},{28,4},{1,25},{... | collective-permute-start | bytes 663560 | tf_op jit(solution)/shard_map/ppermute | solution.py:286
  132.9 20.7 %collective-permute-start.19 = (f32[360,384]{1,0:T(8,128)}, f32[360,384]{1,0:T(8,128)}, u32[]{:S(2)}, u32[]{:S(2)}) collective-permute-start(f32[360,384]{1,0:T(8,128)} %add.125), channel_id=1, source_target_pairs={{1,0},{5,1},{0,2},{4,3},{3,4},{7,5},{2,6},{6,7},{10,8},{14,9},{11,... | collective-permute-start | bytes 1658888 | tf_op jit(solution)/shard_map/ppermute | solution.py:315
  152.7 7.9 %collective-permute-start.26 = (f32[108,128]{1,0:T(8,128)S(1)}, f32[108,128]{1,0:T(8,128)S(1)}, u32[]{:S(2)}, u32[]{:S(2)}) collective-permute-start(f32[108,128]{1,0:T(8,128)S(1)} %get-tuple-element.123), channel_id=1, source_target_pairs={{0,2},{1,3},{2,0},{3,1},{4,6},{5,7},{6,4},{7,5},{8,10},{9,11},{10,... | collective-permute-start | bytes 165896 | tf_op jit(solution)/shard_map/ppermute | solution.py:286
  153.6 7.0 %collective-permute-start.27 = (f32[108,128]{1,0:T(8,128)S(1)}, f32[108,128]{1,0:T(8,128)S(1)}, u32[]{:S(2)}, u32[]{:S(2)}) collective-permute-start(f32[108,128]{1,0:T(8,128)S(1)} %get-tuple-element.122), channel_id=1, source_target_pairs={{0,3},{1,2},{2,1},{3,0},{4,7},{5,6},{6,5},{7,4},{8,11},{9,10},{10,... | collective-permute-start | bytes 165896 | tf_op jit(solution)/shard_map/ppermute | solution.py:286
  160.6 6.6 %collective-permute-start.30 = (f32[108,128]{1,0:T(8,128)S(1)}, f32[108,128]{1,0:T(8,128)S(1)}, u32[]{:S(2)}, u32[]{:S(2)}) collective-permute-start(f32[108,128]{1,0:T(8,128)S(1)} %get-tuple-element.104), channel_id=1, source_target_pairs={{0,1},{1,0},{2,3},{3,2},{4,5},{5,4},{6,7},{7,6},{8,9},{9,8},{10,11... | collective-permute-start | bytes 165896 | tf_op jit(solution)/shard_map/ppermute | solution.py:299
  165.1 11.9 %collective-permute-start.28 = (f32[360,384]{1,0:T(8,128)S(1)}, f32[360,384]{1,0:T(8,128)S(1)}, u32[]{:S(2)}, u32[]{:S(2)}) collective-permute-start(f32[360,384]{1,0:T(8,128)S(1)} %add.129), channel_id=1, source_target_pairs={{0,0},{4,1},{1,2},{5,3},{2,4},{6,5},{3,6},{7,7},{11,8},{15,9},{10,... | collective-permute-start | bytes 1658888 | tf_op jit(solution)/shard_map/ppermute | solution.py:315
  165.8 18.4 %collective-permute-start.29 = (f32[360,384]{1,0:T(8,128)S(1)}, f32[360,384]{1,0:T(8,128)S(1)}, u32[]{:S(2)}, u32[]{:S(2)}) collective-permute-start(f32[360,384]{1,0:T(8,128)S(1)} %add.138), channel_id=1, source_target_pairs={{1,0},{5,1},{0,2},{4,3},{3,4},{7,5},{2,6},{6,7},{10,8},{14,9},{11,... | collective-permute-start | bytes 1658888 | tf_op jit(solution)/shard_map/ppermute | solution.py:315
  169.9 9.3 %collective-permute-start.35 = (f32[144,384]{1,0:T(8,128)S(1)}, f32[144,384]{1,0:T(8,128)S(1)}, u32[]{:S(2)}, u32[]{:S(2)}) collective-permute-start(f32[144,384]{1,0:T(8,128)S(1)} %reshape_reshape.7), channel_id=1, source_target_pairs={{0,24},{4,28},{8,16},{12,20},{16,8},{20,12},{24,0},{28,4},{1,25},{... | collective-permute-start | bytes 663560 | tf_op jit(solution)/shard_map/ppermute | solution.py:299
  170.4 12.4 %collective-permute-start.34 = (f32[144,384]{1,0:T(8,128)S(1)}, f32[144,384]{1,0:T(8,128)S(1)}, u32[]{:S(2)}, u32[]{:S(2)}) collective-permute-start(f32[144,384]{1,0:T(8,128)S(1)} %reshape_reshape.7), channel_id=1, source_target_pairs={{0,16},{4,20},{8,24},{12,28},{16,0},{20,4},{24,8},{28,12},{1,17},{... | collective-permute-start | bytes 663560 | tf_op jit(solution)/shard_map/ppermute | solution.py:299
  172.8 11.4 %collective-permute-start.33 = (f32[144,384]{1,0:T(8,128)S(1)}, f32[144,384]{1,0:T(8,128)S(1)}, u32[]{:S(2)}, u32[]{:S(2)}) collective-permute-start(f32[144,384]{1,0:T(8,128)S(1)} %reshape_reshape.7), channel_id=1, source_target_pairs={{0,8},{4,12},{8,0},{12,4},{16,24},{20,28},{24,16},{28,20},{1,9},{5... | collective-permute-start | bytes 663560 | tf_op jit(solution)/shard_map/ppermute | solution.py:299
  184.4 10.5 %collective-permute-start.36 = (f32[576,384]{1,0:T(8,128)S(1)}, f32[576,384]{1,0:T(8,128)S(1)}, u32[]{:S(2)}, u32[]{:S(2)}) collective-permute-start(f32[576,384]{1,0:T(8,128)S(1)} %bitcast.92), channel_id=1, source_target_pairs={{0,4},{4,0},{8,12},{12,8},{16,20},{20,16},{24,28},{28,24},{1,5},{5... | collective-permute-start | bytes 2654216 | tf_op jit(solution)/shard_map/ppermute | solution.py:409
  (28 other events, 225.4 us)

commit v5 on v4

--- a/solution.py
+++ b/solution.py
@@ -10,7 +10,7 @@
 
 AXES = ("lat", "lon")
 SLOTS = 4
-VMEM = 48 * 2**20
+VMEM = 51 * 2**20
 BF16 = jnp.bfloat16
 
 

time: 198 us -> 195 us (0.985)
  local copies, waits for them, and re-layouts: 17.6 us -> 13.2 us
  Pallas kernels: 47.6 us -> 50.4 us
  waiting for transfers between devices: 27.8 us -> 25.8 us
    pallas_call x2, Pallas kernels: 12.2 us -> 14.3 us  [transform(): kernel_call(body, (), [REMAIN] * (count + 1), WHOLE, jax.ShapeDtypeStruct...]
  transfers between devices with their start and end apart: 37 -> 37, of which waited for: 12 -> 12; matrix products, arithmetic and copies ran while one was open for 14% -> 13% of each run, Pallas kernels for 24% -> 26%
where the time goes in v5:
time: 195 us; the launch traced here: 194 us
  starting transfers between devices  83.5 us (43%)
  Pallas kernels  50.4 us (26%)
  waiting for transfers between devices  25.8 us (13%)
  other arithmetic  18.6 us (10%)
  local copies, waits for them, and re-layouts  13.2 us (7%)
  between operations  2.51 us (1%)
    ppermute x20, starting transfers between devices, send(): return lax.ppermute(x, AXES, pairs)  46.9 us
    pallas_call x2, Pallas kernels, mix(): kernel_call(body, (), [REMAIN] * n_rows + [WHOLE] + [REMAIN] * 2, [WHOLE]...  32.8 us
    ppermute x6, starting transfers between devices, shares_sent(): lax.ppermute(piece, axis, [(a, a ^ g * stride) for a in range(size)])  14.7 us
    pallas_call x2, Pallas kernels, transform(): kernel_call(body, (), [REMAIN] * (count + 1), WHOLE, jax.ShapeDtypeStruct...  14.3 us
    ppermute x20, waiting for transfers between devices, send(): return lax.ppermute(x, AXES, pairs)  13.5 us
    ppermute x6, waiting for transfers between devices, share_shown(): lax.ppermute(x, axis, [(a, a ^ g * stride) for a in range(size)])  10.5 us
    ppermute x2, starting transfers between devices, swap_core(): return lax.ppermute(x, 'lat', swap)  9.2 us
    ppermute x6, starting transfers between devices, share_shown(): lax.ppermute(x, axis, [(a, a ^ g * stride) for a in range(size)])  8.12 us
  transfers between devices with their start and end apart: 37, of which 12 were waited for; matrix products, arithmetic and copies ran while one was open for 13% of the time, Pallas kernels for 26%

profile of v5, /device:TPU:0, one launch (start us, length us, event | category | flops | bytes accessed | tf_op | source)
XLA Modules:
  0.0 193.9 jit_solution(13133373955393061770)
XLA Ops:
  2.7 2.2 %dynamic-slice_bitcast_fusion.3 = (f32[360,384]{1,0:T(8,128)}, f32[360,384]{1,0:T(8,128)S(1)}) fusion(f32[2,360,384]{2,1,0:T(8,128)} %param.7, s32[]{:T(128)S(6)} %select_n.249, s32[]{:T(128)S(6)} %select_n.248), kind=kLoop, calls=%fused_computation.13 | loop fusion | bytes 2211848 | tf_op jit(solution)/shard_map/jit(dynamic_index_in_dim)/squeeze | solution.py:345
  4.9 3.0 %collective-permute-start.1 = (f32[360,384]{1,0:T(8,128)}, f32[360,384]{1,0:T(8,128)S(1)}, u32[]{:S(2)}, u32[]{:S(2)}) collective-permute-start(f32[360,384]{1,0:T(8,128)} %get-tuple-element.113), channel_id=1, source_target_pairs={{0,1},{1,5},{2,0},{3,4},{4,3},{5,7},{6,2},{7,6},{8,10},{9,14},{10,... | collective-permute-start | bytes 1658888 | tf_op jit(solution)/shard_map/ppermute | solution.py:315
  11.9 3.0 %reduce-precision_convert_fusion = (bf16[1152,384]{1,0:T(8,128)(2,1)}, bf16[1152,384]{1,0:T(8,128)(2,1)}) fusion(f32[3,384,384]{2,1,0:T(8,128)} %copy.11), kind=kLoop, calls=%fused_computation.1 | loop fusion | flops 1769472 | bytes 3538944 | tf_op jit(solution)/shard_map/convert_element_type | solution.py:92
  15.7 2.3 %dynamic-slice_bitcast_fusion.1 = (f32[360,384]{1,0:T(8,128)}, f32[360,384]{1,0:T(8,128)}) fusion(f32[2,360,384]{2,1,0:T(8,128)} %param.11, s32[]{:T(128)S(6)} %select_n.249, s32[]{:T(128)S(6)} %select_n.248), kind=kLoop, calls=%fused_computation.11 | loop fusion | bytes 2211848 | tf_op jit(solution)/shard_map/jit(dynamic_index_in_dim)/squeeze | solution.py:345
  18.0 3.7 %pad_maximum_fusion = (bf16[1152,768]{1,0:T(8,128)(2,1)}, bf16[1152,768]{1,0:T(8,128)(2,1)}) fusion(bf16[1152,384]{1,0:T(8,128)(2,1)S(1)} %copy-done.2, bf16[1152,384]{1,0:T(8,128)(2,1)S(1)} %copy-done.1, bf16[1152,384]{1,0:T(8,128)(2,1)} %get-tuple-element.108, bf16[1152,384]{1,0:T(8,128)(2,1)} %get-tuple-element.107), kind=kLoop, calls=%fused_computation.6 | loop fusion | flops 7077888 | bytes 7077888 | tf_op jit(solution)/shard_map/concatenate | solution.py:92
  21.7 6.6 %collective-permute-start.3 = (f32[360,384]{1,0:T(8,128)S(1)}, f32[360,384]{1,0:T(8,128)S(1)}, u32[]{:S(2)}, u32[]{:S(2)}) collective-permute-start(f32[360,384]{1,0:T(8,128)S(1)} %collective-permute-done.1.refs_1_), channel_id=1, source_target_pairs={{0,4},{4,0},{1,5},{5,1},{2,6},{6,2},{3,7},{7,3},{11,15},{15,11},{1... | collective-permute-start | bytes 1658888 | tf_op jit(solution)/shard_map/ppermute | solution.py:315
  28.3 13.1 %collective-permute-start.9 = (f32[360,384]{1,0:T(8,128)}, f32[360,384]{1,0:T(8,128)S(1)}, u32[]{:S(2)}, u32[]{:S(2)}) collective-permute-start(f32[360,384]{1,0:T(8,128)} %get-tuple-element.58), channel_id=1, source_target_pairs={{0,1},{1,5},{2,0},{3,4},{4,3},{5,7},{6,2},{7,6},{8,10},{9,14},{10,... | collective-permute-start | bytes 1658888 | tf_op jit(solution)/shard_map/ppermute | solution.py:315
  46.3 2.0 %collective-permute-start.8 = (f32[36,360]{1,0:T(8,128)S(1)}, f32[36,360]{1,0:T(8,128)}, u32[]{:S(2)}, u32[]{:S(2)}) collective-permute-start(f32[36,360]{1,0:T(8,128)S(1)} %constant_dynamic-slice_fusion), channel_id=1, source_target_pairs={{0,4},{4,0},{8,12},{12,8},{16,20},{20,16},{24,28},{28,24},{1,5},{5... | collective-permute-start | bytes 155528 | tf_op jit(solution)/shard_map/ppermute | solution.py:396
  50.4 7.1 %shard_map.94.refs_1_ = f32[736,384]{1,0:T(8,128)} custom-call(s32[2]{0:T(128)S(1)} %pad_add_fusion.1.place, f32[360,384]{1,0:T(8,128)S(1)} %collective-permute-done.refs_0_, f32[360,384]{1,0:T(8,128)S(1)} %collective-permute-done.1.refs_1_, f32[360,384]{1,0:T(8,128)S(1)} %collective-permute-done.2.refs_2_, f32[360,384]{1,0:T(8,128)S(1)} %collective-permute-done.3.refs_3_, ...), custom_call_target="tpu_custom_call" | custom-call | flops 1 | bytes 1 | tf_op jit(solution)/shard_map/pallas_call | solution.py:175
  60.3 4.3 %collective-permute-start.4 = (f32[736,384]{1,0:T(8,128)}, f32[736,384]{1,0:T(8,128)S(1)}, u32[]{:S(2)}, u32[]{:S(2)}) collective-permute-start(f32[736,384]{1,0:T(8,128)} %shard_map.94.refs_1_), channel_id=1, source_target_pairs={{0,1},{4,5},{1,2},{5,6},{2,3},{6,7},{3,11},{7,15},{11,10},{15,14},... | collective-permute-start | bytes 3391496 | tf_op jit(solution)/shard_map/ppermute | solution.py:315
  64.6 7.2 %shard_map.95.refs_3_.refs_1_ = f32[736,384]{1,0:T(8,128)} custom-call(s32[2]{0:T(128)S(1)} %pad_add_fusion.1.place, f32[360,384]{1,0:T(8,128)S(1)} %collective-permute-done.5.refs_0_, f32[360,384]{1,0:T(8,128)S(1)} %collective-permute-done.9.refs_1_, f32[360,384]{1,0:T(8,128)S(1)} %collective-permute-done.10.refs_2_, ...), custom_call_target="tpu_custom_call" | custom-call | flops 1 | bytes 1 | tf_op jit(solution)/shard_map/pallas_call | solution.py:175
  73.1 5.6 %collective-permute-start.15 = (f32[736,384]{1,0:T(8,128)}, f32[736,384]{1,0:T(8,128)}, u32[]{:S(2)}, u32[]{:S(2)}) collective-permute-start(f32[736,384]{1,0:T(8,128)} %shard_map.95.refs_3_.refs_1_), channel_id=1, source_target_pairs={{0,1},{4,5},{1,2},{5,6},{2,3},{6,7},{3,11},{7,15},{11,10},{15,14},... | collective-permute-start | bytes 3391496 | tf_op jit(solution)/shard_map/ppermute | solution.py:315
  78.7 8.6 %collective-permute-done.12.refs_2_ = f32[736,384]{1,0:T(8,128)S(1)} collective-permute-done((f32[736,384]{1,0:T(8,128)}, f32[736,384]{1,0:T(8,128)S(1)}, u32[]{:S(2)}, u32[]{:S(2)}) %collective-permute-start.12) | collective-permute-done | bytes 1130528 | tf_op jit(solution)/shard_map/ppermute | solution.py:315
  87.3 2.8 %collective-permute-done.4.refs_0_ = f32[736,384]{1,0:T(8,128)S(1)} collective-permute-done((f32[736,384]{1,0:T(8,128)}, f32[736,384]{1,0:T(8,128)S(1)}, u32[]{:S(2)}, u32[]{:S(2)}) %collective-permute-start.4) | collective-permute-done | bytes 1130528 | tf_op jit(solution)/shard_map/ppermute | solution.py:315
  91.2 17.9 %shard_map.96 = (f32[360,384]{1,0:T(8,128)S(1)}, f32[360,384]{1,0:T(8,128)S(1)}, f32[360,384]{1,0:T(8,128)S(1)}, f32[360,384]{1,0:T(8,128)S(1)}, f32[1152,384]{1,0:T(8,128)}) custom-call(s32[2]{0:T(128)S(1)} %pad_add_fusion.1.place, f32[736,384]{1,0:T(8,128)} %copy-done.6, f32[736,384]{1,0:T(8,128)} %shard_map.94.refs_1_, f32[736,384]{1,0:T(8,128)} %copy-done.5, ...), custom_call_target="tpu_custom_call" | custom-call | flops 1 | bytes 1 | tf_op jit(solution)/shard_map/pallas_call | solution.py:246
  109.7 2.1 %dynamic-slice_bitcast_fusion = f32[576,384]{1,0:T(8,128)} fusion(f32[2,576,384]{2,1,0:T(8,128)} %bitcast.94, s32[]{:T(128)S(6)} %select_n.274), kind=kLoop, calls=%fused_computation.10 | loop fusion | bytes 1769476 | tf_op jit(solution)/shard_map/jit(dynamic_index_in_dim)/squeeze | solution.py:423
  111.8 2.0 %collective-permute-done.15.refs_0_ = f32[736,384]{1,0:T(8,128)} collective-permute-done((f32[736,384]{1,0:T(8,128)}, f32[736,384]{1,0:T(8,128)}, u32[]{:S(2)}, u32[]{:S(2)}) %collective-permute-start.15) | collective-permute-done | bytes 1130528 | tf_op jit(solution)/shard_map/ppermute | solution.py:315
  119.6 8.7 %collective-permute-start.21 = (f32[144,384]{1,0:T(8,128)S(1)}, f32[144,384]{1,0:T(8,128)}, u32[]{:S(2)}, u32[]{:S(2)}) collective-permute-start(f32[144,384]{1,0:T(8,128)S(1)} %get-tuple-element.115), channel_id=1, source_target_pairs={{0,8},{4,12},{8,0},{12,4},{16,24},{20,28},{24,16},{28,20},{1,9},{5... | collective-permute-start | bytes 663560 | tf_op jit(solution)/shard_map/ppermute | solution.py:286
  129.8 3.6 %collective-permute-start.19 = (f32[360,384]{1,0:T(8,128)}, f32[360,384]{1,0:T(8,128)S(1)}, u32[]{:S(2)}, u32[]{:S(2)}) collective-permute-start(f32[360,384]{1,0:T(8,128)} %add.125), channel_id=1, source_target_pairs={{1,0},{5,1},{0,2},{4,3},{3,4},{7,5},{2,6},{6,7},{10,8},{14,9},{11,... | collective-permute-start | bytes 1658888 | tf_op jit(solution)/shard_map/ppermute | solution.py:315
  133.4 14.9 %shard_map.97 = (f32[360,384]{1,0:T(8,128)S(1)}, f32[360,384]{1,0:T(8,128)S(1)}, f32[360,384]{1,0:T(8,128)S(1)}, f32[360,384]{1,0:T(8,128)}) custom-call(s32[2]{0:T(128)S(1)} %pad_add_fusion.1.place, f32[736,384]{1,0:T(8,128)} %collective-permute-done.15.refs_0_, f32[736,384]{1,0:T(8,128)} %shard_map.95.refs_3_.refs_1_, f32[736,384]{1,0:T(8,128)} %copy-done.4, ...), custom_call_target="tpu_custom_call" | custom-call | flops 1 | bytes 1 | tf_op jit(solution)/shard_map/pallas_call | solution.py:246
  151.1 3.5 %collective-permute-start.27 = (f32[108,128]{1,0:T(8,128)S(1)}, f32[108,128]{1,0:T(8,128)S(1)}, u32[]{:S(2)}, u32[]{:S(2)}) collective-permute-start(f32[108,128]{1,0:T(8,128)S(1)} %get-tuple-element.122), channel_id=1, source_target_pairs={{0,3},{1,2},{2,1},{3,0},{4,7},{5,6},{6,5},{7,4},{8,11},{9,10},{10,... | collective-permute-start | bytes 165896 | tf_op jit(solution)/shard_map/ppermute | solution.py:286
  172.8 3.9 %collective-permute-done.35 = f32[144,384]{1,0:T(8,128)S(1)} collective-permute-done((f32[144,384]{1,0:T(8,128)S(1)}, f32[144,384]{1,0:T(8,128)S(1)}, u32[]{:S(2)}, u32[]{:S(2)}) %collective-permute-start.35) | collective-permute-done | bytes 221216 | tf_op jit(solution)/shard_map/ppermute | solution.py:299
  176.7 3.2 %collective-permute-done.34 = f32[144,384]{1,0:T(8,128)S(1)} collective-permute-done((f32[144,384]{1,0:T(8,128)S(1)}, f32[144,384]{1,0:T(8,128)S(1)}, u32[]{:S(2)}, u32[]{:S(2)}) %collective-permute-start.34) | collective-permute-done | bytes 221216 | tf_op jit(solution)/shard_map/ppermute | solution.py:299
  181.2 9.2 %collective-permute-start.36 = (f32[576,384]{1,0:T(8,128)S(1)}, f32[576,384]{1,0:T(8,128)S(1)}, u32[]{:S(2)}, u32[]{:S(2)}) collective-permute-start(f32[576,384]{1,0:T(8,128)S(1)} %bitcast.92), channel_id=1, source_target_pairs={{0,4},{4,0},{8,12},{12,8},{16,20},{20,16},{24,28},{28,24},{1,5},{5... | collective-permute-start | bytes 2654216 | tf_op jit(solution)/shard_map/ppermute | solution.py:409
  (117 shorter events, 51.0 us)
Async XLA Ops:
  4.9 16.8 %collective-permute-start.1 = (f32[360,384]{1,0:T(8,128)}, f32[360,384]{1,0:T(8,128)S(1)}, u32[]{:S(2)}, u32[]{:S(2)}) collective-permute-start(f32[360,384]{1,0:T(8,128)} %get-tuple-element.113), channel_id=1, source_target_pairs={{0,1},{1,5},{2,0},{3,4},{4,3},{5,7},{6,2},{7,6},{8,10},{9,14},{10,... | collective-permute-start | bytes 1658888 | tf_op jit(solution)/shard_map/ppermute | solution.py:315
  8.0 13.8 %collective-permute-start = (f32[360,384]{1,0:T(8,128)S(1)}, f32[360,384]{1,0:T(8,128)S(1)}, u32[]{:S(2)}, u32[]{:S(2)}) collective-permute-start(f32[360,384]{1,0:T(8,128)S(1)} %get-tuple-element.114), channel_id=1, source_target_pairs={{0,0},{1,4},{2,1},{3,5},{4,2},{5,6},{6,3},{7,7},{8,11},{9,15},{10,... | collective-permute-start | bytes 1658888 | tf_op jit(solution)/shard_map/ppermute | solution.py:315
  21.7 28.6 %collective-permute-start.3 = (f32[360,384]{1,0:T(8,128)S(1)}, f32[360,384]{1,0:T(8,128)S(1)}, u32[]{:S(2)}, u32[]{:S(2)}) collective-permute-start(f32[360,384]{1,0:T(8,128)S(1)} %collective-permute-done.1.refs_1_), channel_id=1, source_target_pairs={{0,4},{4,0},{1,5},{5,1},{2,6},{6,2},{3,7},{7,3},{11,15},{15,11},{1... | collective-permute-start | bytes 1658888 | tf_op jit(solution)/shard_map/ppermute | solution.py:315
  28.3 22.1 %collective-permute-start.2 = (f32[360,384]{1,0:T(8,128)S(1)}, f32[360,384]{1,0:T(8,128)S(1)}, u32[]{:S(2)}, u32[]{:S(2)}) collective-permute-start(f32[360,384]{1,0:T(8,128)S(1)} %collective-permute-done.refs_0_), channel_id=1, source_target_pairs={{0,4},{4,0},{1,5},{5,1},{2,6},{6,2},{3,7},{7,3},{11,15},{15,11},{1... | collective-permute-start | bytes 1658888 | tf_op jit(solution)/shard_map/ppermute | solution.py:315
  28.3 30.6 %collective-permute-start.9 = (f32[360,384]{1,0:T(8,128)}, f32[360,384]{1,0:T(8,128)S(1)}, u32[]{:S(2)}, u32[]{:S(2)}) collective-permute-start(f32[360,384]{1,0:T(8,128)} %get-tuple-element.58), channel_id=1, source_target_pairs={{0,1},{1,5},{2,0},{3,4},{4,3},{5,7},{6,2},{7,6},{8,10},{9,14},{10,... | collective-permute-start | bytes 1658888 | tf_op jit(solution)/shard_map/ppermute | solution.py:315
  44.2 16.0 %collective-permute-start.5 = (f32[360,384]{1,0:T(8,128)}, f32[360,384]{1,0:T(8,128)S(1)}, u32[]{:S(2)}, u32[]{:S(2)}) collective-permute-start(f32[360,384]{1,0:T(8,128)} %get-tuple-element.55), channel_id=1, source_target_pairs={{0,0},{1,4},{2,1},{3,5},{4,2},{5,6},{6,3},{7,7},{8,11},{9,15},{10,... | collective-permute-start | bytes 1658888 | tf_op jit(solution)/shard_map/ppermute | solution.py:315
  57.5 29.8 %collective-permute-start.12 = (f32[736,384]{1,0:T(8,128)}, f32[736,384]{1,0:T(8,128)S(1)}, u32[]{:S(2)}, u32[]{:S(2)}) collective-permute-start(f32[736,384]{1,0:T(8,128)} %shard_map.94.refs_1_), channel_id=1, source_target_pairs={{1,0},{5,4},{2,1},{6,5},{3,2},{7,6},{11,3},{15,7},{10,11},{14,15},... | collective-permute-start | bytes 3391496 | tf_op jit(solution)/shard_map/ppermute | solution.py:315
  60.3 29.8 %collective-permute-start.4 = (f32[736,384]{1,0:T(8,128)}, f32[736,384]{1,0:T(8,128)S(1)}, u32[]{:S(2)}, u32[]{:S(2)}) collective-permute-start(f32[736,384]{1,0:T(8,128)} %shard_map.94.refs_1_), channel_id=1, source_target_pairs={{0,1},{4,5},{1,2},{5,6},{2,3},{6,7},{3,11},{7,15},{11,10},{15,14},... | collective-permute-start | bytes 3391496 | tf_op jit(solution)/shard_map/ppermute | solution.py:315
  71.8 40.0 %collective-permute-start.17 = (f32[736,384]{1,0:T(8,128)}, f32[736,384]{1,0:T(8,128)S(1)}, u32[]{:S(2)}, u32[]{:S(2)}) collective-permute-start(f32[736,384]{1,0:T(8,128)} %shard_map.95.refs_3_.refs_1_), channel_id=1, source_target_pairs={{1,0},{5,4},{2,1},{6,5},{3,2},{7,6},{11,3},{15,7},{10,11},{14,15},... | collective-permute-start | bytes 3391496 | tf_op jit(solution)/shard_map/ppermute | solution.py:315
  73.1 40.7 %collective-permute-start.15 = (f32[736,384]{1,0:T(8,128)}, f32[736,384]{1,0:T(8,128)}, u32[]{:S(2)}, u32[]{:S(2)}) collective-permute-start(f32[736,384]{1,0:T(8,128)} %shard_map.95.refs_3_.refs_1_), channel_id=1, source_target_pairs={{0,1},{4,5},{1,2},{5,6},{2,3},{6,7},{3,11},{7,15},{11,10},{15,14},... | collective-permute-start | bytes 3391496 | tf_op jit(solution)/shard_map/ppermute | solution.py:315
  115.0 33.3 %collective-permute-start.14 = (f32[360,384]{1,0:T(8,128)S(1)}, f32[360,384]{1,0:T(8,128)S(1)}, u32[]{:S(2)}, u32[]{:S(2)}) collective-permute-start(f32[360,384]{1,0:T(8,128)S(1)} %add.124), channel_id=1, source_target_pairs={{0,0},{4,1},{1,2},{5,3},{2,4},{6,5},{3,6},{7,7},{11,8},{15,9},{10,... | collective-permute-start | bytes 1658888 | tf_op jit(solution)/shard_map/ppermute | solution.py:315
  119.6 28.7 %collective-permute-start.21 = (f32[144,384]{1,0:T(8,128)S(1)}, f32[144,384]{1,0:T(8,128)}, u32[]{:S(2)}, u32[]{:S(2)}) collective-permute-start(f32[144,384]{1,0:T(8,128)S(1)} %get-tuple-element.115), channel_id=1, source_target_pairs={{0,8},{4,12},{8,0},{12,4},{16,24},{20,28},{24,16},{28,20},{1,9},{5... | collective-permute-start | bytes 663560 | tf_op jit(solution)/shard_map/ppermute | solution.py:286
  128.4 20.5 %collective-permute-start.22 = (f32[144,384]{1,0:T(8,128)}, f32[144,384]{1,0:T(8,128)}, u32[]{:S(2)}, u32[]{:S(2)}) collective-permute-start(f32[144,384]{1,0:T(8,128)} %get-tuple-element.117), channel_id=1, source_target_pairs={{0,16},{4,20},{8,24},{12,28},{16,0},{20,4},{24,8},{28,12},{1,17},{... | collective-permute-start | bytes 663560 | tf_op jit(solution)/shard_map/ppermute | solution.py:286
  128.4 20.5 %collective-permute-start.23 = (f32[144,384]{1,0:T(8,128)S(1)}, f32[144,384]{1,0:T(8,128)}, u32[]{:S(2)}, u32[]{:S(2)}) collective-permute-start(f32[144,384]{1,0:T(8,128)S(1)} %get-tuple-element.116), channel_id=1, source_target_pairs={{0,24},{4,28},{8,16},{12,20},{16,8},{20,12},{24,0},{28,4},{1,25},{... | collective-permute-start | bytes 663560 | tf_op jit(solution)/shard_map/ppermute | solution.py:286
  129.8 21.3 %collective-permute-start.19 = (f32[360,384]{1,0:T(8,128)}, f32[360,384]{1,0:T(8,128)S(1)}, u32[]{:S(2)}, u32[]{:S(2)}) collective-permute-start(f32[360,384]{1,0:T(8,128)} %add.125), channel_id=1, source_target_pairs={{1,0},{5,1},{0,2},{4,3},{3,4},{7,5},{2,6},{6,7},{10,8},{14,9},{11,... | collective-permute-start | bytes 1658888 | tf_op jit(solution)/shard_map/ppermute | solution.py:315
  148.4 7.4 %collective-permute-start.20 = (f32[360,384]{1,0:T(8,128)S(1)}, f32[360,384]{1,0:T(8,128)}, u32[]{:S(2)}, u32[]{:S(2)}) collective-permute-start(f32[360,384]{1,0:T(8,128)S(1)} %get-tuple-element.80), channel_id=1, source_target_pairs={{0,4},{4,0},{1,5},{5,1},{2,6},{6,2},{3,7},{7,3},{11,15},{15,11},{1... | collective-permute-start | bytes 1658888 | tf_op jit(solution)/shard_map/ppermute | solution.py:315
  150.1 7.5 %collective-permute-start.25 = (f32[108,128]{1,0:T(8,128)S(1)}, f32[108,128]{1,0:T(8,128)S(1)}, u32[]{:S(2)}, u32[]{:S(2)}) collective-permute-start(f32[108,128]{1,0:T(8,128)S(1)} %get-tuple-element.121), channel_id=1, source_target_pairs={{0,1},{1,0},{2,3},{3,2},{4,5},{5,4},{6,7},{7,6},{8,9},{9,8},{10,11... | collective-permute-start | bytes 165896 | tf_op jit(solution)/shard_map/ppermute | solution.py:286
  150.2 7.9 %collective-permute-start.26 = (f32[108,128]{1,0:T(8,128)S(1)}, f32[108,128]{1,0:T(8,128)S(1)}, u32[]{:S(2)}, u32[]{:S(2)}) collective-permute-start(f32[108,128]{1,0:T(8,128)S(1)} %get-tuple-element.123), channel_id=1, source_target_pairs={{0,2},{1,3},{2,0},{3,1},{4,6},{5,7},{6,4},{7,5},{8,10},{9,11},{10,... | collective-permute-start | bytes 165896 | tf_op jit(solution)/shard_map/ppermute | solution.py:286
  162.7 10.1 %collective-permute-start.28 = (f32[360,384]{1,0:T(8,128)}, f32[360,384]{1,0:T(8,128)S(1)}, u32[]{:S(2)}, u32[]{:S(2)}) collective-permute-start(f32[360,384]{1,0:T(8,128)} %add.129), channel_id=1, source_target_pairs={{0,0},{4,1},{1,2},{5,3},{2,4},{6,5},{3,6},{7,7},{11,8},{15,9},{10,... | collective-permute-start | bytes 1658888 | tf_op jit(solution)/shard_map/ppermute | solution.py:315
  164.4 16.7 %collective-permute-start.29 = (f32[360,384]{1,0:T(8,128)S(1)}, f32[360,384]{1,0:T(8,128)S(1)}, u32[]{:S(2)}, u32[]{:S(2)}) collective-permute-start(f32[360,384]{1,0:T(8,128)S(1)} %add.138), channel_id=1, source_target_pairs={{1,0},{5,1},{0,2},{4,3},{3,4},{7,5},{2,6},{6,7},{10,8},{14,9},{11,... | collective-permute-start | bytes 1658888 | tf_op jit(solution)/shard_map/ppermute | solution.py:315
  167.4 9.3 %collective-permute-start.35 = (f32[144,384]{1,0:T(8,128)S(1)}, f32[144,384]{1,0:T(8,128)S(1)}, u32[]{:S(2)}, u32[]{:S(2)}) collective-permute-start(f32[144,384]{1,0:T(8,128)S(1)} %reshape_reshape.7), channel_id=1, source_target_pairs={{0,24},{4,28},{8,16},{12,20},{16,8},{20,12},{24,0},{28,4},{1,25},{... | collective-permute-start | bytes 663560 | tf_op jit(solution)/shard_map/ppermute | solution.py:299
  168.0 11.9 %collective-permute-start.34 = (f32[144,384]{1,0:T(8,128)S(1)}, f32[144,384]{1,0:T(8,128)S(1)}, u32[]{:S(2)}, u32[]{:S(2)}) collective-permute-start(f32[144,384]{1,0:T(8,128)S(1)} %reshape_reshape.7), channel_id=1, source_target_pairs={{0,16},{4,20},{8,24},{12,28},{16,0},{20,4},{24,8},{28,12},{1,17},{... | collective-permute-start | bytes 663560 | tf_op jit(solution)/shard_map/ppermute | solution.py:299
  169.7 11.4 %collective-permute-start.33 = (f32[144,384]{1,0:T(8,128)S(1)}, f32[144,384]{1,0:T(8,128)S(1)}, u32[]{:S(2)}, u32[]{:S(2)}) collective-permute-start(f32[144,384]{1,0:T(8,128)S(1)} %reshape_reshape.7), channel_id=1, source_target_pairs={{0,8},{4,12},{8,0},{12,4},{16,24},{20,28},{24,16},{28,20},{1,9},{5... | collective-permute-start | bytes 663560 | tf_op jit(solution)/shard_map/ppermute | solution.py:299
  181.2 11.2 %collective-permute-start.36 = (f32[576,384]{1,0:T(8,128)S(1)}, f32[576,384]{1,0:T(8,128)S(1)}, u32[]{:S(2)}, u32[]{:S(2)}) collective-permute-start(f32[576,384]{1,0:T(8,128)S(1)} %bitcast.92), channel_id=1, source_target_pairs={{0,4},{4,0},{8,12},{12,8},{16,20},{20,16},{24,28},{28,24},{1,5},{5... | collective-permute-start | bytes 2654216 | tf_op jit(solution)/shard_map/ppermute | solution.py:409
  (22 other events, 162.3 us)

commit v6 on v5

--- a/solution.py
+++ b/solution.py
@@ -10,7 +10,7 @@
 
 AXES = ("lat", "lon")
 SLOTS = 4
-VMEM = 51 * 2**20
+VMEM = 53 * 2**20
 BF16 = jnp.bfloat16
 
 

time: 195 us -> 197 us (1.010)
  other arithmetic: 18.6 us -> 12.5 us
  Pallas kernels: 50.4 us -> 55.4 us
  local copies, waits for them, and re-layouts: 13.2 us -> 16.7 us
    unnamed x18 -> x32, local copies, waits for them, and re-layouts: 1.15 us -> 5.04 us
    pallas_call x2, Pallas kernels: 14.3 us -> 17.2 us  [transform(): kernel_call(body, (), [REMAIN] * (count + 1), WHOLE, jax.ShapeDtypeStruct...]
    ppermute x6, waiting for transfers between devices: 0.51 us -> 3.41 us  [shares_sent(): lax.ppermute(piece, axis, [(a, a ^ g * stride) for a in range(size)])]
    add x4, other arithmetic: 6.07 us -> 3.33 us  [total(): return [own[t] + sum((other[t] for other in others)) for t in range(2)]]
    ppermute x20, waiting for transfers between devices: 13.5 us -> 11.3 us  [send(): return lax.ppermute(x, AXES, pairs)]
    pallas_call x2, Pallas kernels: 3.32 us -> 5.45 us  [arrange(): kernel_call(body, (), [WHOLE, WHOLE], WHOLE, jax.ShapeDtypeStruct((2, par...]
  transfers between devices with their start and end apart: 37 -> 37, of which waited for: 12 -> 12; matrix products, arithmetic and copies ran while one was open for 13% -> 10% of each run, Pallas kernels for 26% -> 28%
where the time goes in v6:
time: 197 us; the launch traced here: 196 us
  starting transfers between devices  83.5 us (42%)
  Pallas kernels  55.4 us (28%)
  waiting for transfers between devices  25.3 us (13%)
  local copies, waits for them, and re-layouts  16.7 us (8%)
  other arithmetic  12.5 us (6%)
  between operations  2.6 us (1%)
    ppermute x20, starting transfers between devices, send(): return lax.ppermute(x, AXES, pairs)  46.9 us
    pallas_call x2, Pallas kernels, mix(): kernel_call(body, (), [REMAIN] * n_rows + [WHOLE] + [REMAIN] * 2, [WHOLE]...  32.8 us
    pallas_call x2, Pallas kernels, transform(): kernel_call(body, (), [REMAIN] * (count + 1), WHOLE, jax.ShapeDtypeStruct...  17.2 us
    ppermute x6, starting transfers between devices, shares_sent(): lax.ppermute(piece, axis, [(a, a ^ g * stride) for a in range(size)])  14.7 us
    ppermute x20, waiting for transfers between devices, send(): return lax.ppermute(x, AXES, pairs)  11.3 us
    ppermute x6, waiting for transfers between devices, share_shown(): lax.ppermute(x, axis, [(a, a ^ g * stride) for a in range(size)])  9.78 us
    ppermute x2, starting transfers between devices, swap_core(): return lax.ppermute(x, 'lat', swap)  8.74 us
    ppermute x6, starting transfers between devices, share_shown(): lax.ppermute(x, axis, [(a, a ^ g * stride) for a in range(size)])  8.55 us
  transfers between devices with their start and end apart: 37, of which 12 were waited for; matrix products, arithmetic and copies ran while one was open for 10% of the time, Pallas kernels for 28%

profile of v6, /device:TPU:0, one launch (start us, length us, event | category | flops | bytes accessed | tf_op | source)
XLA Modules:
  0.0 196.0 jit_solution(7922909254637053649)
XLA Ops:
  2.8 2.4 %dynamic-slice_bitcast_fusion.3 = (f32[360,384]{1,0:T(8,128)}, f32[360,384]{1,0:T(8,128)}) fusion(f32[2,360,384]{2,1,0:T(8,128)} %param.7, s32[]{:T(128)S(6)} %select_n.249, s32[]{:T(128)S(6)} %select_n.248), kind=kLoop, calls=%fused_computation.13 | loop fusion | bytes 2211848 | tf_op jit(solution)/shard_map/jit(dynamic_index_in_dim)/squeeze | solution.py:345
  5.2 3.0 %collective-permute-start.1 = (f32[360,384]{1,0:T(8,128)}, f32[360,384]{1,0:T(8,128)}, u32[]{:S(2)}, u32[]{:S(2)}) collective-permute-start(f32[360,384]{1,0:T(8,128)} %get-tuple-element.113), channel_id=1, source_target_pairs={{0,1},{1,5},{2,0},{3,4},{4,3},{5,7},{6,2},{7,6},{8,10},{9,14},{10,... | collective-permute-start | bytes 1658888 | tf_op jit(solution)/shard_map/ppermute | solution.py:315
  12.9 2.7 %reduce-precision_convert_fusion = (bf16[1152,384]{1,0:T(8,128)(2,1)S(1)}, bf16[1152,384]{1,0:T(8,128)(2,1)}) fusion(f32[3,384,384]{2,1,0:T(8,128)} %copy.11), kind=kLoop, calls=%fused_computation.1 | loop fusion | flops 1769472 | bytes 3538944 | tf_op jit(solution)/shard_map/convert_element_type | solution.py:92
  16.4 2.4 %dynamic-slice_bitcast_fusion.1 = (f32[360,384]{1,0:T(8,128)}, f32[360,384]{1,0:T(8,128)}) fusion(f32[2,360,384]{2,1,0:T(8,128)} %param.11, s32[]{:T(128)S(6)} %select_n.249, s32[]{:T(128)S(6)} %select_n.248), kind=kLoop, calls=%fused_computation.11 | loop fusion | bytes 2211848 | tf_op jit(solution)/shard_map/jit(dynamic_index_in_dim)/squeeze | solution.py:345
  22.1 6.5 %collective-permute-start.3 = (f32[360,384]{1,0:T(8,128)}, f32[360,384]{1,0:T(8,128)S(1)}, u32[]{:S(2)}, u32[]{:S(2)}) collective-permute-start(f32[360,384]{1,0:T(8,128)} %collective-permute-done.1.refs_1_), channel_id=1, source_target_pairs={{0,4},{4,0},{1,5},{5,1},{2,6},{6,2},{3,7},{7,3},{11,15},{15,11},{1... | collective-permute-start | bytes 1658888 | tf_op jit(solution)/shard_map/ppermute | solution.py:315
  28.6 13.1 %collective-permute-start.9 = (f32[360,384]{1,0:T(8,128)}, f32[360,384]{1,0:T(8,128)S(1)}, u32[]{:S(2)}, u32[]{:S(2)}) collective-permute-start(f32[360,384]{1,0:T(8,128)} %get-tuple-element.58), channel_id=1, source_target_pairs={{0,1},{1,5},{2,0},{3,4},{4,3},{5,7},{6,2},{7,6},{8,10},{9,14},{10,... | collective-permute-start | bytes 1658888 | tf_op jit(solution)/shard_map/ppermute | solution.py:315
  51.4 8.6 %shard_map.94.refs_1_ = f32[736,384]{1,0:T(8,128)} custom-call(s32[2]{0:T(128)S(1)} %pad_add_fusion.1.place, f32[360,384]{1,0:T(8,128)S(1)} %collective-permute-done.refs_0_, f32[360,384]{1,0:T(8,128)} %collective-permute-done.1.refs_1_, f32[360,384]{1,0:T(8,128)} %copy-done.8, f32[360,384]{1,0:T(8,128)} %copy-done.7, ...), custom_call_target="tpu_custom_call" | custom-call | flops 1 | bytes 1 | tf_op jit(solution)/shard_map/pallas_call | solution.py:175
  61.9 4.6 %collective-permute-start.4 = (f32[736,384]{1,0:T(8,128)}, f32[736,384]{1,0:T(8,128)S(1)}, u32[]{:S(2)}, u32[]{:S(2)}) collective-permute-start(f32[736,384]{1,0:T(8,128)} %shard_map.94.refs_1_), channel_id=1, source_target_pairs={{0,1},{4,5},{1,2},{5,6},{2,3},{6,7},{3,11},{7,15},{11,10},{15,14},... | collective-permute-start | bytes 3391496 | tf_op jit(solution)/shard_map/ppermute | solution.py:315
  68.2 8.6 %shard_map.95.refs_3_.refs_1_ = f32[736,384]{1,0:T(8,128)} custom-call(s32[2]{0:T(128)S(1)} %pad_add_fusion.1.place, f32[360,384]{1,0:T(8,128)S(1)} %collective-permute-done.5.refs_0_, f32[360,384]{1,0:T(8,128)} %copy-done.6, f32[360,384]{1,0:T(8,128)} %copy-done.10, f32[360,384]{1,0:T(8,128)} %copy-done.9, ...), custom_call_target="tpu_custom_call" | custom-call | flops 1 | bytes 1 | tf_op jit(solution)/shard_map/pallas_call | solution.py:175
  78.1 5.6 %collective-permute-start.15 = (f32[736,384]{1,0:T(8,128)}, f32[736,384]{1,0:T(8,128)}, u32[]{:S(2)}, u32[]{:S(2)}) collective-permute-start(f32[736,384]{1,0:T(8,128)} %shard_map.95.refs_3_.refs_1_), channel_id=1, source_target_pairs={{0,1},{4,5},{1,2},{5,6},{2,3},{6,7},{3,11},{7,15},{11,10},{15,14},... | collective-permute-start | bytes 3391496 | tf_op jit(solution)/shard_map/ppermute | solution.py:315
  83.7 6.2 %collective-permute-done.12.refs_2_ = f32[736,384]{1,0:T(8,128)S(1)} collective-permute-done((f32[736,384]{1,0:T(8,128)}, f32[736,384]{1,0:T(8,128)S(1)}, u32[]{:S(2)}, u32[]{:S(2)}) %collective-permute-start.12) | collective-permute-done | bytes 1130528 | tf_op jit(solution)/shard_map/ppermute | solution.py:315
  89.9 2.2 %collective-permute-done.4.refs_0_ = f32[736,384]{1,0:T(8,128)S(1)} collective-permute-done((f32[736,384]{1,0:T(8,128)}, f32[736,384]{1,0:T(8,128)S(1)}, u32[]{:S(2)}, u32[]{:S(2)}) %collective-permute-start.4) | collective-permute-done | bytes 1130528 | tf_op jit(solution)/shard_map/ppermute | solution.py:315
  93.1 18.0 %shard_map.96 = (f32[360,384]{1,0:T(8,128)S(1)}, f32[360,384]{1,0:T(8,128)}, f32[360,384]{1,0:T(8,128)}, f32[360,384]{1,0:T(8,128)}, f32[1152,384]{1,0:T(8,128)}) custom-call(s32[2]{0:T(128)S(1)} %pad_add_fusion.1.place, f32[736,384]{1,0:T(8,128)} %copy-done.5, f32[736,384]{1,0:T(8,128)} %shard_map.94.refs_1_, f32[736,384]{1,0:T(8,128)} %copy-done.4, ...), custom_call_target="tpu_custom_call" | custom-call | flops 1 | bytes 1 | tf_op jit(solution)/shard_map/pallas_call | solution.py:246
  121.0 8.8 %collective-permute-start.21 = (f32[144,384]{1,0:T(8,128)S(1)}, f32[144,384]{1,0:T(8,128)}, u32[]{:S(2)}, u32[]{:S(2)}) collective-permute-start(f32[144,384]{1,0:T(8,128)S(1)} %get-tuple-element.115), channel_id=1, source_target_pairs={{0,8},{4,12},{8,0},{12,4},{16,24},{20,28},{24,16},{28,20},{1,9},{5... | collective-permute-start | bytes 663560 | tf_op jit(solution)/shard_map/ppermute | solution.py:286
  131.3 3.5 %collective-permute-start.19 = (f32[360,384]{1,0:T(8,128)}, f32[360,384]{1,0:T(8,128)}, u32[]{:S(2)}, u32[]{:S(2)}) collective-permute-start(f32[360,384]{1,0:T(8,128)} %add.125), channel_id=1, source_target_pairs={{1,0},{5,1},{0,2},{4,3},{3,4},{7,5},{2,6},{6,7},{10,8},{14,9},{11,... | collective-permute-start | bytes 1658888 | tf_op jit(solution)/shard_map/ppermute | solution.py:315
  134.8 14.8 %shard_map.97 = (f32[360,384]{1,0:T(8,128)S(1)}, f32[360,384]{1,0:T(8,128)}, f32[360,384]{1,0:T(8,128)}, f32[360,384]{1,0:T(8,128)}) custom-call(s32[2]{0:T(128)S(1)} %pad_add_fusion.1.place, f32[736,384]{1,0:T(8,128)} %collective-permute-done.15.refs_0_, f32[736,384]{1,0:T(8,128)} %shard_map.95.refs_3_.refs_1_, f32[736,384]{1,0:T(8,128)} %collective-permute-done.17.refs_2_, ...), custom_call_target="tpu_custom_call" | custom-call | flops 1 | bytes 1 | tf_op jit(solution)/shard_map/pallas_call | solution.py:246
  153.1 2.9 %collective-permute-start.27 = (f32[108,128]{1,0:T(8,128)S(1)}, f32[108,128]{1,0:T(8,128)S(1)}, u32[]{:S(2)}, u32[]{:S(2)}) collective-permute-start(f32[108,128]{1,0:T(8,128)S(1)} %get-tuple-element.122), channel_id=1, source_target_pairs={{0,3},{1,2},{2,1},{3,0},{4,7},{5,6},{6,5},{7,4},{8,11},{9,10},{10,... | collective-permute-start | bytes 165896 | tf_op jit(solution)/shard_map/ppermute | solution.py:286
  156.6 3.0 %collective-permute-done.26 = f32[108,128]{1,0:T(8,128)S(1)} collective-permute-done((f32[108,128]{1,0:T(8,128)S(1)}, f32[108,128]{1,0:T(8,128)S(1)}, u32[]{:S(2)}, u32[]{:S(2)}) %collective-permute-start.26) | collective-permute-done | bytes 55328 | tf_op jit(solution)/shard_map/ppermute | solution.py:286
  169.4 2.2 %collective-permute-start.34 = (f32[144,384]{1,0:T(8,128)S(1)}, f32[144,384]{1,0:T(8,128)S(1)}, u32[]{:S(2)}, u32[]{:S(2)}) collective-permute-start(f32[144,384]{1,0:T(8,128)S(1)} %reshape_reshape.7), channel_id=1, source_target_pairs={{0,16},{4,20},{8,24},{12,28},{16,0},{20,4},{24,8},{28,12},{1,17},{... | collective-permute-start | bytes 663560 | tf_op jit(solution)/shard_map/ppermute | solution.py:299
  173.0 2.7 %shard_map.98 = f32[2,360,384]{2,1,0:T(8,128)} custom-call(s32[2]{0:T(128)S(1)} %pad_add_fusion.flags, f32[360,384]{1,0:T(8,128)S(1)} %collective-permute-done.14.a, f32[360,384]{1,0:T(8,128)} %collective-permute-done.19.b), custom_call_target="tpu_custom_call" | custom-call | flops 1 | bytes 1 | tf_op jit(solution)/shard_map/pallas_call | solution.py:271
  175.7 2.4 %collective-permute-done.35 = f32[144,384]{1,0:T(8,128)S(1)} collective-permute-done((f32[144,384]{1,0:T(8,128)S(1)}, f32[144,384]{1,0:T(8,128)S(1)}, u32[]{:S(2)}, u32[]{:S(2)}) %collective-permute-start.35) | collective-permute-done | bytes 221216 | tf_op jit(solution)/shard_map/ppermute | solution.py:299
  178.1 3.6 %collective-permute-done.34 = f32[144,384]{1,0:T(8,128)S(1)} collective-permute-done((f32[144,384]{1,0:T(8,128)S(1)}, f32[144,384]{1,0:T(8,128)S(1)}, u32[]{:S(2)}, u32[]{:S(2)}) %collective-permute-start.34) | collective-permute-done | bytes 221216 | tf_op jit(solution)/shard_map/ppermute | solution.py:299
  183.1 8.7 %collective-permute-start.36 = (f32[576,384]{1,0:T(8,128)S(1)}, f32[576,384]{1,0:T(8,128)S(1)}, u32[]{:S(2)}, u32[]{:S(2)}) collective-permute-start(f32[576,384]{1,0:T(8,128)S(1)} %bitcast.92), channel_id=1, source_target_pairs={{0,4},{4,0},{8,12},{12,8},{16,20},{20,16},{24,28},{28,24},{1,5},{5... | collective-permute-start | bytes 2654216 | tf_op jit(solution)/shard_map/ppermute | solution.py:409
  191.8 2.7 %shard_map.99 = f32[2,360,384]{2,1,0:T(8,128)} custom-call(s32[2]{0:T(128)S(1)} %pad_add_fusion.flags, f32[360,384]{1,0:T(8,128)S(1)} %collective-permute-done.28.a, f32[360,384]{1,0:T(8,128)} %copy-done.13), custom_call_target="tpu_custom_call" | custom-call | flops 1 | bytes 1 | tf_op jit(solution)/shard_map/pallas_call | solution.py:271
  (131 shorter events, 54.2 us)
Async XLA Ops:
  5.2 16.9 %collective-permute-start.1 = (f32[360,384]{1,0:T(8,128)}, f32[360,384]{1,0:T(8,128)}, u32[]{:S(2)}, u32[]{:S(2)}) collective-permute-start(f32[360,384]{1,0:T(8,128)} %get-tuple-element.113), channel_id=1, source_target_pairs={{0,1},{1,5},{2,0},{3,4},{4,3},{5,7},{6,2},{7,6},{8,10},{9,14},{10,... | collective-permute-start | bytes 1658888 | tf_op jit(solution)/shard_map/ppermute | solution.py:315
  8.3 13.9 %collective-permute-start = (f32[360,384]{1,0:T(8,128)}, f32[360,384]{1,0:T(8,128)S(1)}, u32[]{:S(2)}, u32[]{:S(2)}) collective-permute-start(f32[360,384]{1,0:T(8,128)} %get-tuple-element.114), channel_id=1, source_target_pairs={{0,0},{1,4},{2,1},{3,5},{4,2},{5,6},{6,3},{7,7},{8,11},{9,15},{10,... | collective-permute-start | bytes 1658888 | tf_op jit(solution)/shard_map/ppermute | solution.py:315
  22.1 27.7 %collective-permute-start.3 = (f32[360,384]{1,0:T(8,128)}, f32[360,384]{1,0:T(8,128)S(1)}, u32[]{:S(2)}, u32[]{:S(2)}) collective-permute-start(f32[360,384]{1,0:T(8,128)} %collective-permute-done.1.refs_1_), channel_id=1, source_target_pairs={{0,4},{4,0},{1,5},{5,1},{2,6},{6,2},{3,7},{7,3},{11,15},{15,11},{1... | collective-permute-start | bytes 1658888 | tf_op jit(solution)/shard_map/ppermute | solution.py:315
  28.6 21.2 %collective-permute-start.2 = (f32[360,384]{1,0:T(8,128)S(1)}, f32[360,384]{1,0:T(8,128)S(1)}, u32[]{:S(2)}, u32[]{:S(2)}) collective-permute-start(f32[360,384]{1,0:T(8,128)S(1)} %collective-permute-done.refs_0_), channel_id=1, source_target_pairs={{0,4},{4,0},{1,5},{5,1},{2,6},{6,2},{3,7},{7,3},{11,15},{15,11},{1... | collective-permute-start | bytes 1658888 | tf_op jit(solution)/shard_map/ppermute | solution.py:315
  28.6 32.7 %collective-permute-start.9 = (f32[360,384]{1,0:T(8,128)}, f32[360,384]{1,0:T(8,128)S(1)}, u32[]{:S(2)}, u32[]{:S(2)}) collective-permute-start(f32[360,384]{1,0:T(8,128)} %get-tuple-element.58), channel_id=1, source_target_pairs={{0,1},{1,5},{2,0},{3,4},{4,3},{5,7},{6,2},{7,6},{8,10},{9,14},{10,... | collective-permute-start | bytes 1658888 | tf_op jit(solution)/shard_map/ppermute | solution.py:315
  44.5 17.3 %collective-permute-start.5 = (f32[360,384]{1,0:T(8,128)}, f32[360,384]{1,0:T(8,128)S(1)}, u32[]{:S(2)}, u32[]{:S(2)}) collective-permute-start(f32[360,384]{1,0:T(8,128)} %get-tuple-element.55), channel_id=1, source_target_pairs={{0,0},{1,4},{2,1},{3,5},{4,2},{5,6},{6,3},{7,7},{8,11},{9,15},{10,... | collective-permute-start | bytes 1658888 | tf_op jit(solution)/shard_map/ppermute | solution.py:315
  60.0 29.8 %collective-permute-start.12 = (f32[736,384]{1,0:T(8,128)}, f32[736,384]{1,0:T(8,128)S(1)}, u32[]{:S(2)}, u32[]{:S(2)}) collective-permute-start(f32[736,384]{1,0:T(8,128)} %shard_map.94.refs_1_), channel_id=1, source_target_pairs={{1,0},{5,4},{2,1},{6,5},{3,2},{7,6},{11,3},{15,7},{10,11},{14,15},... | collective-permute-start | bytes 3391496 | tf_op jit(solution)/shard_map/ppermute | solution.py:315
  61.9 30.1 %collective-permute-start.4 = (f32[736,384]{1,0:T(8,128)}, f32[736,384]{1,0:T(8,128)S(1)}, u32[]{:S(2)}, u32[]{:S(2)}) collective-permute-start(f32[736,384]{1,0:T(8,128)} %shard_map.94.refs_1_), channel_id=1, source_target_pairs={{0,1},{4,5},{1,2},{5,6},{2,3},{6,7},{3,11},{7,15},{11,10},{15,14},... | collective-permute-start | bytes 3391496 | tf_op jit(solution)/shard_map/ppermute | solution.py:315
  76.8 37.0 %collective-permute-start.17 = (f32[736,384]{1,0:T(8,128)}, f32[736,384]{1,0:T(8,128)}, u32[]{:S(2)}, u32[]{:S(2)}) collective-permute-start(f32[736,384]{1,0:T(8,128)} %shard_map.95.refs_3_.refs_1_), channel_id=1, source_target_pairs={{1,0},{5,4},{2,1},{6,5},{3,2},{7,6},{11,3},{15,7},{10,11},{14,15},... | collective-permute-start | bytes 3391496 | tf_op jit(solution)/shard_map/ppermute | solution.py:315
  78.1 37.4 %collective-permute-start.15 = (f32[736,384]{1,0:T(8,128)}, f32[736,384]{1,0:T(8,128)}, u32[]{:S(2)}, u32[]{:S(2)}) collective-permute-start(f32[736,384]{1,0:T(8,128)} %shard_map.95.refs_3_.refs_1_), channel_id=1, source_target_pairs={{0,1},{4,5},{1,2},{5,6},{2,3},{6,7},{3,11},{7,15},{11,10},{15,14},... | collective-permute-start | bytes 3391496 | tf_op jit(solution)/shard_map/ppermute | solution.py:315
  117.4 32.3 %collective-permute-start.14 = (f32[360,384]{1,0:T(8,128)S(1)}, f32[360,384]{1,0:T(8,128)S(1)}, u32[]{:S(2)}, u32[]{:S(2)}) collective-permute-start(f32[360,384]{1,0:T(8,128)S(1)} %add.124), channel_id=1, source_target_pairs={{0,0},{4,1},{1,2},{5,3},{2,4},{6,5},{3,6},{7,7},{11,8},{15,9},{10,... | collective-permute-start | bytes 1658888 | tf_op jit(solution)/shard_map/ppermute | solution.py:315
  121.0 28.7 %collective-permute-start.21 = (f32[144,384]{1,0:T(8,128)S(1)}, f32[144,384]{1,0:T(8,128)}, u32[]{:S(2)}, u32[]{:S(2)}) collective-permute-start(f32[144,384]{1,0:T(8,128)S(1)} %get-tuple-element.115), channel_id=1, source_target_pairs={{0,8},{4,12},{8,0},{12,4},{16,24},{20,28},{24,16},{28,20},{1,9},{5... | collective-permute-start | bytes 663560 | tf_op jit(solution)/shard_map/ppermute | solution.py:286
  129.8 20.4 %collective-permute-start.22 = (f32[144,384]{1,0:T(8,128)}, f32[144,384]{1,0:T(8,128)}, u32[]{:S(2)}, u32[]{:S(2)}) collective-permute-start(f32[144,384]{1,0:T(8,128)} %get-tuple-element.117), channel_id=1, source_target_pairs={{0,16},{4,20},{8,24},{12,28},{16,0},{20,4},{24,8},{28,12},{1,17},{... | collective-permute-start | bytes 663560 | tf_op jit(solution)/shard_map/ppermute | solution.py:286
  129.8 20.4 %collective-permute-start.23 = (f32[144,384]{1,0:T(8,128)S(1)}, f32[144,384]{1,0:T(8,128)}, u32[]{:S(2)}, u32[]{:S(2)}) collective-permute-start(f32[144,384]{1,0:T(8,128)S(1)} %get-tuple-element.116), channel_id=1, source_target_pairs={{0,24},{4,28},{8,16},{12,20},{16,8},{20,12},{24,0},{28,4},{1,25},{... | collective-permute-start | bytes 663560 | tf_op jit(solution)/shard_map/ppermute | solution.py:286
  131.3 21.9 %collective-permute-start.19 = (f32[360,384]{1,0:T(8,128)}, f32[360,384]{1,0:T(8,128)}, u32[]{:S(2)}, u32[]{:S(2)}) collective-permute-start(f32[360,384]{1,0:T(8,128)} %add.125), channel_id=1, source_target_pairs={{1,0},{5,1},{0,2},{4,3},{3,4},{7,5},{2,6},{6,7},{10,8},{14,9},{11,... | collective-permute-start | bytes 1658888 | tf_op jit(solution)/shard_map/ppermute | solution.py:315
  151.6 7.9 %collective-permute-start.26 = (f32[108,128]{1,0:T(8,128)S(1)}, f32[108,128]{1,0:T(8,128)S(1)}, u32[]{:S(2)}, u32[]{:S(2)}) collective-permute-start(f32[108,128]{1,0:T(8,128)S(1)} %get-tuple-element.123), channel_id=1, source_target_pairs={{0,2},{1,3},{2,0},{3,1},{4,6},{5,7},{6,4},{7,5},{8,10},{9,11},{10,... | collective-permute-start | bytes 165896 | tf_op jit(solution)/shard_map/ppermute | solution.py:286
  153.1 6.4 %collective-permute-start.27 = (f32[108,128]{1,0:T(8,128)S(1)}, f32[108,128]{1,0:T(8,128)S(1)}, u32[]{:S(2)}, u32[]{:S(2)}) collective-permute-start(f32[108,128]{1,0:T(8,128)S(1)} %get-tuple-element.122), channel_id=1, source_target_pairs={{0,3},{1,2},{2,1},{3,0},{4,7},{5,6},{6,5},{7,4},{8,11},{9,10},{10,... | collective-permute-start | bytes 165896 | tf_op jit(solution)/shard_map/ppermute | solution.py:286
  159.6 6.6 %collective-permute-start.30 = (f32[108,128]{1,0:T(8,128)S(1)}, f32[108,128]{1,0:T(8,128)S(1)}, u32[]{:S(2)}, u32[]{:S(2)}) collective-permute-start(f32[108,128]{1,0:T(8,128)S(1)} %get-tuple-element.104), channel_id=1, source_target_pairs={{0,1},{1,0},{2,3},{3,2},{4,5},{5,4},{6,7},{7,6},{8,9},{9,8},{10,11... | collective-permute-start | bytes 165896 | tf_op jit(solution)/shard_map/ppermute | solution.py:299
  164.1 11.6 %collective-permute-start.28 = (f32[360,384]{1,0:T(8,128)S(1)}, f32[360,384]{1,0:T(8,128)S(1)}, u32[]{:S(2)}, u32[]{:S(2)}) collective-permute-start(f32[360,384]{1,0:T(8,128)S(1)} %add.129), channel_id=1, source_target_pairs={{0,0},{4,1},{1,2},{5,3},{2,4},{6,5},{3,6},{7,7},{11,8},{15,9},{10,... | collective-permute-start | bytes 1658888 | tf_op jit(solution)/shard_map/ppermute | solution.py:315
  164.8 18.2 %collective-permute-start.29 = (f32[360,384]{1,0:T(8,128)S(1)}, f32[360,384]{1,0:T(8,128)S(1)}, u32[]{:S(2)}, u32[]{:S(2)}) collective-permute-start(f32[360,384]{1,0:T(8,128)S(1)} %add.138), channel_id=1, source_target_pairs={{1,0},{5,1},{0,2},{4,3},{3,4},{7,5},{2,6},{6,7},{10,8},{14,9},{11,... | collective-permute-start | bytes 1658888 | tf_op jit(solution)/shard_map/ppermute | solution.py:315
  168.8 9.3 %collective-permute-start.35 = (f32[144,384]{1,0:T(8,128)S(1)}, f32[144,384]{1,0:T(8,128)S(1)}, u32[]{:S(2)}, u32[]{:S(2)}) collective-permute-start(f32[144,384]{1,0:T(8,128)S(1)} %reshape_reshape.7), channel_id=1, source_target_pairs={{0,24},{4,28},{8,16},{12,20},{16,8},{20,12},{24,0},{28,4},{1,25},{... | collective-permute-start | bytes 663560 | tf_op jit(solution)/shard_map/ppermute | solution.py:299
  169.4 12.4 %collective-permute-start.34 = (f32[144,384]{1,0:T(8,128)S(1)}, f32[144,384]{1,0:T(8,128)S(1)}, u32[]{:S(2)}, u32[]{:S(2)}) collective-permute-start(f32[144,384]{1,0:T(8,128)S(1)} %reshape_reshape.7), channel_id=1, source_target_pairs={{0,16},{4,20},{8,24},{12,28},{16,0},{20,4},{24,8},{28,12},{1,17},{... | collective-permute-start | bytes 663560 | tf_op jit(solution)/shard_map/ppermute | solution.py:299
  171.5 11.4 %collective-permute-start.33 = (f32[144,384]{1,0:T(8,128)S(1)}, f32[144,384]{1,0:T(8,128)S(1)}, u32[]{:S(2)}, u32[]{:S(2)}) collective-permute-start(f32[144,384]{1,0:T(8,128)S(1)} %reshape_reshape.7), channel_id=1, source_target_pairs={{0,8},{4,12},{8,0},{12,4},{16,24},{20,28},{24,16},{28,20},{1,9},{5... | collective-permute-start | bytes 663560 | tf_op jit(solution)/shard_map/ppermute | solution.py:299
  183.1 11.5 %collective-permute-start.36 = (f32[576,384]{1,0:T(8,128)S(1)}, f32[576,384]{1,0:T(8,128)S(1)}, u32[]{:S(2)}, u32[]{:S(2)}) collective-permute-start(f32[576,384]{1,0:T(8,128)S(1)} %bitcast.92), channel_id=1, source_target_pairs={{0,4},{4,0},{8,12},{12,8},{16,20},{20,16},{24,28},{28,24},{1,5},{5... | collective-permute-start | bytes 2654216 | tf_op jit(solution)/shard_map/ppermute | solution.py:409
  (29 other events, 161.7 us)
